TPU v7x, 256 devices: a whole 4x4x8 slice. The times are simulated.
256 devices in a mesh: ctx: 64 (over z, x, core), head: 4 (over y).
Axes of the slice: x: 4, y: 4, z: 8, core: 2. Of those that a mesh axis runs over, the one named last changes fastest.
Arguments:
- query: bfloat16 [32768, 4096], P('ctx', 'head'), may hold values from -40 to 40
- keys: bfloat16 [32768, 4096], P('ctx', 'head'), may hold values from -6 to 6
- values: bfloat16 [32768, 4096], P('ctx', 'head'), may hold values from -6 to 6
- gain: float32 [4096], P('head'), may hold values from 0.5 to 2
- cotangent: bfloat16 [32768, 4096], P('ctx', 'head'), may hold values from -6 to 6
Outputs:
- attended: bfloat16 [32768, 4096], P('ctx', 'head')
- grad_query: bfloat16 [32768, 4096], P('ctx', 'head')
- grad_keys: bfloat16 [32768, 4096], P('ctx', 'head')
- grad_values: bfloat16 [32768, 4096], P('ctx', 'head')
All inputs are finite; a program needn't handle non-finite values.
Results may differ from a plain program's by a relative error of at most 0.006.
Values sent between devices are 32-bit elements; how exact they have to be, the bound alone decides.
No kernel may reach another device: no remote copies, remote signals or barrier semaphores. Data moves between devices by JAX's collectives and lax.ppermute only.
A program may use at most 128 MiB of HBM per device.

v0:
```python
import jax
import jax.numpy as jnp
from jax import lax
from jax.sharding import PartitionSpec as P

HEADS = 32
HEAD_DIM = 128


EPSILON = 1e-05


def carried_in(part, axis, combine, identity, reverse):
    count = lax.axis_size(axis)
    place = lax.axis_index(axis)
    ahead = count - 1 - place if reverse else place
    gathered = lax.all_gather(part, axis)
    state = jnp.zeros_like(part) + jnp.asarray(identity, part.dtype)

    def one(step, state):
        source = count - 1 - step if reverse else step
        return combine(state, lax.dynamic_index_in_dim(gathered, source, 0, False))

    return lax.fori_loop(0, ahead, one, state)


def add_pair(earlier, later):
    return earlier + later


def causal_mask(length):
    rows = lax.broadcasted_iota(jnp.int32, (length, length), 0)
    cols = lax.broadcasted_iota(jnp.int32, (length, length), 1)
    return cols <= rows


def body(query, keys, values, gain, cotangent):
    length = query.shape[0]
    heads_here = query.shape[1] // HEAD_DIM
    layout = (length, heads_here, HEAD_DIM)
    width_all = HEADS * HEAD_DIM
    q_heads = query.reshape(layout)
    k_heads = keys.reshape(layout)
    v_heads = values.reshape(layout)
    local_state = jnp.einsum("thd,the->hde", k_heads, v_heads, preferred_element_type=jnp.float32)
    before = carried_in(local_state, "ctx", add_pair, jnp.zeros_like(local_state), False)
    state_round = before.astype(jnp.bfloat16)
    causal = causal_mask(length)
    scores = jnp.einsum("thd,shd->hts", q_heads, k_heads, preferred_element_type=jnp.float32)
    weights = jnp.where(causal[None], scores, 0.0).astype(jnp.bfloat16)
    mixture = jnp.einsum("hts,she->the", weights, v_heads, preferred_element_type=jnp.float32)
    mixture = mixture + jnp.einsum(
        "thd,hde->the", q_heads, state_round, preferred_element_type=jnp.float32
    )
    flattened = mixture.reshape(length, heads_here * HEAD_DIM)
    squares = lax.psum(jnp.sum(flattened * flattened, axis=1), "head")
    inverse = lax.rsqrt(squares / width_all + EPSILON)
    attended = (flattened * inverse[:, None] * gain[None, :]).astype(jnp.bfloat16)
    scaled = cotangent.astype(jnp.float32) * gain[None, :]
    products = lax.psum(jnp.sum(scaled * flattened, axis=1), "head")
    grad_flat = inverse[:, None] * scaled - flattened * (inverse**3 * products / width_all)[:, None]
    grad_mixture = grad_flat.astype(jnp.bfloat16).reshape(layout)
    back_state = jnp.einsum(
        "thd,the->hde", q_heads, grad_mixture, preferred_element_type=jnp.float32
    )
    after = carried_in(back_state, "ctx", add_pair, jnp.zeros_like(back_state), True)
    after_round = after.astype(jnp.bfloat16)
    grad_scores = jnp.einsum(
        "the,she->hts", grad_mixture, v_heads, preferred_element_type=jnp.float32
    )
    grad_weights = jnp.where(causal[None], grad_scores, 0.0).astype(jnp.bfloat16)
    grad_q = jnp.einsum("hts,shd->thd", grad_weights, k_heads, preferred_element_type=jnp.float32)
    grad_q = grad_q + jnp.einsum(
        "the,hde->thd", grad_mixture, state_round, preferred_element_type=jnp.float32
    )
    grad_k = jnp.einsum("hts,thd->shd", grad_weights, q_heads, preferred_element_type=jnp.float32)
    grad_k = grad_k + jnp.einsum(
        "she,hde->shd", v_heads, after_round, preferred_element_type=jnp.float32
    )
    grad_v = jnp.einsum("hts,the->she", weights, grad_mixture, preferred_element_type=jnp.float32)
    grad_v = grad_v + jnp.einsum(
        "shd,hde->she", k_heads, after_round, preferred_element_type=jnp.float32
    )
    shape_out = (length, heads_here * HEAD_DIM)
    return (
        attended,
        grad_q.astype(jnp.bfloat16).reshape(shape_out),
        grad_k.astype(jnp.bfloat16).reshape(shape_out),
        grad_v.astype(jnp.bfloat16).reshape(shape_out),
    )


def solution(mesh):
    placed = (P("ctx", "head"), P("ctx", "head"), P("ctx", "head"), P("head"), P("ctx", "head"))
    return jax.shard_map(
        body,
        mesh=mesh,
        in_specs=placed,
        out_specs=(P("ctx", "head"), P("ctx", "head"), P("ctx", "head"), P("ctx", "head")),
        check_vma=False,
    )
```

profile of v0, /device:TPU:1, one launch (start us, length us, event | category | flops | bytes accessed | tf_op | source)
XLA Modules:
  0.0 487.9 jit_solution(4331954591690999653)
XLA Ops:
  7.2 2.6 copy.65
  9.8 1.6 copy.37
  11.5 1.2 fusion.7
  12.9 2.5 select_convert_fusion.1
  15.5 2.0 copy-done.1
  17.4 2.9 fusion.2
  20.3 139.3 %all-gather.5.cloned.1.call-done = f32[512,128,128]{2,1,0:T(8,128)} async-done(((f32[8,128,128]{2,1,0:T(8,128)}), f32[512,128,128]{2,1,0:T(8,128)}) %all-gather.5.cloned.1.call-update) | async-done | bytes 33554448 | tf_op jit(solution)/shard_map/all_gather | solution.py:17
  159.7 1.2 while.22
  159.7 1.2 bitcast_add_fusion.7
  160.9 3.5 multiply_reduce_fusion.1
  164.3 3.0 copy.41
  167.4 1.9 multiply_reduce_fusion
  169.3 8.5 %all-reduce = (f32[512]{0:T(512)S(1)}, f32[512]{0:T(512)S(1)}) all-reduce(f32[512]{0:T(512)S(1)} %get-tuple-element.119, f32[512]{0:T(512)S(1)} %multiply_reduce_fusion), channel_id=1, replica_groups=mesh['ctx'=64,'head'=4] {'head'}, use_global_device_ids=true, to_apply=%region_3.4 | all-reduce | flops 1024 | bytes 8192 | tf_op jit(solution)/shard_map/psum | solution.py:56
  177.8 3.5 subtract_convert_fusion
  181.3 1.5 copy.61
  184.3 2.7 select_convert_fusion
  187.0 1.5 fusion.31
  189.1 1.4 fusion.1
  190.5 2.3 copy.56
  192.8 4.3 fusion.32
  197.0 197.2 %all-gather.7.cloned.1.call-done = f32[512,128,128]{2,1,0:T(8,128)} async-done(((f32[8,128,128]{2,1,0:T(8,128)}), f32[512,128,128]{2,1,0:T(8,128)}) %all-gather.7.cloned.1.call-update) | async-done | bytes 33554448 | tf_op jit(solution)/shard_map/all_gather | solution.py:17
  394.3 74.0 %while.23 = (s32[]{:T(128)}, f32[8,128,128]{2,1,0:T(8,128)S(1)}, s32[]{:T(128)}, f32[64,8,128,128]{3,2,1,0:T(8,128)}, s32[]{:T(128)}, /*index=5*/s32[]{:T(128)}, s32[]{:T(128)}, s32[]{:T(128)}) while((s32[]{:T(128)}, f32[8,128,128]{2,1,0:T(8,128)S(1)}, s32[]{:T(128)}, f32[64,8,128,128]{3,2,1,0:T(8,128)}, s32[]{:T(128)}, /*index=5*/s32[]{:T(128)}, ...), condition=%wide.region_7.8_spmd, body=%wide.region_6.7_spmd.sunk | while | flops 131078 | bytes 1573007 | solution.py:24
  394.3 1.3 bitcast_add_fusion.8
  406.3 1.2 bitcast_add_fusion.8
  407.5 1.2 bitcast_add_fusion.8
  408.7 1.2 bitcast_add_fusion.8
  409.9 1.2 bitcast_add_fusion.8
  468.3 1.8 fusion.4
  470.9 1.5 add_convert_fusion
  472.4 2.4 copy.58
  474.8 4.0 fusion
  478.8 2.3 copy.57
  (90 shorter events, 69.8 us)
Async XLA Ops:
  7.2 5.8 %copy-start = (bf16[512,1024]{1,0:T(8,128)(2,1)S(1)}, bf16[512,1024]{1,0:T(8,128)(2,1)}, u32[]{:S(2)}) copy-start(bf16[512,1024]{1,0:T(8,128)(2,1)} %param.9) | copy-start | bytes 3145732
  7.2 152.5 %all-gather.5.cloned.1.call-start = ((), (), s32[]{:S(2)}) async-start(), calls=%async_computation | async-start | bytes 34078720 | tf_op jit(solution)/shard_map/all_gather | solution.py:17
  7.2 4.3 copy-start.3
  11.5 4.0 copy-start.5
  12.8 381.5 %all-gather.7.cloned.1.call-start = ((), (), s32[]{:S(2)}) async-start(), calls=%async_computation.1 | async-start | bytes 34078720 | tf_op jit(solution)/shard_map/all_gather | solution.py:17
  15.5 2.0 copy-start.1
  164.3 3.0 copy-start.9
  164.3 3.0 copy-start.11
  184.3 2.7 copy-start.6
  187.0 2.1 copy-start.2
  394.3 74.0 %copy-start.4 = (bf16[512,1024]{1,0:T(8,128)(2,1)S(1)}, bf16[512,1024]{1,0:T(8,128)(2,1)}, u32[]{:S(2)}) copy-start(bf16[512,1024]{1,0:T(8,128)(2,1)} %param.11) | copy-start | bytes 3145732
  468.3 1.9 copy-start.7
  468.3 2.6 copy-start.10
  472.4 2.4 copy-start.8
Sparse Core Ops, SparseCore 0:
  12.9 146.6 all-gather.4
  184.4 209.8 all-gather.6
where the time goes:
time: 491 us; the launch traced here: 488 us
  waiting for transfers between devices  337 us (69%)
  other arithmetic  79.3 us (16%)
  matrix products  27.7 us (6%)
  local copies, waits for them, and re-layouts  20.1 us (4%)
  between operations  14.2 us (3%)
  blocking collectives  8.46 us (2%)
    all_gather x2, waiting for transfers between devices, carried_in(): gathered = lax.all_gather(part, axis)  337 us
    add x63, other arithmetic, add_pair(): return earlier + later  73.7 us
    unnamed x28, local copies, waits for them, and re-layouts  12.9 us
  transfers between devices with their start and end apart: 2, of which 2 were waited for; matrix products, arithmetic and copies ran while one was open for 4% of the time, Pallas kernels for 0%

commit v1 on v0

v1 whole, which is shorter than its diff:
```python
import functools

import jax
import jax.numpy as jnp
from jax import lax
from jax.experimental import pallas as pl
from jax.experimental.pallas import tpu as pltpu
from jax.sharding import PartitionSpec as P

HEADS = 32
HEAD_DIM = 128
EPSILON = 1e-05
BF = jnp.bfloat16
F32 = jnp.float32

CORES = 2


def dot(a, b, ca, cb):
    return lax.dot_general(a, b, (((ca,), (cb,)), ((), ())), preferred_element_type=F32)


def call(kernel, outs, args, flops, vmem=24):
    whole = pl.BlockSpec(memory_space=pltpu.VMEM)
    nbytes = sum(a.size * a.dtype.itemsize for a in args)
    nbytes += sum(o.size * o.dtype.itemsize for o in outs)
    return pl.pallas_call(
        kernel,
        out_shape=outs,
        in_specs=[whole] * len(args),
        out_specs=[whole] * len(outs),
        compiler_params=pltpu.CompilerParams(vmem_limit_bytes=vmem << 20),
        cost_estimate=pl.CostEstimate(flops=flops, bytes_accessed=nbytes, transcendentals=0),
    )(*args)


def cols(h):
    return pl.ds(pl.multiple_of(h * HEAD_DIM, HEAD_DIM), HEAD_DIM)


def state_kernel(a_ref, b_ref, s_ref):
    heads = a_ref.shape[1] // HEAD_DIM

    def one(h, _):
        s_ref[cols(h), :] = dot(a_ref[:, cols(h)], b_ref[:, cols(h)], 0, 0)
        return 0

    lax.fori_loop(0, heads, one, 0)


def triangle(n):
    rows = lax.broadcasted_iota(jnp.int32, (n, n), 0)
    return lax.broadcasted_iota(jnp.int32, (n, n), 1) <= rows


def lower(a, b):
    n = a.shape[0] // 2
    keep = triangle(n)
    top = jnp.where(keep, dot(a[:n], b[:n], 1, 1), 0.0).astype(BF)
    left = dot(a[n:], b[:n], 1, 1).astype(BF)
    right = jnp.where(keep, dot(a[n:], b[n:], 1, 1), 0.0).astype(BF)
    return top, left, right


def times(w, v):
    n = v.shape[0] // 2
    top, left, right = w
    return dot(top, v[:n], 1, 0), dot(left, v[:n], 1, 0) + dot(right, v[n:], 1, 0)


def times_t(w, v):
    n = v.shape[0] // 2
    top, left, right = w
    return dot(top, v[:n], 0, 0) + dot(left, v[n:], 0, 0), dot(right, v[n:], 0, 0)


def intra_kernel(q_ref, k_ref, v_ref, o_ref):
    n = q_ref.shape[0] // 2

    def one(h, _):
        c = cols(h)
        w = lower(q_ref[:, c], k_ref[:, c])
        a, b = times(w, v_ref[:, c])
        o_ref[:n, c] = a
        o_ref[n:, c] = b
        return 0

    lax.fori_loop(0, q_ref.shape[1] // HEAD_DIM, one, 0)


def mix_kernel(q_ref, s_ref, i_ref, c_ref, g_ref, m_ref, p_ref, sq_ref, pr_ref):
    length = q_ref.shape[0]
    sq_ref[...] = jnp.zeros_like(sq_ref)
    pr_ref[...] = jnp.zeros_like(pr_ref)

    def one(h, _):
        c = cols(h)
        m = i_ref[:, c] + dot(q_ref[:, c], s_ref[c, :].astype(BF), 1, 0)
        m_ref[:, c] = m
        sq_ref[...] += m * m
        pr_ref[...] += (c_ref[:, c].astype(F32) * g_ref[:, c]) * m
        return 0

    lax.fori_loop(0, q_ref.shape[1] // HEAD_DIM, one, 0)
    for i in range(length // 128):
        rows = pl.ds(i * 128, 128)
        p_ref[pl.ds(i, 1), :] = jnp.sum(sq_ref[rows, :].T, axis=0, keepdims=True)
        p_ref[pl.ds(4 + i, 1), :] = jnp.sum(pr_ref[rows, :].T, axis=0, keepdims=True)


def spread(row):
    return jnp.broadcast_to(row, (128, 128)).T


def grad_kernel(q_ref, m_ref, c_ref, g_ref, p0, p1, p2, p3, gm_ref, b_ref, n_ref, inv_ref, cf_ref):
    width = HEADS * HEAD_DIM
    sums = p0[...] + p1[...] + p2[...] + p3[...]
    inverse = lax.rsqrt(sums[:4] / width + EPSILON)
    coef = inverse * inverse * inverse * sums[4:] / width
    for i in range(4):
        rows = pl.ds(i * 128, 128)
        inv_ref[rows, :] = spread(inverse[i : i + 1])
        cf_ref[rows, :] = spread(coef[i : i + 1])
    n_ref[...] = inv_ref[...]

    def one(h, _):
        c = cols(h)
        scaled = c_ref[:, c].astype(F32) * g_ref[:, c]
        gm = (inv_ref[...] * scaled - m_ref[:, c] * cf_ref[...]).astype(BF)
        gm_ref[:, c] = gm
        b_ref[c, :] = dot(q_ref[:, c], gm, 0, 0)
        return 0

    lax.fori_loop(0, q_ref.shape[1] // HEAD_DIM, one, 0)


def back_kernel(q_ref, k_ref, v_ref, gm_ref, s_ref, m_ref, n_ref, g_ref, at_ref, gq_ref, gk_ref, gv_ref):
    n = q_ref.shape[0] // 2

    def one(h, _):
        c = cols(h)
        at_ref[:, c] = (m_ref[:, c] * n_ref[...] * g_ref[:, c]).astype(BF)
        q, k, v, gm = q_ref[:, c], k_ref[:, c], v_ref[:, c], gm_ref[:, c]
        gw = lower(gm, v)
        a, b = times(gw, k)
        s = s_ref[c, :].astype(BF)
        gq_ref[:n, c] = (a + dot(gm[:n], s, 1, 1)).astype(BF)
        gq_ref[n:, c] = (b + dot(gm[n:], s, 1, 1)).astype(BF)
        a, b = times_t(gw, q)
        gk_ref[:n, c] = a
        gk_ref[n:, c] = b
        a, b = times_t(lower(q, k), gm)
        gv_ref[:n, c] = a
        gv_ref[n:, c] = b
        return 0

    lax.fori_loop(0, q_ref.shape[1] // HEAD_DIM, one, 0)


def last_kernel(k_ref, v_ref, a_ref, gki_ref, gvi_ref, gk_ref, gv_ref):
    def one(h, _):
        c = cols(h)
        a = a_ref[c, :].astype(BF)
        gk_ref[:, c] = (gki_ref[:, c] + dot(v_ref[:, c], a, 1, 1)).astype(BF)
        gv_ref[:, c] = (gvi_ref[:, c] + dot(k_ref[:, c], a, 1, 0)).astype(BF)
        return 0

    lax.fori_loop(0, k_ref.shape[1] // HEAD_DIM, one, 0)


def running_kernel(reverse, g_ref, o_ref):
    n = g_ref.shape[0]
    total = jnp.zeros(g_ref.shape[1:], F32)
    order = list(range(n))
    if reverse:
        order.reverse()
    for i in order:
        o_ref[i] = total
        if i != order[-1]:
            total = total + g_ref[i]


def carried(part, reverse):
    count = lax.axis_size("ctx")
    chips = count // CORES
    core = lax.rem(lax.axis_index("ctx"), CORES)
    swap = [(i, i ^ 1) for i in range(count)]
    groups = [[i * CORES + c for i in range(chips)] for c in range(CORES)]
    half = part.shape[0] // 2
    first, second = part[:half], part[half:]
    keep = jnp.where(core == 0, first, second)
    other = lax.ppermute(jnp.where(core == 0, second, first), "ctx", swap)
    ahead = jnp.where((core == 0) != reverse, keep, other)
    pieces = (keep + other).reshape(chips, -1, HEAD_DIM)
    pieces = lax.all_to_all(pieces, "ctx", 0, 0, axis_index_groups=groups)
    (pieces,) = call(
        functools.partial(running_kernel, reverse),
        [jax.ShapeDtypeStruct(pieces.shape, F32)],
        [pieces],
        pieces.size,
        4,
    )
    pieces = lax.all_to_all(pieces, "ctx", 0, 0, axis_index_groups=groups)
    near = pieces.reshape(half, HEAD_DIM)
    far = near + ahead
    mine = jnp.where((core == 0) != reverse, near, far)
    theirs = jnp.where((core == 0) != reverse, far, near)
    theirs = lax.ppermute(theirs, "ctx", swap)
    return jnp.concatenate(
        [jnp.where(core == 0, mine, theirs), jnp.where(core == 0, theirs, mine)], axis=0
    )


def body(query, keys, values, gain, cotangent):
    length, width = query.shape
    square = 2 * length * length * width
    small = 2 * length * HEAD_DIM * width
    gain = gain.reshape(1, width)
    shape = lambda dtype: jax.ShapeDtypeStruct((length, width), dtype)
    states = jax.ShapeDtypeStruct((width, HEAD_DIM), F32)
    rows = jax.ShapeDtypeStruct((8, 128), F32)

    (local,) = call(state_kernel, [states], [keys, values], small)
    before = carried(local, False)
    (intra,) = call(intra_kernel, [shape(F32)], [query, keys, values], 2 * square)
    lanes = pltpu.VMEM((length, 128), F32)
    whole = pl.BlockSpec(memory_space=pltpu.VMEM)
    mixture, sums = pl.pallas_call(
        mix_kernel,
        out_shape=[shape(F32), rows],
        in_specs=[whole] * 5,
        out_specs=[whole] * 2,
        scratch_shapes=[lanes, lanes],
        compiler_params=pltpu.CompilerParams(vmem_limit_bytes=24 << 20),
    )(query, before, intra, cotangent, gain)
    heads = lax.axis_size("head")
    others = [
        lax.ppermute(sums, "head", [(i, i ^ j) for i in range(heads)]) for j in (1, 3, 2)
    ]
    grad_mixture, back, inverse = pl.pallas_call(
        grad_kernel,
        out_shape=[shape(BF), states, jax.ShapeDtypeStruct((length, 128), F32)],
        in_specs=[whole] * 8,
        out_specs=[whole] * 3,
        scratch_shapes=[lanes, lanes],
        compiler_params=pltpu.CompilerParams(vmem_limit_bytes=24 << 20),
    )(query, mixture, cotangent, gain, sums, *others)
    after = carried(back, True)
    attended, grad_q, grad_k, grad_v = call(
        back_kernel,
        [shape(BF), shape(BF), shape(F32), shape(F32)],
        [query, keys, values, grad_mixture, before, mixture, inverse, gain],
        5 * square,
    )
    grad_k, grad_v = call(
        last_kernel, [shape(BF), shape(BF)], [keys, values, after, grad_k, grad_v], 2 * small
    )
    return attended, grad_q, grad_k, grad_v


def solution(mesh):
    spec = P("ctx", "head")
    return jax.shard_map(
        body,
        mesh=mesh,
        in_specs=(spec, spec, spec, P("head"), spec),
        out_specs=(spec,) * 4,
        check_vma=False,
    )
```

time: 491 us -> 122 us (0.25)
  waiting for transfers between devices: 337 us -> 15.6 us
  other arithmetic: 79.3 us -> 3.19 us
  blocking collectives: 8.46 us -> 50.6 us
  matrix products: 27.7 us -> 0 us
  Pallas kernels: 0 us -> 23.2 us
  starting transfers between devices: 0.08 us -> 20.6 us
  between operations: 14.2 us -> 0.86 us
  local copies, waits for them, and re-layouts: 20.1 us -> 7.62 us
    all_gather x2 -> x0, waiting for transfers between devices: 337 us -> none  [carried_in(): gathered = lax.all_gather(part, axis)]
    add x63 -> x2, other arithmetic: 73.7 us -> 0.86 us  [carried(): pieces = (keep + other).reshape(chips, -1, HEAD_DIM)]
    all_to_all x0 -> x3, blocking collectives: none -> 50.6 us  [carried(): pieces = lax.all_to_all(pieces, 'ctx', 0, 0, axis_index_groups=groups)]
    dot_general x12 -> x0, matrix products: 27.7 us -> none  [the longest x1 4.28 us: body(): jnp.einsum('hts,the->she', weights, grad_mixture, preferred_element_type=...]
    pallas_call x0 -> x8, Pallas kernels: none -> 23.2 us  [the longest x6 18.6 us: call(): pl.pallas_call(kernel, out_shape=outs, in_specs=[whole] * len(args), out_...]
    ppermute x0 -> x7, starting transfers between devices: none -> 15.9 us  [the longest x2 7.22 us: carried(): theirs = lax.ppermute(theirs, 'ctx', swap)]
    all_to_all x0 -> x1, waiting for transfers between devices: none -> 10.4 us  [carried(): pieces = lax.all_to_all(pieces, 'ctx', 0, 0, axis_index_groups=groups)]
    psum x1 -> x0, blocking collectives: 8.46 us -> none  [body(): squares = lax.psum(jnp.sum(flattened * flattened, axis=1), 'head')]
  transfers between devices with their start and end apart: 2 -> 8, of which waited for: 2 -> 5; matrix products, arithmetic and copies ran while one was open for 4% -> 0% of each run, Pallas kernels for 0% -> 10%
where the time goes in v1:
time: 122 us
  blocking collectives  50.6 us (41%)
  Pallas kernels  23.2 us (19%)
  starting transfers between devices  20.6 us (17%)
  waiting for transfers between devices  15.6 us (13%)
  local copies, waits for them, and re-layouts  7.62 us (6%)
  other arithmetic  3.19 us (3%)
    all_to_all x3, blocking collectives, carried(): pieces = lax.all_to_all(pieces, 'ctx', 0, 0, axis_index_groups=groups)  50.6 us
    pallas_call x6, Pallas kernels, call(): pl.pallas_call(kernel, out_shape=outs, in_specs=[whole] * len(args), out_...  18.6 us
    all_to_all x1, waiting for transfers between devices, carried(): pieces = lax.all_to_all(pieces, 'ctx', 0, 0, axis_index_groups=groups)  10.4 us
    unnamed x32, local copies, waits for them, and re-layouts  7.62 us
    ppermute x2, starting transfers between devices, carried(): theirs = lax.ppermute(theirs, 'ctx', swap)  7.22 us
    ppermute x2, starting transfers between devices, carried(): other = lax.ppermute(jnp.where(core == 0, second, first), 'ctx', swap)  4.87 us
    all_to_all x1, starting transfers between devices, carried(): pieces = lax.all_to_all(pieces, 'ctx', 0, 0, axis_index_groups=groups)  4.73 us
    ppermute x3, starting transfers between devices, body(): lax.ppermute(sums, 'head', [(i, i ^ j) for i in range(heads)])  3.78 us
  transfers between devices with their start and end apart: 8, of which 5 were waited for; matrix products, arithmetic and copies ran while one was open for 0% of the time, Pallas kernels for 10%

profile of v1, /device:TPU:1, one launch (start us, length us, event | category | flops | bytes accessed | tf_op | source)
XLA Modules:
  0.0 121.6 jit_solution(17857501684297401398)
XLA Ops:
  0.6 1.2 copy-done.1
  1.9 1.2 %copy-done.3 = bf16[512,1024]{1,0:T(8,128)(2,1)S(1)} copy-done((bf16[512,1024]{1,0:T(8,128)(2,1)S(1)}, bf16[512,1024]{1,0:T(8,128)(2,1)}, u32[]{:S(2)}) %copy-start.3) | copy-done | bytes 1048600
  3.1 2.1 %shard_map.84 = f32[1024,128]{1,0:T(8,128)S(1)} custom-call(bf16[512,1024]{1,0:T(8,128)(2,1)S(1)} %copy-done.1, bf16[512,1024]{1,0:T(8,128)(2,1)S(1)} %copy-done.3), custom_call_target="tpu_custom_call" | custom-call | flops 134217728 | bytes 2621440 | tf_op jit(solution)/shard_map/pallas_call | solution.py:27
  5.3 3.3 %collective-permute-start = (f32[512,128]{1,0:T(8,128)S(1)}, f32[512,128]{1,0:T(8,128)S(1)}, u32[]{:S(2)}, u32[]{:S(2)}) collective-permute-start(f32[512,128]{1,0:T(8,128)S(1)} %slice_select_fusion), channel_id=1, source_target_pairs={{0,4},{4,0},{8,12},{12,8},{16,20},{20,16},{24,28},{28,24},{32,36},... | collective-permute-start | bytes 786440 | tf_op jit(solution)/shard_map/ppermute | solution.py:192
  8.6 1.2 collective-permute-done
  9.8 20.7 %all_to_all.20.g_ref = f32[32,16,128]{2,1,0:T(8,128)S(1)} all-to-all(f32[32,16,128]{2,1,0:T(8,128)S(1)} %bitcast.17), channel_id=1, replica_groups={{0,8,16,24,32,40,48,56,64,72,80,88,96,104,112,120,128,136,144,152,160,1..., dimensions={0} | all-to-all | bytes 524288 | tf_op jit(solution)/shard_map/all_to_all | solution.py:195
  30.5 15.0 %all_to_all.21 = f32[32,16,128]{2,1,0:T(8,128)S(1)} all-to-all(f32[32,16,128]{2,1,0:T(8,128)S(1)} %shard_map.85), channel_id=1, replica_groups={{0,8,16,24,32,40,48,56,64,72,80,88,96,104,112,120,128,136,144,152,160,1..., dimensions={0} | all-to-all | bytes 524288 | tf_op jit(solution)/shard_map/all_to_all | solution.py:203
  45.6 3.4 %collective-permute-start.1 = (f32[512,128]{1,0:T(8,128)S(1)}, f32[512,128]{1,0:T(8,128)S(1)}, u32[]{:S(2)}, u32[]{:S(2)}) collective-permute-start(f32[512,128]{1,0:T(8,128)S(1)} %add_select_fusion.2), channel_id=1, source_target_pairs={{0,4},{4,0},{8,12},{12,8},{16,20},{20,16},{24,28},{28,24},{32,36},... | collective-permute-start | bytes 786440 | tf_op jit(solution)/shard_map/ppermute | solution.py:208
  48.9 3.5 %shard_map.86.i_ref = f32[512,1024]{1,0:T(8,128)S(1)} custom-call(bf16[512,1024]{1,0:T(8,128)(2,1)S(1)} %copy-done, bf16[512,1024]{1,0:T(8,128)(2,1)S(1)} %copy-done.1, bf16[512,1024]{1,0:T(8,128)(2,1)S(1)} %copy-done.3), custom_call_target="tpu_custom_call" | custom-call | flops 1073741824 | bytes 5242880 | tf_op jit(solution)/shard_map/pallas_call | solution.py:27
  52.5 0.1 broadcast_select_fusion.4
  52.6 1.3 %copy-done.5 = bf16[512,1024]{1,0:T(8,128)(2,1)S(1)} copy-done((bf16[512,1024]{1,0:T(8,128)(2,1)S(1)}, bf16[512,1024]{1,0:T(8,128)(2,1)}, u32[]{:S(2)}) %copy-start.5) | copy-done | bytes 1048600
  53.9 2.0 %shard_map.87 = (f32[512,1024]{1,0:T(8,128)S(1)}, f32[8,128]{1,0:T(8,128)S(1)}) custom-call(bf16[512,1024]{1,0:T(8,128)(2,1)S(1)} %copy-done, f32[1024,128]{1,0:T(8,128)S(1)} %pad_maximum_fusion.s_ref, f32[512,1024]{1,0:T(8,128)S(1)} %shard_map.86.i_ref, bf16[512,1024]{1,0:T(8,128)(2,1)S(1)} %copy-done.5, f32[1,1024]{1,0:T(1,128)S(1)} %bitcast.14), custom_call_target="tpu_custom_call" | custom-call | tf_op jit(solution)/shard_map/pallas_call | solution.py:228
  55.9 3.0 %collective-permute-start.4 = (f32[8,128]{1,0:T(8,128)S(1)}, f32[8,128]{1,0:T(8,128)S(1)}, u32[]{:S(2)}, u32[]{:S(2)}) collective-permute-start(f32[8,128]{1,0:T(8,128)S(1)} %get-tuple-element.16.p0), channel_id=1, source_target_pairs={{0,2},{1,3},{2,0},{3,1},{4,6},{5,7},{6,4},{7,5},{8,10},{9,11},{10,... | collective-permute-start | bytes 12296 | tf_op jit(solution)/shard_map/ppermute | solution.py:238
  58.9 0.8 collective-permute-start.3
  59.7 0.3 collective-permute-done.4.p3
  60.0 2.6 %collective-permute-done.3.p2 = f32[8,128]{1,0:T(8,128)S(1)} collective-permute-done((f32[8,128]{1,0:T(8,128)S(1)}, f32[8,128]{1,0:T(8,128)S(1)}, u32[]{:S(2)}, u32[]{:S(2)}) %collective-permute-start.3) | collective-permute-done | bytes 4128 | tf_op jit(solution)/shard_map/ppermute | solution.py:238
  62.6 2.6 %shard_map.88 = (bf16[512,1024]{1,0:T(8,128)(2,1)S(1)}, f32[1024,128]{1,0:T(8,128)S(1)}, f32[512,128]{1,0:T(8,128)S(1)}) custom-call(bf16[512,1024]{1,0:T(8,128)(2,1)S(1)} %copy-done, f32[512,1024]{1,0:T(8,128)S(1)} %get-tuple-element.15.m_ref, bf16[512,1024]{1,0:T(8,128)(2,1)S(1)} %copy-done.5, f32[1,1024]{1,0:T(1,128)S(1)} %bitcast.15, ...), custom_call_target="tpu_custom_call" | custom-call | tf_op jit(solution)/shard_map/pallas_call | solution.py:240
  65.2 1.5 %collective-permute-start.5 = (f32[512,128]{1,0:T(8,128)S(1)}, f32[512,128]{1,0:T(8,128)S(1)}, u32[]{:S(2)}, u32[]{:S(2)}) collective-permute-start(f32[512,128]{1,0:T(8,128)S(1)} %slice_select_fusion.2), channel_id=1, source_target_pairs={{0,4},{4,0},{8,12},{12,8},{16,20},{20,16},{24,28},{28,24},{32,36},... | collective-permute-start | bytes 786440 | tf_op jit(solution)/shard_map/ppermute | solution.py:192
  66.8 1.2 collective-permute-done.5
  68.0 0.8 fusion
  68.8 14.9 %all_to_all.22.g_ref = f32[32,16,128]{2,1,0:T(8,128)S(1)} all-to-all(f32[32,16,128]{2,1,0:T(8,128)S(1)} %bitcast.18), channel_id=1, replica_groups={{0,8,16,24,32,40,48,56,64,72,80,88,96,104,112,120,128,136,144,152,160,1..., dimensions={0} | all-to-all | bytes 524288 | tf_op jit(solution)/shard_map/all_to_all | solution.py:195
  83.7 0.7 shard_map.90
  84.4 4.7 %all-to-all-start.3 = ((f32[32,16,128]{2,1,0:T(8,128)}), f32[32,16,128]{2,1,0:T(8,128)}, u32[]{:S(2)}, u32[]{:S(2)}) async-start(f32[32,16,128]{2,1,0:T(8,128)} %shard_map.90), calls=%async_computation.3 | async-start | bytes 524288 | tf_op jit(solution)/shard_map/all_to_all | solution.py:203
  89.2 10.4 %all-to-all-done.3 = f32[32,16,128]{2,1,0:T(8,128)} async-done(((f32[32,16,128]{2,1,0:T(8,128)}), f32[32,16,128]{2,1,0:T(8,128)}, u32[]{:S(2)}, u32[]{:S(2)}) %all-to-all-start.3) | async-done | bytes 262176 | tf_op jit(solution)/shard_map/all_to_all | solution.py:203
  99.5 1.1 add_select_fusion
  100.6 3.8 %collective-permute-start.6 = (f32[512,128]{1,0:T(8,128)S(1)}, f32[512,128]{1,0:T(8,128)S(1)}, u32[]{:S(2)}, u32[]{:S(2)}) collective-permute-start(f32[512,128]{1,0:T(8,128)S(1)} %add_select_fusion), channel_id=1, source_target_pairs={{0,4},{4,0},{8,12},{12,8},{16,20},{20,16},{24,28},{28,24},{32,36},... | collective-permute-start | bytes 786440 | tf_op jit(solution)/shard_map/ppermute | solution.py:208
  104.5 1.6 %copy-done.7 = f32[512,1024]{1,0:T(8,128)S(1)} copy-done((f32[512,1024]{1,0:T(8,128)S(1)}, f32[512,1024]{1,0:T(8,128)}, u32[]{:S(2)}) %copy-start.7) | copy-done | bytes 2097176
  106.1 1.0 copy-done.9
  107.1 1.2 %copy-done.12 = bf16[512,1024]{1,0:T(8,128)(2,1)S(1)} copy-done((bf16[512,1024]{1,0:T(8,128)(2,1)S(1)}, bf16[512,1024]{1,0:T(8,128)(2,1)}, u32[]{:S(2)}) %copy-start.12) | copy-done | bytes 1048600
  108.3 9.0 %shard_map.89 = (bf16[512,1024]{1,0:T(8,128)(2,1)}, bf16[512,1024]{1,0:T(8,128)(2,1)}, f32[512,1024]{1,0:T(8,128)S(1)}, f32[512,1024]{1,0:T(8,128)S(1)}) custom-call(bf16[512,1024]{1,0:T(8,128)(2,1)S(1)} %copy-done, bf16[512,1024]{1,0:T(8,128)(2,1)S(1)} %copy-done.2, bf16[512,1024]{1,0:T(8,128)(2,1)S(1)} %copy-done.4, bf16[512,1024]{1,0:T(8,128)(2,1)S(1)} %copy-done.12, ...), custom_call_target="tpu_custom_call" | custom-call | flops 2684354560 | bytes 13373440 | tf_op jit(solution)/shard_map/pallas_call | solution.py:27
  117.3 1.0 broadcast_select_fusion.2
  118.4 3.2 %shard_map.91 = (bf16[512,1024]{1,0:T(8,128)(2,1)}, bf16[512,1024]{1,0:T(8,128)(2,1)}) custom-call(bf16[512,1024]{1,0:T(8,128)(2,1)S(1)} %copy-done.2, bf16[512,1024]{1,0:T(8,128)(2,1)S(1)} %copy-done.4, f32[1024,128]{1,0:T(8,128)S(1)} %pad_maximum_fusion.1.a_ref, f32[512,1024]{1,0:T(8,128)S(1)} %get-tuple-element.22.gki_ref, ...), custom_call_target="tpu_custom_call" | custom-call | flops 268435456 | bytes 8912896 | tf_op jit(solution)/shard_map/pallas_call | solution.py:27
  (38 shorter events, 0.4 us)
Async XLA Ops:
  0.6 1.2 %copy-start.1 = (bf16[512,1024]{1,0:T(8,128)(2,1)S(1)}, bf16[512,1024]{1,0:T(8,128)(2,1)}, u32[]{:S(2)}) copy-start(bf16[512,1024]{1,0:T(8,128)(2,1)} %k_ref.5) | copy-start | bytes 3145732
  1.9 1.2 %copy-start.3 = (bf16[512,1024]{1,0:T(8,128)(2,1)S(1)}, bf16[512,1024]{1,0:T(8,128)(2,1)}, u32[]{:S(2)}) copy-start(bf16[512,1024]{1,0:T(8,128)(2,1)} %v_ref.5) | copy-start | bytes 3145732
  5.3 43.7 %copy-start = (bf16[512,1024]{1,0:T(8,128)(2,1)S(1)}, bf16[512,1024]{1,0:T(8,128)(2,1)}, u32[]{:S(2)}) copy-start(bf16[512,1024]{1,0:T(8,128)(2,1)} %q_ref.7) | copy-start | bytes 3145732
  5.3 4.5 %collective-permute-start = (f32[512,128]{1,0:T(8,128)S(1)}, f32[512,128]{1,0:T(8,128)S(1)}, u32[]{:S(2)}, u32[]{:S(2)}) collective-permute-start(f32[512,128]{1,0:T(8,128)S(1)} %slice_select_fusion), channel_id=1, source_target_pairs={{0,4},{4,0},{8,12},{12,8},{16,20},{20,16},{24,28},{28,24},{32,36},... | collective-permute-start | bytes 786440 | tf_op jit(solution)/shard_map/ppermute | solution.py:192
  45.6 6.9 %collective-permute-start.1 = (f32[512,128]{1,0:T(8,128)S(1)}, f32[512,128]{1,0:T(8,128)S(1)}, u32[]{:S(2)}, u32[]{:S(2)}) collective-permute-start(f32[512,128]{1,0:T(8,128)S(1)} %add_select_fusion.2), channel_id=1, source_target_pairs={{0,4},{4,0},{8,12},{12,8},{16,20},{20,16},{24,28},{28,24},{32,36},... | collective-permute-start | bytes 786440 | tf_op jit(solution)/shard_map/ppermute | solution.py:208
  52.4 1.4 %copy-start.5 = (bf16[512,1024]{1,0:T(8,128)(2,1)S(1)}, bf16[512,1024]{1,0:T(8,128)(2,1)}, u32[]{:S(2)}) copy-start(bf16[512,1024]{1,0:T(8,128)(2,1)} %c_ref.3) | copy-start | bytes 3145732
  52.5 1.4 %copy-start.10 = (f32[1024]{0:T(1024)S(1)}, f32[1024]{0:T(1024)}, u32[]{:S(2)}) copy-start(f32[1024]{0:T(1024)} %param.8) | copy-start | bytes 12292
  52.6 3.3 %copy-start.8 = (f32[1024,128]{1,0:T(8,128)}, f32[1024,128]{1,0:T(8,128)S(1)}, u32[]{:S(2)}) copy-start(f32[1024,128]{1,0:T(8,128)S(1)} %pad_maximum_fusion.s_ref) | copy-start | bytes 1572868
  55.9 9.3 %copy-start.6 = (f32[512,1024]{1,0:T(8,128)}, f32[512,1024]{1,0:T(8,128)S(1)}, u32[]{:S(2)}) copy-start(f32[512,1024]{1,0:T(8,128)S(1)} %get-tuple-element.15.m_ref) | copy-start | bytes 6291460
  55.9 4.0 %collective-permute-start.4 = (f32[8,128]{1,0:T(8,128)S(1)}, f32[8,128]{1,0:T(8,128)S(1)}, u32[]{:S(2)}, u32[]{:S(2)}) collective-permute-start(f32[8,128]{1,0:T(8,128)S(1)} %get-tuple-element.16.p0), channel_id=1, source_target_pairs={{0,2},{1,3},{2,0},{3,1},{4,6},{5,7},{6,4},{7,5},{8,10},{9,11},{10,... | collective-permute-start | bytes 12296 | tf_op jit(solution)/shard_map/ppermute | solution.py:238
  58.9 3.7 %collective-permute-start.3 = (f32[8,128]{1,0:T(8,128)S(1)}, f32[8,128]{1,0:T(8,128)S(1)}, u32[]{:S(2)}, u32[]{:S(2)}) collective-permute-start(f32[8,128]{1,0:T(8,128)S(1)} %get-tuple-element.16.p0), channel_id=1, source_target_pairs={{0,3},{1,2},{2,1},{3,0},{4,7},{5,6},{6,5},{7,4},{8,11},{9,10},{10,... | collective-permute-start | bytes 12296 | tf_op jit(solution)/shard_map/ppermute | solution.py:238
  59.7 2.9 %collective-permute-start.2 = (f32[8,128]{1,0:T(8,128)S(1)}, f32[8,128]{1,0:T(8,128)S(1)}, u32[]{:S(2)}, u32[]{:S(2)}) collective-permute-start(f32[8,128]{1,0:T(8,128)S(1)} %get-tuple-element.16.p0), channel_id=1, source_target_pairs={{0,1},{1,0},{2,3},{3,2},{4,5},{5,4},{6,7},{7,6},{8,9},{9,8},{10,11... | collective-permute-start | bytes 12296 | tf_op jit(solution)/shard_map/ppermute | solution.py:238
  65.2 3.6 %copy-start.11 = (bf16[512,1024]{1,0:T(8,128)(2,1)}, bf16[512,1024]{1,0:T(8,128)(2,1)S(1)}, u32[]{:S(2)}) copy-start(bf16[512,1024]{1,0:T(8,128)(2,1)S(1)} %get-tuple-element.17.gm_ref) | copy-start | bytes 3145732
  65.2 39.2 %copy-start.2 = (bf16[512,1024]{1,0:T(8,128)(2,1)S(1)}, bf16[512,1024]{1,0:T(8,128)(2,1)}, u32[]{:S(2)}) copy-start(bf16[512,1024]{1,0:T(8,128)(2,1)} %k_ref.5) | copy-start | bytes 3145732
  65.2 39.2 %copy-start.4 = (bf16[512,1024]{1,0:T(8,128)(2,1)S(1)}, bf16[512,1024]{1,0:T(8,128)(2,1)}, u32[]{:S(2)}) copy-start(bf16[512,1024]{1,0:T(8,128)(2,1)} %v_ref.5) | copy-start | bytes 3145732
  65.2 2.7 %collective-permute-start.5 = (f32[512,128]{1,0:T(8,128)S(1)}, f32[512,128]{1,0:T(8,128)S(1)}, u32[]{:S(2)}, u32[]{:S(2)}) collective-permute-start(f32[512,128]{1,0:T(8,128)S(1)} %slice_select_fusion.2), channel_id=1, source_target_pairs={{0,4},{4,0},{8,12},{12,8},{16,20},{20,16},{24,28},{28,24},{32,36},... | collective-permute-start | bytes 786440 | tf_op jit(solution)/shard_map/ppermute | solution.py:192
  67.9 0.8 copy-start.13
  84.4 15.1 %all-to-all-start.3 = ((f32[32,16,128]{2,1,0:T(8,128)}), f32[32,16,128]{2,1,0:T(8,128)}, u32[]{:S(2)}, u32[]{:S(2)}) async-start(f32[32,16,128]{2,1,0:T(8,128)} %shard_map.90), calls=%async_computation.3 | async-start | bytes 524288 | tf_op jit(solution)/shard_map/all_to_all | solution.py:203
  100.6 16.7 %collective-permute-start.6 = (f32[512,128]{1,0:T(8,128)S(1)}, f32[512,128]{1,0:T(8,128)S(1)}, u32[]{:S(2)}, u32[]{:S(2)}) collective-permute-start(f32[512,128]{1,0:T(8,128)S(1)} %add_select_fusion), channel_id=1, source_target_pairs={{0,4},{4,0},{8,12},{12,8},{16,20},{20,16},{24,28},{28,24},{32,36},... | collective-permute-start | bytes 786440 | tf_op jit(solution)/shard_map/ppermute | solution.py:208
  104.5 1.6 %copy-start.7 = (f32[512,1024]{1,0:T(8,128)S(1)}, f32[512,1024]{1,0:T(8,128)}, u32[]{:S(2)}) copy-start(f32[512,1024]{1,0:T(8,128)} %copy-done.6) | copy-start | bytes 6291460
  106.1 1.0 copy-start.9
  107.1 1.2 %copy-start.12 = (bf16[512,1024]{1,0:T(8,128)(2,1)S(1)}, bf16[512,1024]{1,0:T(8,128)(2,1)}, u32[]{:S(2)}) copy-start(bf16[512,1024]{1,0:T(8,128)(2,1)} %copy-done.11) | copy-start | bytes 3145732
  108.3 9.0 %copy-start.14 = (f32[512,128]{1,0:T(8,128)S(1)}, f32[512,128]{1,0:T(8,128)}, u32[]{:S(2)}) copy-start(f32[512,128]{1,0:T(8,128)} %copy-done.13) | copy-start | bytes 786436
  108.3 9.0 %copy-start.15 = (f32[512,128]{1,0:T(8,128)S(1)}, f32[512,128]{1,0:T(8,128)}, u32[]{:S(2)}) copy-start(f32[512,128]{1,0:T(8,128)} %get-tuple-element.29) | copy-start | bytes 786436

commit v2 on v0

v2 whole, which is shorter than its diff:
```python
import functools

import jax
import jax.numpy as jnp
from jax import lax
from jax.experimental import pallas as pl
from jax.experimental.pallas import tpu as pltpu
from jax.sharding import PartitionSpec as P

HEADS = 32
HEAD_DIM = 128
EPSILON = 1e-05
BF = jnp.bfloat16
F32 = jnp.float32

X = 4
CORES = 2
PAIR = 2 * X

VMEM = pl.BlockSpec(memory_space=pltpu.VMEM)
HBM = pl.BlockSpec(memory_space=pltpu.HBM)
ANY = pl.BlockSpec(memory_space=pl.ANY)


def dot(a, b, ca, cb):
    return lax.dot_general(a, b, (((ca,), (cb,)), ((), ())), preferred_element_type=F32)


def call(kernel, outs, args, flops, after=(), ins=VMEM, out=VMEM, scratch=(), vmem=16):
    nbytes = sum(a.size * a.dtype.itemsize for a in args)
    nbytes += sum(o.size * o.dtype.itemsize for o in outs)

    def body(*refs):
        kernel(*refs[: len(args)], *refs[len(args) + len(after) :])

    return pl.pallas_call(
        body,
        out_shape=outs,
        in_specs=[ins] * len(args) + [ANY] * len(after),
        out_specs=[out] * len(outs),
        scratch_shapes=list(scratch),
        compiler_params=pltpu.CompilerParams(vmem_limit_bytes=vmem << 20),
        cost_estimate=pl.CostEstimate(flops=flops, bytes_accessed=nbytes, transcendentals=0),
    )(*args, *after)


def array(shape, dtype):
    return jax.ShapeDtypeStruct(shape, dtype)


def at(h):
    return slice(h * HEAD_DIM, (h + 1) * HEAD_DIM)


def my_core():
    return lax.rem(lax.axis_index("ctx"), CORES)


def put(h, half, value, keep_ref, send_ref):
    mine = my_core() == h // half
    rows = at(h % half)

    @pl.when(mine)
    def _():
        keep_ref[rows, :] = value

    @pl.when(jnp.logical_not(mine))
    def _():
        send_ref[rows, :] = value


def join(mine_ref, theirs_ref, out_ref):
    half = mine_ref.shape[0]
    first = my_core() == 0
    mine, theirs = mine_ref[...].astype(BF), theirs_ref[...].astype(BF)
    out_ref[:half] = jnp.where(first, mine, theirs)
    out_ref[half:] = jnp.where(first, theirs, mine)


CHUNK = 2


def state_kernel(a_hbm, b_hbm, keep_ref, send_ref, a_ref, b_ref, sems):
    heads = a_ref.shape[1] // HEAD_DIM
    copies = []
    for i in range(0, heads, CHUNK):
        c = slice(i * HEAD_DIM, (i + CHUNK) * HEAD_DIM)
        for j, (src, dst) in enumerate(((a_hbm, a_ref), (b_hbm, b_ref))):
            copy = pltpu.make_async_copy(src.at[:, c], dst.at[:, c], sems.at[i // CHUNK, j])
            copy.start()
            copies.append(copy)
    for h in range(heads):
        if h % CHUNK == 0:
            copies[h // CHUNK * 2].wait()
            copies[h // CHUNK * 2 + 1].wait()
        put(h, heads // 2, dot(a_ref[:, at(h)], b_ref[:, at(h)], 0, 0), keep_ref, send_ref)


def triangle(n, flip=False):
    rows = lax.broadcasted_iota(jnp.int32, (n, n), 0)
    cols = lax.broadcasted_iota(jnp.int32, (n, n), 1)
    return rows <= cols if flip else cols <= rows


def lower(a, b):
    n = a.shape[0] // 2
    keep = triangle(n)
    top = jnp.where(keep, dot(a[:n], b[:n], 1, 1), 0.0).astype(BF)
    left = dot(a[n:], b[:n], 1, 1).astype(BF)
    right = jnp.where(keep, dot(a[n:], b[n:], 1, 1), 0.0).astype(BF)
    return top, left, right


def lower_t(a, b):
    n = a.shape[0] // 2
    keep = triangle(n, True)
    top = jnp.where(keep, dot(b[:n], a[:n], 1, 1), 0.0).astype(BF)
    left = dot(b[:n], a[n:], 1, 1).astype(BF)
    right = jnp.where(keep, dot(b[n:], a[n:], 1, 1), 0.0).astype(BF)
    return top, left, right


def intra_kernel(heads, q_ref, k_ref, v_ref, qt_ref, wt_ref, o_ref):
    n = q_ref.shape[0] // 2
    for i, h in enumerate(heads):
        q, k, v = q_ref[:, at(h)], k_ref[:, at(h)], v_ref[:, at(h)]
        qt_ref[at(i), :] = q.T
        top, left, right = lower(q, k)
        o_ref[:n, at(i)] = dot(top, v[:n], 1, 0)
        o_ref[n:, at(i)] = dot(left, v[:n], 1, 0) + dot(right, v[n:], 1, 0)
        for j, block in enumerate(lower_t(q, k)):
            wt_ref[3 * i + j] = block


def mix_kernel(parts, *refs):
    q_ref, mine_ref, theirs_ref, c_ref, g_ref = refs[:5]
    i_refs = refs[5 : 5 + len(parts)]
    m_ref, r_ref, p_ref = refs[5 + len(parts) :]
    join(mine_ref, theirs_ref, r_ref)
    for i in range(q_ref.shape[0] // 128):
        rows = slice(i * 128, (i + 1) * 128)
        squares = jnp.zeros((128, HEAD_DIM), F32)
        products = jnp.zeros((128, HEAD_DIM), F32)
        for heads, i_ref in zip(parts, i_refs):
            for j, h in enumerate(heads):
                m = i_ref[rows, at(j)] + dot(q_ref[rows, at(h)], r_ref[at(h), :], 1, 0)
                m_ref[rows, at(h)] = m
                squares = squares + m * m
                products = products + (c_ref[rows, at(h)].astype(F32) * g_ref[:, at(h)]) * m
        p_ref[i : i + 1, :] = jnp.sum(squares.T, axis=0, keepdims=True)
        p_ref[4 + i : 5 + i, :] = jnp.sum(products.T, axis=0, keepdims=True)


def spread(row):
    return jnp.broadcast_to(row, (128, 128)).T


def grad_kernel(parts, *refs):
    m_ref, c_ref, g_ref, p0, p1, p2, p3 = refs[:7]
    t_refs = refs[7 : 7 + len(parts)]
    gm_ref, n_ref, keep_ref, send_ref = refs[7 + len(parts) :]
    width = HEADS * HEAD_DIM
    sums = p0[...] + p1[...] + p2[...] + p3[...]
    inverse = lax.rsqrt(sums[:4] / width + EPSILON)
    coef = inverse * inverse * inverse * sums[4:] / width
    count = m_ref.shape[1] // HEAD_DIM
    for i in range(4):
        rows = slice(i * 128, (i + 1) * 128)
        inv = spread(inverse[i : i + 1])
        cf = spread(coef[i : i + 1])
        n_ref[rows, :] = inv
        for h in range(count):
            scaled = c_ref[rows, at(h)].astype(F32) * g_ref[:, at(h)]
            gm_ref[rows, at(h)] = (inv * scaled - m_ref[rows, at(h)] * cf).astype(BF)
    for heads, t_ref in zip(parts, t_refs):
        for j, h in enumerate(heads):
            put(h, count // 2, dot(t_ref[at(j), :], gm_ref[:, at(h)], 1, 0), keep_ref, send_ref)


def back_kernel(heads, parts, *refs):
    q_ref, k_ref, v_ref, gm_ref, r_ref, m_ref, n_ref, g_ref = refs[:8]
    w_refs = refs[8 : 8 + len(parts)]
    at_ref, gq_ref, gk_ref, gv_ref = refs[8 + len(parts) :]
    n = q_ref.shape[0] // 2
    for i, h in enumerate(heads):
        at_ref[:, at(i)] = (m_ref[:, at(h)] * n_ref[...] * g_ref[:, at(h)]).astype(BF)
        q, k, v, gm = q_ref[:, at(h)], k_ref[:, at(h)], v_ref[:, at(h)], gm_ref[:, at(h)]
        top, left, right = lower(gm, v)
        s = r_ref[at(h), :]
        gq_ref[:n, at(i)] = (dot(top, k[:n], 1, 0) + dot(gm[:n], s, 1, 1)).astype(BF)
        gq_ref[n:, at(i)] = (
            dot(left, k[:n], 1, 0) + dot(right, k[n:], 1, 0) + dot(gm[n:], s, 1, 1)
        ).astype(BF)
        gk_ref[:n, at(i)] = dot(top, q[:n], 0, 0) + dot(left, q[n:], 0, 0)
        gk_ref[n:, at(i)] = dot(right, q[n:], 0, 0)
        (w_ref, j) = next((r, p.index(h)) for r, p in zip(w_refs, parts) if h in p)
        top, left, right = w_ref[3 * j], w_ref[3 * j + 1], w_ref[3 * j + 2]
        gv_ref[:n, at(i)] = dot(top, gm[:n], 1, 0) + dot(left, gm[n:], 1, 0)
        gv_ref[n:, at(i)] = dot(right, gm[n:], 1, 0)


def flush_kernel(parts, *refs):
    k = len(parts)
    pieces, outs, sems = refs[: 2 * k], refs[2 * k : 2 * k + 2], refs[-1]
    copies = []
    for i, heads in enumerate(parts):
        c = slice(heads[0] * HEAD_DIM, (heads[-1] + 1) * HEAD_DIM)
        for j in range(2):
            copy = pltpu.make_async_copy(pieces[j * k + i], outs[j].at[:, c], sems.at[i, j])
            copy.start()
            copies.append(copy)
    for copy in copies:
        copy.wait()


def last_kernel(parts, *refs):
    k_ref, v_ref, mine_ref, theirs_ref = refs[:4]
    n = len(parts)
    gki, gvi = refs[4 : 4 + n], refs[4 + n : 4 + 2 * n]
    gk_hbm, gv_hbm, gk_ref, gv_ref, r_ref, sems = refs[4 + 2 * n :]
    join(mine_ref, theirs_ref, r_ref)
    copies = []
    for heads, gki_ref, gvi_ref in zip(parts, gki, gvi):
        for j, h in enumerate(heads):
            a = r_ref[at(h), :]
            gk_ref[:, at(h)] = (gki_ref[:, at(j)] + dot(v_ref[:, at(h)], a, 1, 1)).astype(BF)
            gv_ref[:, at(h)] = (gvi_ref[:, at(j)] + dot(k_ref[:, at(h)], a, 1, 0)).astype(BF)
            if h % CHUNK == CHUNK - 1:
                c = slice((h - CHUNK + 1) * HEAD_DIM, (h + 1) * HEAD_DIM)
                for i, (src, dst) in enumerate(((gk_ref, gk_hbm), (gv_ref, gv_hbm))):
                    copy = pltpu.make_async_copy(
                        src.at[:, c], dst.at[:, c], sems.at[h // CHUNK, i]
                    )
                    copy.start()
                    copies.append(copy)
    for copy in copies:
        copy.wait()


def add_kernel(a_ref, b_ref, o_ref):
    o_ref[...] = (a_ref[...] + b_ref[...]).reshape(o_ref.shape)


def finish_kernel(reverse, g_ref, keep_ref, other_ref, mine_ref, give_ref):
    first = g_ref[...].reshape(keep_ref.shape)
    leads = my_core() == (1 if reverse else 0)
    second = first + jnp.where(leads, keep_ref[...], other_ref[...])
    mine_ref[...] = jnp.where(leads, first, second)
    give_ref[...] = jnp.where(leads, second, first)


def running_kernel(reverse, g_ref, o_ref, t_ref):
    total = jnp.zeros(g_ref.shape[1:], F32)
    for i in range(g_ref.shape[0]) if not reverse else reversed(range(g_ref.shape[0])):
        o_ref[i] = total
        total = total + g_ref[i]
    t_ref[...] = total


def outer_kernel(reverse, g_ref, near_ref, far_ref, o_ref):
    z = lax.axis_index("ctx") // (X * CORES)
    bit = 0 if reverse else 1
    near, far = lax.rem(z // 2, 2) == bit, z // 4 == bit
    total = jnp.where(near, near_ref[...], 0.0) + jnp.where(far, far_ref[...], 0.0)
    for i in range(g_ref.shape[0]):
        o_ref[i] = g_ref[i] + total


def carried(keep, send, reverse, windows):
    count = lax.axis_size("ctx")
    plane = X * CORES
    pieces_of = (PAIR, keep.shape[0] // PAIR, HEAD_DIM)
    swap = [(i, i ^ 1) for i in range(count)]
    groups = [
        [pair * PAIR * CORES + i * CORES + c for i in range(PAIR)]
        for pair in range(count // (PAIR * CORES))
        for c in range(CORES)
    ]
    near_z = [(i, (i // plane ^ 2) * plane + i % plane) for i in range(count)]
    across = (6, 7, 4, 5, 2, 3, 0, 1)
    far_z = [(i, across[i // plane] * plane + i % plane) for i in range(count)]
    made = []

    def window(i, operand):
        made.append(windows[i](operand))
        return made[-1][-1:]

    def add(a, b, after, shape):
        return call(add_kernel, [array(shape, F32)], [a, b], a.size, after, vmem=4)[0]

    other = lax.ppermute(send, "ctx", swap)
    after = window(0, send)
    pieces = add(keep, other, after, pieces_of)
    pieces = lax.all_to_all(pieces, "ctx", 0, 0, axis_index_groups=groups)
    inner, total = call(
        functools.partial(running_kernel, reverse),
        [array(pieces.shape, F32), array(pieces.shape[1:], F32)],
        [pieces],
        pieces.size,
        vmem=4,
    )
    near = lax.ppermute(total, "ctx", near_z)
    after = window(1, total)
    total = add(total, near, after, total.shape)
    far = lax.ppermute(total, "ctx", far_z)
    after = window(2, total)
    (pieces,) = call(
        functools.partial(outer_kernel, reverse),
        [array(pieces.shape, F32)],
        [inner, near, far],
        pieces.size,
        after,
        vmem=4,
    )
    pieces = lax.all_to_all(pieces, "ctx", 0, 0, axis_index_groups=groups)
    mine, give = call(
        functools.partial(finish_kernel, reverse),
        [array(keep.shape, F32)] * 2,
        [pieces, keep, other],
        pieces.size,
        vmem=4,
    )
    theirs = lax.ppermute(give, "ctx", swap)
    window(3, give)
    return mine, theirs, made


def body(query, keys, values, gain, cotangent):
    length, width = query.shape
    count = width // HEAD_DIM
    square = 2 * length * length * HEAD_DIM
    small = 2 * length * HEAD_DIM * width
    gain = gain.reshape(1, width)
    whole = lambda dtype: array((length, width), dtype)
    part = lambda heads, dtype: array((length, len(heads) * HEAD_DIM), dtype)
    half = array((width // 2, HEAD_DIM), F32)
    rounded = array((width, HEAD_DIM), BF)
    copied = [pltpu.VMEM((length, width), BF)] * 2
    sems = pltpu.SemaphoreType.DMA((count // CHUNK, 2))
    nothing = lambda ready: [ready]

    keep, send = call(
        state_kernel,
        [half, half],
        [pltpu.with_memory_space_constraint(a, pltpu.HBM) for a in (keys, values)],
        small,
        ins=HBM,
        scratch=copied + [sems],
        vmem=24,
    )

    ahead = [list(range(count // 2)), list(range(count // 2, count))]

    def intra_piece(heads):
        return lambda ready: call(
            functools.partial(intra_kernel, heads),
            [
                array((len(heads) * HEAD_DIM, length), BF),
                array((3 * len(heads), length // 2, length // 2), BF),
                part(heads, F32),
            ],
            [query, keys, values],
            3 * square * len(heads),
            [ready],
        )

    mine, theirs, made = carried(
        keep, send, False, [nothing, intra_piece(ahead[0]), intra_piece(ahead[1]), nothing]
    )
    query_t, weights_t, mixed = zip(*made[1:3])
    mixture, state, sums = call(
        functools.partial(mix_kernel, ahead),
        [whole(F32), rounded, array((8, 128), F32)],
        [query, mine, theirs, cotangent, gain, *mixed],
        small,
    )
    heads = lax.axis_size("head")
    others = [
        lax.ppermute(sums, "head", [(i, i ^ j) for i in range(heads)]) for j in (1, 3, 2)
    ]
    grad_mixture, inverse, keep, send = call(
        functools.partial(grad_kernel, ahead),
        [whole(BF), array((length, 128), F32), half, half],
        [mixture, cotangent, gain, sums, *others, *query_t],
        small,
    )
    behind = [list(range(2)), list(range(2, 5)), list(range(5, count))]

    def back_piece(heads):
        return lambda ready: call(
            functools.partial(back_kernel, heads, ahead),
            [part(heads, BF), part(heads, BF), part(heads, F32), part(heads, F32)],
            [query, keys, values, grad_mixture, state, mixture, inverse, gain, *weights_t],
            4 * square * len(heads),
            [ready],
        )

    flushed = []
    pieces = []

    def kept(heads):
        def one(ready):
            pieces.append(back_piece(heads)(ready))
            return pieces[-1]

        return one

    def flush(ready):
        attended, grad_q = zip(*[p[:2] for p in pieces])
        flushed.extend(
            call(
                functools.partial(flush_kernel, behind),
                [whole(BF), whole(BF)],
                [*attended, *grad_q],
                small,
                [ready],
                out=HBM,
                scratch=[pltpu.SemaphoreType.DMA((len(behind), 2))],
            )
        )
        return flushed

    mine, theirs, _ = carried(keep, send, True, [*map(kept, behind), flush])
    attended, grad_q = flushed
    grad_k, grad_v = call(
        functools.partial(last_kernel, behind),
        [whole(BF), whole(BF)],
        [keys, values, mine, theirs, *[p[2] for p in pieces], *[p[3] for p in pieces]],
        2 * small,
        [attended],
        out=HBM,
        scratch=copied + [pltpu.VMEM((width, HEAD_DIM), BF), sems],
    )
    return attended, grad_q, grad_k, grad_v


def solution(mesh):
    spec = P("ctx", "head")
    return jax.shard_map(
        body,
        mesh=mesh,
        in_specs=(spec, spec, spec, P("head"), spec),
        out_specs=(spec,) * 4,
        check_vma=False,
    )
```

time: 491 us -> 94 us (0.19)
  waiting for transfers between devices: 337 us -> 6.09 us
  other arithmetic: 79.3 us -> 0 us
  starting transfers between devices: 0.08 us -> 30.2 us
  blocking collectives: 8.46 us -> 37.4 us
  matrix products: 27.7 us -> 0 us
  local copies, waits for them, and re-layouts: 20.1 us -> 1.25 us
  Pallas kernels: 0 us -> 17.8 us
  between operations: 14.2 us -> 0.99 us
    all_gather x2 -> x0, waiting for transfers between devices: 337 us -> none  [carried_in(): gathered = lax.all_gather(part, axis)]
    add x63 -> x0, other arithmetic: 73.7 us -> none  [add_pair(): return earlier + later]
    all_to_all x0 -> x4, blocking collectives: none -> 37.4 us  [carried(): pieces = lax.all_to_all(pieces, 'ctx', 0, 0, axis_index_groups=groups)]
    ppermute x0 -> x11, starting transfers between devices: none -> 30.2 us  [the longest x2 9.1 us: carried(): theirs = lax.ppermute(give, 'ctx', swap)]
    dot_general x12 -> x0, matrix products: 27.7 us -> none  [the longest x1 4.28 us: body(): jnp.einsum('hts,the->she', weights, grad_mixture, preferred_element_type=...]
    pallas_call x0 -> x20, Pallas kernels: none -> 17.8 us  [call(): pl.pallas_call(body, out_shape=outs, in_specs=[ins] * len(args) + [ANY] *...]
    unnamed x28 -> x12, local copies, waits for them, and re-layouts: 12.9 us -> 1.25 us
    psum x1 -> x0, blocking collectives: 8.46 us -> none  [body(): squares = lax.psum(jnp.sum(flattened * flattened, axis=1), 'head')]
  transfers between devices with their start and end apart: 2 -> 11, of which waited for: 2 -> 5; matrix products, arithmetic and copies ran while one was open for 4% -> 0% of each run, Pallas kernels for 0% -> 10%
where the time goes in v2:
time: 94 us; the launch traced here: 93.8 us
  blocking collectives  37.4 us (40%)
  starting transfers between devices  30.2 us (32%)
  Pallas kernels  17.8 us (19%)
  waiting for transfers between devices  6.09 us (6%)
  local copies, waits for them, and re-layouts  1.25 us (1%)
  between operations  0.99 us (1%)
    all_to_all x4, blocking collectives, carried(): pieces = lax.all_to_all(pieces, 'ctx', 0, 0, axis_index_groups=groups)  37.4 us
    pallas_call x20, Pallas kernels, call(): pl.pallas_call(body, out_shape=outs, in_specs=[ins] * len(args) + [ANY] *...  17.8 us
    ppermute x2, starting transfers between devices, carried(): theirs = lax.ppermute(give, 'ctx', swap)  9.1 us
    ppermute x2, starting transfers between devices, carried(): far = lax.ppermute(total, 'ctx', far_z)  7.38 us
    ppermute x2, starting transfers between devices, carried(): other = lax.ppermute(send, 'ctx', swap)  5.39 us
    ppermute x2, starting transfers between devices, carried(): near = lax.ppermute(total, 'ctx', near_z)  4.59 us
    ppermute x3, starting transfers between devices, body(): lax.ppermute(sums, 'head', [(i, i ^ j) for i in range(heads)])  3.78 us
    ppermute x3, waiting for transfers between devices, body(): lax.ppermute(sums, 'head', [(i, i ^ j) for i in range(heads)])  2.89 us
  transfers between devices with their start and end apart: 11, of which 5 were waited for; matrix products, arithmetic and copies ran while one was open for 0% of the time, Pallas kernels for 10%

profile of v2, /device:TPU:1, one launch (start us, length us, event | category | flops | bytes accessed | tf_op | source)
XLA Modules:
  0.0 93.8 jit_solution(590879205321933430)
XLA Ops:
  0.7 3.4 %shard_map.84 = (f32[512,128]{1,0:T(8,128)S(1)}, f32[512,128]{1,0:T(8,128)S(1)}) custom-call(bf16[512,1024]{1,0:T(8,128)(2,1)} %refs_0_.15, bf16[512,1024]{1,0:T(8,128)(2,1)} %refs_1_.15), custom_call_target="tpu_custom_call" | custom-call | flops 134217728 | bytes 2621440 | tf_op jit(solution)/shard_map/pallas_call | solution.py:36
  4.1 3.3 %collective-permute-start = (f32[512,128]{1,0:T(8,128)S(1)}, f32[512,128]{1,0:T(8,128)S(1)}, u32[]{:S(2)}, u32[]{:S(2)}) collective-permute-start(f32[512,128]{1,0:T(8,128)S(1)} %get-tuple-element.44.refs_2_), channel_id=1, source_target_pairs={{0,4},{4,0},{8,12},{12,8},{16,20},{20,16},{24,28},{28,24},{32,36},... | collective-permute-start | bytes 786440 | tf_op jit(solution)/shard_map/ppermute | solution.py:291
  7.4 1.2 %collective-permute-done.refs_1_.refs_2_ = f32[512,128]{1,0:T(8,128)S(1)} collective-permute-done((f32[512,128]{1,0:T(8,128)S(1)}, f32[512,128]{1,0:T(8,128)S(1)}, u32[]{:S(2)}, u32[]{:S(2)}) %collective-permute-start) | collective-permute-done | bytes 262176 | tf_op jit(solution)/shard_map/ppermute | solution.py:291
  8.6 9.6 %all_to_all.20.refs_0_ = f32[8,64,128]{2,1,0:T(8,128)S(1)} all-to-all(f32[8,64,128]{2,1,0:T(8,128)S(1)} %shard_map.85), channel_id=1, replica_groups={{0,8,16,24,32,40,48,56},{4,12,20,28,36,44,52,60},{64,72,80,88,96,104,11..., dimensions={0} | all-to-all | bytes 524288 | tf_op jit(solution)/shard_map/all_to_all | solution.py:294
  18.3 3.1 %collective-permute-start.1 = (f32[64,128]{1,0:T(8,128)S(1)}, f32[64,128]{1,0:T(8,128)S(1)}, u32[]{:S(2)}, u32[]{:S(2)}) collective-permute-start(f32[64,128]{1,0:T(8,128)S(1)} %get-tuple-element.46.refs_3_.refs_0_), channel_id=1, source_target_pairs={{0,64},{4,68},{8,72},{12,76},{16,80},{20,84},{24,88},{28,92},{32,9... | collective-permute-start | bytes 98312 | tf_op jit(solution)/shard_map/ppermute | solution.py:302
  21.4 1.6 %shard_map.87 = (bf16[512,512]{1,0:T(8,128)(2,1)S(1)}, bf16[12,256,256]{2,1,0:T(8,128)(2,1)S(1)}, f32[512,512]{1,0:T(8,128)S(1)}) custom-call(bf16[512,1024]{1,0:T(8,128)(2,1)S(1)} %copy-done.2, bf16[512,1024]{1,0:T(8,128)(2,1)S(1)} %copy-done, bf16[512,1024]{1,0:T(8,128)(2,1)S(1)} %copy-done.1, f32[64,128]{1,0:T(8,128)S(1)} %get-tuple-element.46.refs_3_.refs_0_), custom_call_target="tpu_custom_call" | custom-call | flops 805306368 | bytes 6291456 | tf_op jit(solution)/shard_map/pallas_call | solution.py:36
  23.0 4.2 %collective-permute-start.2 = (f32[64,128]{1,0:T(8,128)S(1)}, f32[64,128]{1,0:T(8,128)S(1)}, u32[]{:S(2)}, u32[]{:S(2)}) collective-permute-start(f32[64,128]{1,0:T(8,128)S(1)} %shard_map.88.refs_3_), channel_id=1, source_target_pairs={{0,192},{4,196},{8,200},{12,204},{16,208},{20,212},{24,216},{28,22... | collective-permute-start | bytes 98312 | tf_op jit(solution)/shard_map/ppermute | solution.py:305
  27.1 1.6 %shard_map.89 = (bf16[512,512]{1,0:T(8,128)(2,1)S(1)}, bf16[12,256,256]{2,1,0:T(8,128)(2,1)S(1)}, f32[512,512]{1,0:T(8,128)S(1)}) custom-call(bf16[512,1024]{1,0:T(8,128)(2,1)S(1)} %copy-done.2, bf16[512,1024]{1,0:T(8,128)(2,1)S(1)} %copy-done, bf16[512,1024]{1,0:T(8,128)(2,1)S(1)} %copy-done.1, f32[64,128]{1,0:T(8,128)S(1)} %shard_map.88.refs_3_), custom_call_target="tpu_custom_call" | custom-call | flops 805306368 | bytes 6291456 | tf_op jit(solution)/shard_map/pallas_call | solution.py:36
  28.8 9.4 %all_to_all.21.refs_0_ = f32[8,64,128]{2,1,0:T(8,128)S(1)} all-to-all(f32[8,64,128]{2,1,0:T(8,128)S(1)} %shard_map.90), channel_id=1, replica_groups={{0,8,16,24,32,40,48,56},{4,12,20,28,36,44,52,60},{64,72,80,88,96,104,11..., dimensions={0} | all-to-all | bytes 524288 | tf_op jit(solution)/shard_map/all_to_all | solution.py:315
  38.2 0.1 shard_map.91
  38.3 4.8 %collective-permute-start.3 = (f32[512,128]{1,0:T(8,128)S(1)}, f32[512,128]{1,0:T(8,128)S(1)}, u32[]{:S(2)}, u32[]{:S(2)}) collective-permute-start(f32[512,128]{1,0:T(8,128)S(1)} %get-tuple-element.50), channel_id=1, source_target_pairs={{0,4},{4,0},{8,12},{12,8},{16,20},{20,16},{24,28},{28,24},{32,36},... | collective-permute-start | bytes 786440 | tf_op jit(solution)/shard_map/ppermute | solution.py:323
  43.1 1.2 %collective-permute-done.3.refs_2_ = f32[512,128]{1,0:T(8,128)S(1)} collective-permute-done((f32[512,128]{1,0:T(8,128)S(1)}, f32[512,128]{1,0:T(8,128)S(1)}, u32[]{:S(2)}, u32[]{:S(2)}) %collective-permute-start.3) | collective-permute-done | bytes 262176 | tf_op jit(solution)/shard_map/ppermute | solution.py:323
  44.3 0.9 shard_map.92
  45.2 3.0 %collective-permute-start.6 = (f32[8,128]{1,0:T(8,128)S(1)}, f32[8,128]{1,0:T(8,128)S(1)}, u32[]{:S(2)}, u32[]{:S(2)}) collective-permute-start(f32[8,128]{1,0:T(8,128)S(1)} %get-tuple-element.52.refs_3_), channel_id=1, source_target_pairs={{0,2},{1,3},{2,0},{3,1},{4,6},{5,7},{6,4},{7,5},{8,10},{9,11},{10,... | collective-permute-start | bytes 12296 | tf_op jit(solution)/shard_map/ppermute | solution.py:379
  48.2 0.8 collective-permute-start.5
  48.9 0.3 collective-permute-done.6.refs_6_
  49.2 2.6 %collective-permute-done.5.refs_5_ = f32[8,128]{1,0:T(8,128)S(1)} collective-permute-done((f32[8,128]{1,0:T(8,128)S(1)}, f32[8,128]{1,0:T(8,128)S(1)}, u32[]{:S(2)}, u32[]{:S(2)}) %collective-permute-start.5) | collective-permute-done | bytes 4128 | tf_op jit(solution)/shard_map/ppermute | solution.py:379
  51.8 2.1 %shard_map.93 = (bf16[512,1024]{1,0:T(8,128)(2,1)S(1)}, f32[512,128]{1,0:T(8,128)S(1)}, f32[512,128]{1,0:T(8,128)S(1)}, f32[512,128]{1,0:T(8,128)S(1)}) custom-call(f32[512,1024]{1,0:T(8,128)S(1)} %get-tuple-element.51.refs_0_.refs_5_, bf16[512,1024]{1,0:T(8,128)(2,1)S(1)} %copy-done.3, f32[1,1024]{1,0:T(1,128)S(1)} %bitcast.2, ...), custom_call_target="tpu_custom_call" | custom-call | flops 134217728 | bytes 6049792 | tf_op jit(solution)/shard_map/pallas_call | solution.py:36
  53.9 2.1 %collective-permute-start.7 = (f32[512,128]{1,0:T(8,128)S(1)}, f32[512,128]{1,0:T(8,128)S(1)}, u32[]{:S(2)}, u32[]{:S(2)}) collective-permute-start(f32[512,128]{1,0:T(8,128)S(1)} %get-tuple-element.60.refs_10_), channel_id=1, source_target_pairs={{0,4},{4,0},{8,12},{12,8},{16,20},{20,16},{24,28},{28,24},{32,36},... | collective-permute-start | bytes 786440 | tf_op jit(solution)/shard_map/ppermute | solution.py:291
  56.0 1.3 %shard_map.94 = (bf16[512,256]{1,0:T(8,128)(2,1)S(1)}, bf16[512,256]{1,0:T(8,128)(2,1)S(1)}, f32[512,256]{1,0:T(8,128)S(1)}, f32[512,256]{1,0:T(8,128)S(1)}) custom-call(bf16[512,1024]{1,0:T(8,128)(2,1)S(1)} %copy-done.2, bf16[512,1024]{1,0:T(8,128)(2,1)S(1)} %copy-done, bf16[512,1024]{1,0:T(8,128)(2,1)S(1)} %copy-done.1, ...), custom_call_target="tpu_custom_call" | custom-call | flops 536870912 | bytes 11538432 | tf_op jit(solution)/shard_map/pallas_call | solution.py:36
  57.3 8.5 %all_to_all.22.refs_0_ = f32[8,64,128]{2,1,0:T(8,128)S(1)} all-to-all(f32[8,64,128]{2,1,0:T(8,128)S(1)} %shard_map.95), channel_id=1, replica_groups={{0,8,16,24,32,40,48,56},{4,12,20,28,36,44,52,60},{64,72,80,88,96,104,11..., dimensions={0} | all-to-all | bytes 524288 | tf_op jit(solution)/shard_map/all_to_all | solution.py:294
  65.8 1.5 %collective-permute-start.8 = (f32[64,128]{1,0:T(8,128)S(1)}, f32[64,128]{1,0:T(8,128)S(1)}, u32[]{:S(2)}, u32[]{:S(2)}) collective-permute-start(f32[64,128]{1,0:T(8,128)S(1)} %get-tuple-element.64.refs_10_.refs_0_), channel_id=1, source_target_pairs={{0,64},{4,68},{8,72},{12,76},{16,80},{20,84},{24,88},{28,92},{32,9... | collective-permute-start | bytes 98312 | tf_op jit(solution)/shard_map/ppermute | solution.py:302
  67.4 1.8 %shard_map.97 = (bf16[512,384]{1,0:T(8,128)(2,1)S(1)}, bf16[512,384]{1,0:T(8,128)(2,1)S(1)}, f32[512,384]{1,0:T(8,128)S(1)}, f32[512,384]{1,0:T(8,128)S(1)}) custom-call(bf16[512,1024]{1,0:T(8,128)(2,1)S(1)} %copy-done.2, bf16[512,1024]{1,0:T(8,128)(2,1)S(1)} %copy-done, bf16[512,1024]{1,0:T(8,128)(2,1)S(1)} %copy-done.1, ...), custom_call_target="tpu_custom_call" | custom-call | flops 805306368 | bytes 12324864 | tf_op jit(solution)/shard_map/pallas_call | solution.py:36
  69.2 0.8 collective-permute-done.8.refs_1_
  70.0 3.2 %collective-permute-start.9 = (f32[64,128]{1,0:T(8,128)S(1)}, f32[64,128]{1,0:T(8,128)S(1)}, u32[]{:S(2)}, u32[]{:S(2)}) collective-permute-start(f32[64,128]{1,0:T(8,128)S(1)} %shard_map.98.refs_10_), channel_id=1, source_target_pairs={{0,192},{4,196},{8,200},{12,204},{16,208},{20,212},{24,216},{28,22... | collective-permute-start | bytes 98312 | tf_op jit(solution)/shard_map/ppermute | solution.py:305
  73.2 1.8 %shard_map.99 = (bf16[512,384]{1,0:T(8,128)(2,1)S(1)}, bf16[512,384]{1,0:T(8,128)(2,1)S(1)}, f32[512,384]{1,0:T(8,128)S(1)}, f32[512,384]{1,0:T(8,128)S(1)}) custom-call(bf16[512,1024]{1,0:T(8,128)(2,1)S(1)} %copy-done.2, bf16[512,1024]{1,0:T(8,128)(2,1)S(1)} %copy-done, bf16[512,1024]{1,0:T(8,128)(2,1)S(1)} %copy-done.1, ...), custom_call_target="tpu_custom_call" | custom-call | flops 805306368 | bytes 12324864 | tf_op jit(solution)/shard_map/pallas_call | solution.py:36
  75.0 9.8 %all_to_all.23.refs_0_ = f32[8,64,128]{2,1,0:T(8,128)S(1)} all-to-all(f32[8,64,128]{2,1,0:T(8,128)S(1)} %shard_map.100), channel_id=1, replica_groups={{0,8,16,24,32,40,48,56},{4,12,20,28,36,44,52,60},{64,72,80,88,96,104,11..., dimensions={0} | all-to-all | bytes 524288 | tf_op jit(solution)/shard_map/all_to_all | solution.py:315
  84.9 0.1 shard_map.101
  84.9 4.3 %collective-permute-start.10 = (f32[512,128]{1,0:T(8,128)S(1)}, f32[512,128]{1,0:T(8,128)S(1)}, u32[]{:S(2)}, u32[]{:S(2)}) collective-permute-start(f32[512,128]{1,0:T(8,128)S(1)} %get-tuple-element.73.refs_6_), channel_id=1, source_target_pairs={{0,4},{4,0},{8,12},{12,8},{16,20},{20,16},{24,28},{28,24},{32,36},... | collective-permute-start | bytes 786440 | tf_op jit(solution)/shard_map/ppermute | solution.py:323
  89.2 1.4 %shard_map.102 = (bf16[512,1024]{1,0:T(8,128)(2,1)}, bf16[512,1024]{1,0:T(8,128)(2,1)}) custom-call(bf16[512,256]{1,0:T(8,128)(2,1)S(1)} %get-tuple-element.61.refs_0_, bf16[512,384]{1,0:T(8,128)(2,1)S(1)} %get-tuple-element.65.refs_1_, bf16[512,384]{1,0:T(8,128)(2,1)S(1)} %get-tuple-element.67.refs_2_, bf16[512,256]{1,0:T(8,128)(2,1)S(1)} %get-tuple-element.68.refs_3_, ...), custom_call_target="tpu_custom_call" | custom-call | flops 134217728 | bytes 4194304 | tf_op jit(solution)/shard_map/pallas_call | solution.py:36
  90.6 1.2 %copy-done.4 = bf16[512,1024]{1,0:T(8,128)(2,1)S(1)} copy-done((bf16[512,1024]{1,0:T(8,128)(2,1)S(1)}, bf16[512,1024]{1,0:T(8,128)(2,1)}, u32[]{:S(2)}) %copy-start.4) | copy-done | bytes 1048600
  91.8 1.8 %shard_map.103 = (bf16[512,1024]{1,0:T(8,128)(2,1)}, bf16[512,1024]{1,0:T(8,128)(2,1)}) custom-call(bf16[512,1024]{1,0:T(8,128)(2,1)S(1)} %copy-done, bf16[512,1024]{1,0:T(8,128)(2,1)S(1)} %copy-done.1, f32[512,128]{1,0:T(8,128)S(1)} %get-tuple-element.76.refs_2_, f32[512,128]{1,0:T(8,128)S(1)} %collective-permute-done.10.refs_3_, ...), custom_call_target="tpu_custom_call" | custom-call | flops 268435456 | bytes 8912896 | tf_op jit(solution)/shard_map/pallas_call | solution.py:36
  (26 shorter events, 0.3 us)
Async XLA Ops:
  0.6 20.7 %copy-start.1 = (bf16[512,1024]{1,0:T(8,128)(2,1)S(1)}, bf16[512,1024]{1,0:T(8,128)(2,1)}, u32[]{:S(2)}) copy-start(bf16[512,1024]{1,0:T(8,128)(2,1)} %refs_1_.15) | copy-start | bytes 3145732
  0.6 20.7 %copy-start = (bf16[512,1024]{1,0:T(8,128)(2,1)S(1)}, bf16[512,1024]{1,0:T(8,128)(2,1)}, u32[]{:S(2)}) copy-start(bf16[512,1024]{1,0:T(8,128)(2,1)} %refs_0_.15) | copy-start | bytes 3145732
  0.7 20.7 %copy-start.2 = (bf16[512,1024]{1,0:T(8,128)(2,1)S(1)}, bf16[512,1024]{1,0:T(8,128)(2,1)}, u32[]{:S(2)}) copy-start(bf16[512,1024]{1,0:T(8,128)(2,1)} %refs_0_.14) | copy-start | bytes 3145732
  4.1 4.5 %collective-permute-start = (f32[512,128]{1,0:T(8,128)S(1)}, f32[512,128]{1,0:T(8,128)S(1)}, u32[]{:S(2)}, u32[]{:S(2)}) collective-permute-start(f32[512,128]{1,0:T(8,128)S(1)} %get-tuple-element.44.refs_2_), channel_id=1, source_target_pairs={{0,4},{4,0},{8,12},{12,8},{16,20},{20,16},{24,28},{28,24},{32,36},... | collective-permute-start | bytes 786440 | tf_op jit(solution)/shard_map/ppermute | solution.py:291
  18.3 4.7 %collective-permute-start.1 = (f32[64,128]{1,0:T(8,128)S(1)}, f32[64,128]{1,0:T(8,128)S(1)}, u32[]{:S(2)}, u32[]{:S(2)}) collective-permute-start(f32[64,128]{1,0:T(8,128)S(1)} %get-tuple-element.46.refs_3_.refs_0_), channel_id=1, source_target_pairs={{0,64},{4,68},{8,72},{12,76},{16,80},{20,84},{24,88},{28,92},{32,9... | collective-permute-start | bytes 98312 | tf_op jit(solution)/shard_map/ppermute | solution.py:302
  23.0 5.8 %collective-permute-start.2 = (f32[64,128]{1,0:T(8,128)S(1)}, f32[64,128]{1,0:T(8,128)S(1)}, u32[]{:S(2)}, u32[]{:S(2)}) collective-permute-start(f32[64,128]{1,0:T(8,128)S(1)} %shard_map.88.refs_3_), channel_id=1, source_target_pairs={{0,192},{4,196},{8,200},{12,204},{16,208},{20,212},{24,216},{28,22... | collective-permute-start | bytes 98312 | tf_op jit(solution)/shard_map/ppermute | solution.py:305
  28.7 15.5 %copy-start.3 = (bf16[512,1024]{1,0:T(8,128)(2,1)S(1)}, bf16[512,1024]{1,0:T(8,128)(2,1)}, u32[]{:S(2)}) copy-start(bf16[512,1024]{1,0:T(8,128)(2,1)} %refs_1_.11) | copy-start | bytes 3145732
  28.7 15.5 %copy-start.5 = (f32[1024]{0:T(1024)S(1)}, f32[1024]{0:T(1024)}, u32[]{:S(2)}) copy-start(f32[1024]{0:T(1024)} %param.8) | copy-start | bytes 12292
  38.3 6.0 %collective-permute-start.3 = (f32[512,128]{1,0:T(8,128)S(1)}, f32[512,128]{1,0:T(8,128)S(1)}, u32[]{:S(2)}, u32[]{:S(2)}) collective-permute-start(f32[512,128]{1,0:T(8,128)S(1)} %get-tuple-element.50), channel_id=1, source_target_pairs={{0,4},{4,0},{8,12},{12,8},{16,20},{20,16},{24,28},{28,24},{32,36},... | collective-permute-start | bytes 786440 | tf_op jit(solution)/shard_map/ppermute | solution.py:323
  45.2 4.0 %collective-permute-start.6 = (f32[8,128]{1,0:T(8,128)S(1)}, f32[8,128]{1,0:T(8,128)S(1)}, u32[]{:S(2)}, u32[]{:S(2)}) collective-permute-start(f32[8,128]{1,0:T(8,128)S(1)} %get-tuple-element.52.refs_3_), channel_id=1, source_target_pairs={{0,2},{1,3},{2,0},{3,1},{4,6},{5,7},{6,4},{7,5},{8,10},{9,11},{10,... | collective-permute-start | bytes 12296 | tf_op jit(solution)/shard_map/ppermute | solution.py:379
  48.2 3.7 %collective-permute-start.5 = (f32[8,128]{1,0:T(8,128)S(1)}, f32[8,128]{1,0:T(8,128)S(1)}, u32[]{:S(2)}, u32[]{:S(2)}) collective-permute-start(f32[8,128]{1,0:T(8,128)S(1)} %get-tuple-element.52.refs_3_), channel_id=1, source_target_pairs={{0,3},{1,2},{2,1},{3,0},{4,7},{5,6},{6,5},{7,4},{8,11},{9,10},{10,... | collective-permute-start | bytes 12296 | tf_op jit(solution)/shard_map/ppermute | solution.py:379
  48.9 2.9 %collective-permute-start.4 = (f32[8,128]{1,0:T(8,128)S(1)}, f32[8,128]{1,0:T(8,128)S(1)}, u32[]{:S(2)}, u32[]{:S(2)}) collective-permute-start(f32[8,128]{1,0:T(8,128)S(1)} %get-tuple-element.52.refs_3_), channel_id=1, source_target_pairs={{0,1},{1,0},{2,3},{3,2},{4,5},{5,4},{6,7},{7,6},{8,9},{9,8},{10,11... | collective-permute-start | bytes 12296 | tf_op jit(solution)/shard_map/ppermute | solution.py:379
  53.9 3.3 %collective-permute-start.7 = (f32[512,128]{1,0:T(8,128)S(1)}, f32[512,128]{1,0:T(8,128)S(1)}, u32[]{:S(2)}, u32[]{:S(2)}) collective-permute-start(f32[512,128]{1,0:T(8,128)S(1)} %get-tuple-element.60.refs_10_), channel_id=1, source_target_pairs={{0,4},{4,0},{8,12},{12,8},{16,20},{20,16},{24,28},{28,24},{32,36},... | collective-permute-start | bytes 786440 | tf_op jit(solution)/shard_map/ppermute | solution.py:291
  65.8 4.1 %collective-permute-start.8 = (f32[64,128]{1,0:T(8,128)S(1)}, f32[64,128]{1,0:T(8,128)S(1)}, u32[]{:S(2)}, u32[]{:S(2)}) collective-permute-start(f32[64,128]{1,0:T(8,128)S(1)} %get-tuple-element.64.refs_10_.refs_0_), channel_id=1, source_target_pairs={{0,64},{4,68},{8,72},{12,76},{16,80},{20,84},{24,88},{28,92},{32,9... | collective-permute-start | bytes 98312 | tf_op jit(solution)/shard_map/ppermute | solution.py:302
  70.0 5.0 %collective-permute-start.9 = (f32[64,128]{1,0:T(8,128)S(1)}, f32[64,128]{1,0:T(8,128)S(1)}, u32[]{:S(2)}, u32[]{:S(2)}) collective-permute-start(f32[64,128]{1,0:T(8,128)S(1)} %shard_map.98.refs_10_), channel_id=1, source_target_pairs={{0,192},{4,196},{8,200},{12,204},{16,208},{20,212},{24,216},{28,22... | collective-permute-start | bytes 98312 | tf_op jit(solution)/shard_map/ppermute | solution.py:305
  84.9 5.6 %collective-permute-start.10 = (f32[512,128]{1,0:T(8,128)S(1)}, f32[512,128]{1,0:T(8,128)S(1)}, u32[]{:S(2)}, u32[]{:S(2)}) collective-permute-start(f32[512,128]{1,0:T(8,128)S(1)} %get-tuple-element.73.refs_6_), channel_id=1, source_target_pairs={{0,4},{4,0},{8,12},{12,8},{16,20},{20,16},{24,28},{28,24},{32,36},... | collective-permute-start | bytes 786440 | tf_op jit(solution)/shard_map/ppermute | solution.py:323
  90.6 1.2 %copy-start.4 = (bf16[512,1024]{1,0:T(8,128)(2,1)S(1)}, bf16[512,1024]{1,0:T(8,128)(2,1)}, u32[]{:S(2)}) copy-start(bf16[512,1024]{1,0:T(8,128)(2,1)} %get-tuple-element.39.refs_10_) | copy-start | bytes 3145732

commit v3 on v2

v3 whole, which is shorter than its diff:
```python
import functools

import jax
import jax.numpy as jnp
from jax import lax
from jax.experimental import pallas as pl
from jax.experimental.pallas import tpu as pltpu
from jax.sharding import PartitionSpec as P

HEADS = 32
HEAD_DIM = 128
EPSILON = 1e-05
BF = jnp.bfloat16
F32 = jnp.float32

X = 4
CORES = 2
PAIR = 2 * X

VMEM = pl.BlockSpec(memory_space=pltpu.VMEM)
HBM = pl.BlockSpec(memory_space=pltpu.HBM)
ANY = pl.BlockSpec(memory_space=pl.ANY)


def dot(a, b, ca, cb):
    return lax.dot_general(a, b, (((ca,), (cb,)), ((), ())), preferred_element_type=F32)


def call(kernel, outs, args, flops, after=(), ins=VMEM, out=VMEM, scratch=(), vmem=16):
    nbytes = sum(a.size * a.dtype.itemsize for a in args)
    nbytes += sum(o.size * o.dtype.itemsize for o in outs)

    def body(*refs):
        kernel(*refs[: len(args)], *refs[len(args) + len(after) :])

    return pl.pallas_call(
        body,
        out_shape=outs,
        in_specs=[ins] * len(args) + [ANY] * len(after),
        out_specs=[out] * len(outs),
        scratch_shapes=list(scratch),
        compiler_params=pltpu.CompilerParams(vmem_limit_bytes=vmem << 20),
        cost_estimate=pl.CostEstimate(flops=flops, bytes_accessed=nbytes, transcendentals=0),
    )(*args, *after)


def array(shape, dtype):
    return jax.ShapeDtypeStruct(shape, dtype)


def at(h):
    return slice(h * HEAD_DIM, (h + 1) * HEAD_DIM)


def my_core():
    return lax.rem(lax.axis_index("ctx"), CORES)


def shift(i):
    return i // (2 * X * CORES)


def my_half():
    i = lax.axis_index("ctx")
    return lax.rem(i % CORES + shift(i), 2)


OWN, OTHER = 0, 1


def cols(side, j, half):
    mine = my_half()
    base = (mine if side == OWN else 1 - mine) * (half * HEAD_DIM)
    return pl.ds(pl.multiple_of(base + j * HEAD_DIM, HEAD_DIM), HEAD_DIM)


def state_own_kernel(side, a_ref, b_ref, s_ref):
    half = s_ref.shape[0] // HEAD_DIM
    for j in range(half):
        c = cols(side, j, half)
        s_ref[at(j), :] = dot(a_ref[:, c], b_ref[:, c], 0, 0)


def state_kernel(side, a_hbm, b_hbm, s_ref, a_ref, b_ref, sems):
    half = a_ref.shape[1] // HEAD_DIM
    copies = []
    for j in range(half):
        for i, (src, dst) in enumerate(((a_hbm, a_ref), (b_hbm, b_ref))):
            copy = pltpu.make_async_copy(
                src.at[:, cols(side, j, half)], dst.at[:, at(j)], sems.at[i, j]
            )
            copy.start()
            copies.append(copy)
    for j in range(half):
        copies[2 * j].wait()
        copies[2 * j + 1].wait()
        s_ref[at(j), :] = dot(a_ref[:, at(j)], b_ref[:, at(j)], 0, 0)


def triangle(n, flip=False):
    rows = lax.broadcasted_iota(jnp.int32, (n, n), 0)
    cols = lax.broadcasted_iota(jnp.int32, (n, n), 1)
    return rows <= cols if flip else cols <= rows


def lower(a, b):
    n = a.shape[0] // 2
    keep = triangle(n)
    top = jnp.where(keep, dot(a[:n], b[:n], 1, 1), 0.0).astype(BF)
    left = dot(a[n:], b[:n], 1, 1).astype(BF)
    right = jnp.where(keep, dot(a[n:], b[n:], 1, 1), 0.0).astype(BF)
    return top, left, right


def lower_t(a, b):
    n = a.shape[0] // 2
    keep = triangle(n, True)
    top = jnp.where(keep, dot(b[:n], a[:n], 1, 1), 0.0).astype(BF)
    left = dot(b[:n], a[n:], 1, 1).astype(BF)
    right = jnp.where(keep, dot(b[n:], a[n:], 1, 1), 0.0).astype(BF)
    return top, left, right


def intra_kernel(side, q_ref, k_ref, v_ref, qt_ref, wt_ref, o_ref):
    n = q_ref.shape[0] // 2
    half = o_ref.shape[1] // HEAD_DIM
    for j in range(half):
        c = cols(side, j, half)
        q, k, v = q_ref[:, c], k_ref[:, c], v_ref[:, c]
        qt_ref[at(j), :] = q.T
        top, left, right = lower(q, k)
        o_ref[:n, at(j)] = dot(top, v[:n], 1, 0)
        o_ref[n:, at(j)] = dot(left, v[:n], 1, 0) + dot(right, v[n:], 1, 0)
        for i, block in enumerate(lower_t(q, k)):
            wt_ref[3 * j + i] = block


def mix_kernel(side, q_ref, s_ref, i_ref, c_ref, g_ref, *refs):
    before_ref = refs[0] if side == OTHER else None
    m_ref, p_ref = refs[-2:]
    half = m_ref.shape[1] // HEAD_DIM
    state = [s_ref[at(j), :].astype(BF) for j in range(half)]
    for i in range(q_ref.shape[0] // 128):
        rows = slice(i * 128, (i + 1) * 128)
        squares = jnp.zeros((128, HEAD_DIM), F32)
        products = jnp.zeros((128, HEAD_DIM), F32)
        for j in range(half):
            c = cols(side, j, half)
            m = i_ref[rows, at(j)] + dot(q_ref[rows, c], state[j], 1, 0)
            m_ref[rows, at(j)] = m
            squares = squares + m * m
            products = products + (c_ref[rows, c].astype(F32) * g_ref[:, c]) * m
        for row, value in ((i, squares), (4 + i, products)):
            value = jnp.sum(value.T, axis=0, keepdims=True)
            if side == OTHER:
                value = value + before_ref[row : row + 1, :]
            p_ref[row : row + 1, :] = value


def spread(row):
    return jnp.broadcast_to(row, (128, 128)).T


def grad(side, qt_ref, m_ref, c_ref, g_ref, inv_ref, cf_ref, gm_ref, s_ref):
    half = m_ref.shape[1] // HEAD_DIM
    for j in range(half):
        c = cols(side, j, half)
        scaled = c_ref[:, c].astype(F32) * g_ref[:, c]
        gm = (inv_ref[...] * scaled - m_ref[:, at(j)] * cf_ref[...]).astype(BF)
        gm_ref[:, at(j)] = gm
        s_ref[at(j), :] = dot(qt_ref[at(j), :], gm, 1, 0)


def grad_other_kernel(qt_ref, m_ref, c_ref, g_ref, p0, p1, p2, p3, gm_ref, s_ref, inv_ref, cf_ref):
    width = HEADS * HEAD_DIM
    sums = p0[...] + p1[...] + p2[...] + p3[...]
    inverse = lax.rsqrt(sums[:4] / width + EPSILON)
    coef = inverse * inverse * inverse * sums[4:] / width
    for i in range(4):
        rows = slice(i * 128, (i + 1) * 128)
        inv_ref[rows, :] = spread(inverse[i : i + 1])
        cf_ref[rows, :] = spread(coef[i : i + 1])
    grad(OTHER, qt_ref, m_ref, c_ref, g_ref, inv_ref, cf_ref, gm_ref, s_ref)


def grad_own_kernel(qt_ref, m_ref, c_ref, g_ref, inv_ref, cf_ref, gm_ref, s_ref):
    grad(OWN, qt_ref, m_ref, c_ref, g_ref, inv_ref, cf_ref, gm_ref, s_ref)


def back_kernel(
    side, q_ref, k_ref, v_ref, gm_ref, s_ref, m_ref, inv_ref, g_ref, wt_ref,
    at_ref, gq_ref, gk_ref, gv_ref,
):
    n = q_ref.shape[0] // 2
    half = gm_ref.shape[1] // HEAD_DIM
    for j in range(half):
        c = cols(side, j, half)
        at_ref[:, at(j)] = (m_ref[:, at(j)] * inv_ref[...] * g_ref[:, c]).astype(BF)
        q, k, v, gm = q_ref[:, c], k_ref[:, c], v_ref[:, c], gm_ref[:, at(j)]
        top, left, right = lower(gm, v)
        s = s_ref[at(j), :].astype(BF)
        gq_ref[:n, at(j)] = (dot(top, k[:n], 1, 0) + dot(gm[:n], s, 1, 1)).astype(BF)
        gq_ref[n:, at(j)] = (
            dot(left, k[:n], 1, 0) + dot(right, k[n:], 1, 0) + dot(gm[n:], s, 1, 1)
        ).astype(BF)
        gk_ref[:n, at(j)] = dot(top, q[:n], 0, 0) + dot(left, q[n:], 0, 0)
        gk_ref[n:, at(j)] = dot(right, q[n:], 0, 0)
        top, left, right = wt_ref[3 * j], wt_ref[3 * j + 1], wt_ref[3 * j + 2]
        gv_ref[:n, at(j)] = dot(top, gm[:n], 1, 0) + dot(left, gm[n:], 1, 0)
        gv_ref[n:, at(j)] = dot(right, gm[n:], 1, 0)


def send_out(pairs, half, sems):
    mine = my_half()
    copies = []
    for i, (side, src, dst) in enumerate(pairs):
        base = (mine if side == OWN else 1 - mine) * (half * HEAD_DIM)
        c = pl.ds(pl.multiple_of(base, half * HEAD_DIM), half * HEAD_DIM)
        copies.append(pltpu.make_async_copy(src, dst.at[:, c], sems.at[i]))
        copies[-1].start()
    return copies


def last(side, k_ref, v_ref, s_ref, gki_ref, gvi_ref, gk_ref, gv_ref, then=lambda j: None):
    half = gki_ref.shape[1] // HEAD_DIM
    for j in range(half):
        c = cols(side, j, half)
        s = s_ref[at(j), :].astype(BF)
        gk_ref[:, at(j)] = (gki_ref[:, at(j)] + dot(v_ref[:, c], s, 1, 1)).astype(BF)
        gv_ref[:, at(j)] = (gvi_ref[:, at(j)] + dot(k_ref[:, c], s, 1, 0)).astype(BF)
        then(j)


def last_own_kernel(
    k_ref, v_ref, s_ref, gki_ref, gvi_ref, ato_ref, ats_ref, gqo_ref, gqs_ref,
    gk_ref, gv_ref, at_hbm, gq_hbm, sems,
):
    half = gki_ref.shape[1] // HEAD_DIM
    pairs = [
        (OWN, ato_ref, at_hbm), (OTHER, ats_ref, at_hbm),
        (OWN, gqo_ref, gq_hbm), (OTHER, gqs_ref, gq_hbm),
    ]
    copies = send_out(pairs, half, sems)
    last(OWN, k_ref, v_ref, s_ref, gki_ref, gvi_ref, gk_ref, gv_ref)
    for copy in copies:
        copy.wait()


def last_other_kernel(
    k_ref, v_ref, s_ref, gki_ref, gvi_ref, gko_ref, gvo_ref,
    gk_hbm, gv_hbm, gk_ref, gv_ref, sems, head_sems,
):
    half = gki_ref.shape[1] // HEAD_DIM
    copies = send_out([(OWN, gko_ref, gk_hbm), (OWN, gvo_ref, gv_hbm)], half, sems)

    def then(j):
        for i, (src, dst) in enumerate(((gk_ref, gk_hbm), (gv_ref, gv_hbm))):
            copy = pltpu.make_async_copy(
                src.at[:, at(j)], dst.at[:, cols(OTHER, j, half)], head_sems.at[i, j]
            )
            copy.start()
            copies.append(copy)

    last(OTHER, k_ref, v_ref, s_ref, gki_ref, gvi_ref, gk_ref, gv_ref, then)
    for copy in copies:
        copy.wait()


def add_kernel(a_ref, b_ref, o_ref):
    o_ref[...] = (a_ref[...] + b_ref[...]).reshape(o_ref.shape)


def finish_kernel(reverse, g_ref, keep_ref, other_ref, mine_ref, give_ref):
    first = g_ref[...].reshape(keep_ref.shape)
    leads = my_core() == (1 if reverse else 0)
    second = first + jnp.where(leads, keep_ref[...], other_ref[...])
    mine_ref[...] = jnp.where(leads, first, second)
    give_ref[...] = jnp.where(leads, second, first)


def running_kernel(reverse, g_ref, o_ref, t_ref):
    total = jnp.zeros(g_ref.shape[1:], F32)
    for i in range(g_ref.shape[0]) if not reverse else reversed(range(g_ref.shape[0])):
        o_ref[i] = total
        total = total + g_ref[i]
    t_ref[...] = total


def outer_kernel(reverse, g_ref, near_ref, far_ref, o_ref):
    z = lax.axis_index("ctx") // (X * CORES)
    bit = 0 if reverse else 1
    near, far = lax.rem(z // 2, 2) == bit, z // 4 == bit
    total = jnp.where(near, near_ref[...], 0.0) + jnp.where(far, far_ref[...], 0.0)
    for i in range(g_ref.shape[0]):
        o_ref[i] = g_ref[i] + total


def carried(send, reverse, windows):
    count = lax.axis_size("ctx")
    pieces_of = (PAIR, send.shape[0] // PAIR, HEAD_DIM)
    swap = [(i, i ^ 1) for i in range(count)]
    def on(chip, half):
        return chip * CORES + (half + shift(chip * CORES)) % CORES

    groups = [
        [on(pair * PAIR + i, half) for i in range(PAIR)]
        for pair in range(count // (PAIR * CORES))
        for half in range(2)
    ]
    across = (6, 7, 4, 5, 2, 3, 0, 1)

    def partners(of):
        chips = [(z * X + x, of(z) * X + x) for z in range(len(across)) for x in range(X)]
        return [(on(a, half), on(b, half)) for a, b in chips for half in range(2)]

    near_z = partners(lambda z: z ^ 2)
    far_z = partners(lambda z: across[z])

    def add(a, b, after, shape):
        return call(add_kernel, [array(shape, F32)], [a, b], a.size, after, vmem=4)[0]

    other = lax.ppermute(send, "ctx", swap)
    keep = windows[0](send)[-1]
    pieces = add(keep, other, (), pieces_of)
    pieces = lax.all_to_all(pieces, "ctx", 0, 0, axis_index_groups=groups)
    inner, total = call(
        functools.partial(running_kernel, reverse),
        [array(pieces.shape, F32), array(pieces.shape[1:], F32)],
        [pieces],
        pieces.size,
        vmem=4,
    )
    near = lax.ppermute(total, "ctx", near_z)
    after = windows[1](total)[-1:]
    total = add(total, near, after, total.shape)
    far = lax.ppermute(total, "ctx", far_z)
    after = windows[2](total)[-1:]
    (pieces,) = call(
        functools.partial(outer_kernel, reverse),
        [array(pieces.shape, F32)],
        [inner, near, far],
        pieces.size,
        after,
        vmem=4,
    )
    pieces = lax.all_to_all(pieces, "ctx", 0, 0, axis_index_groups=groups)
    mine, give = call(
        functools.partial(finish_kernel, reverse),
        [array(send.shape, F32)] * 2,
        [pieces, keep, other],
        pieces.size,
        vmem=4,
    )
    theirs = lax.ppermute(give, "ctx", swap)
    windows[3](give, mine)
    return mine, theirs


def body(query, keys, values, gain, cotangent):
    length, width = query.shape
    half = width // HEAD_DIM // 2
    square = 2 * length * length * HEAD_DIM * half
    small = 2 * length * HEAD_DIM * HEAD_DIM * half
    gain = gain.reshape(1, width)
    whole = array((length, width), BF)
    part = lambda dtype: array((length, half * HEAD_DIM), dtype)
    states = array((half * HEAD_DIM, HEAD_DIM), F32)
    lanes = array((length, HEAD_DIM), F32)
    rows = array((8, 128), F32)
    dmas = pltpu.SemaphoreType.DMA
    halves = [pltpu.VMEM((length, half * HEAD_DIM), BF)] * 2
    made = {}

    def made_by(name, side, kernel, outs, args, flops, after=(), **options):
        made[name, side] = call(functools.partial(kernel, side), outs, args, flops, after, **options)
        return made[name, side]

    in_hbm = [pltpu.with_memory_space_constraint(a, pltpu.HBM) for a in (keys, values)]

    (send,) = made_by(
        "state", OTHER, state_kernel, [states], in_hbm, small,
        ins=HBM, scratch=halves + [dmas((2, half))],
    )

    def state_own(ready):
        return made_by("state", OWN, state_own_kernel, [states], [keys, values], small, [ready])

    def intra(side, ready):
        outs = [
            array((half * HEAD_DIM, length), BF),
            array((3 * half, length // 2, length // 2), BF),
            part(F32),
        ]
        args = [query, keys, values]
        return made_by("intra", side, intra_kernel, outs, args, 3 * square, [ready])

    def mix(side, before, after, *sums):
        args = [query, before, made["intra", side][2], cotangent, gain, *sums]
        return made_by("mix", side, mix_kernel, [part(F32), rows], args, small, after)

    mine, theirs = carried(
        send,
        False,
        [
            state_own,
            lambda ready: intra(OWN, ready),
            lambda ready: intra(OTHER, ready),
            lambda ready, mine: mix(OWN, mine, [ready]),
        ],
    )
    before = (mine, theirs)
    _, sums = mix(OTHER, theirs, (), made["mix", OWN][1])
    heads = lax.axis_size("head")
    others = [
        lax.ppermute(sums, "head", [(i, i ^ j) for i in range(heads)]) for j in (1, 3, 2)
    ]

    def grad_args(side):
        return [made["intra", side][0], made["mix", side][0], cotangent, gain]

    gm_other, send, inverse, coef = call(
        grad_other_kernel,
        [part(BF), states, lanes, lanes],
        grad_args(OTHER) + [sums, *others],
        small,
    )

    def grad_own(ready):
        made["grad"] = call(
            grad_own_kernel,
            [part(BF), states],
            grad_args(OWN) + [inverse, coef],
            small,
            [ready],
        )
        return made["grad"]

    def back(side, ready):
        gm = gm_other if side == OTHER else made["grad"][0]
        mixture, weights = made["mix", side][0], made["intra", side][1]
        args = [query, keys, values, gm, before[side], mixture, inverse, gain, weights]
        outs = [part(BF), part(BF), part(F32), part(F32)]
        return made_by("back", side, back_kernel, outs, args, 4 * square, [ready])

    def last_own(ready, mine):
        own, other = made["back", OWN], made["back", OTHER]
        made["last"] = pl.pallas_call(
            lambda *refs: last_own_kernel(*refs[:9], *refs[10:]),
            out_shape=[part(BF), part(BF), whole, whole],
            in_specs=[VMEM] * 9 + [ANY],
            out_specs=[VMEM, VMEM, HBM, HBM],
            scratch_shapes=[dmas((4,))],
            compiler_params=pltpu.CompilerParams(vmem_limit_bytes=16 << 20),
            cost_estimate=pl.CostEstimate(
                flops=2 * small, bytes_accessed=8 * whole.size, transcendentals=0
            ),
        )(keys, values, mine, own[2], own[3], own[0], other[0], own[1], other[1], ready)
        return made["last"]

    mine, theirs = carried(
        send,
        True,
        [
            grad_own,
            lambda ready: back(OTHER, ready),
            lambda ready: back(OWN, ready),
            last_own,
        ],
    )
    gk_own, gv_own, attended, grad_q = made["last"]
    grad_k, grad_v = call(
        last_other_kernel,
        [whole, whole],
        [keys, values, theirs, *made["back", OTHER][2:], gk_own, gv_own],
        2 * small,
        out=HBM,
        scratch=halves + [dmas((2,)), dmas((2, half))],
    )
    return attended, grad_q, grad_k, grad_v


def solution(mesh):
    spec = P("ctx", "head")
    return jax.shard_map(
        body,
        mesh=mesh,
        in_specs=(spec, spec, spec, P("head"), spec),
        out_specs=(spec,) * 4,
        check_vma=False,
    )
```

time: 94 us -> 89 us (0.947)
  starting transfers between devices: 30.2 us -> 27.8 us
  local copies, waits for them, and re-layouts: 1.25 us -> 0.03 us
  Pallas kernels: 17.8 us -> 16.6 us
    ppermute x2, starting transfers between devices: 9.1 us -> 2.82 us  [carried(): theirs = lax.ppermute(give, 'ctx', swap)]
    ppermute x2, starting transfers between devices: 4.59 us -> 8.88 us  [carried(): near = lax.ppermute(total, 'ctx', near_z)]
    pallas_call x20 -> x21, Pallas kernels: 17.8 us -> 14.9 us  [call(): pl.pallas_call(body, out_shape=outs, in_specs=[ins] * len(args) + [ANY] *...]
    pallas_call x0 -> x1, Pallas kernels: none -> 1.79 us  [last_own(): pl.pallas_call(lambda *refs: last_own_kernel(*refs[:9], *refs[10:]), out_...]
    unnamed x12 -> x10, local copies, waits for them, and re-layouts: 1.25 us -> 0.03 us
  transfers between devices with their start and end apart: 11 -> 11, of which waited for: 5 -> 8; matrix products, arithmetic and copies ran while one was open for 0% -> 0% of each run, Pallas kernels for 10% -> 13%
where the time goes in v3:
time: 89 us; the launch traced here: 88.7 us
  blocking collectives  37.1 us (42%)
  starting transfers between devices  27.8 us (31%)
  Pallas kernels  16.6 us (19%)
  waiting for transfers between devices  6.14 us (7%)
  between operations  0.96 us (1%)
    all_to_all x4, blocking collectives, carried(): pieces = lax.all_to_all(pieces, 'ctx', 0, 0, axis_index_groups=groups)  37.1 us
    pallas_call x21, Pallas kernels, call(): pl.pallas_call(body, out_shape=outs, in_specs=[ins] * len(args) + [ANY] *...  14.9 us
    ppermute x2, starting transfers between devices, carried(): near = lax.ppermute(total, 'ctx', near_z)  8.88 us
    ppermute x2, starting transfers between devices, carried(): far = lax.ppermute(total, 'ctx', far_z)  7.18 us
    ppermute x2, starting transfers between devices, carried(): other = lax.ppermute(send, 'ctx', swap)  5.19 us
    ppermute x3, starting transfers between devices, body(): lax.ppermute(sums, 'head', [(i, i ^ j) for i in range(heads)])  3.78 us
    ppermute x3, waiting for transfers between devices, body(): lax.ppermute(sums, 'head', [(i, i ^ j) for i in range(heads)])  2.89 us
    ppermute x2, starting transfers between devices, carried(): theirs = lax.ppermute(give, 'ctx', swap)  2.82 us
  transfers between devices with their start and end apart: 11, of which 8 were waited for; matrix products, arithmetic and copies ran while one was open for 0% of the time, Pallas kernels for 13%

profile of v3, /device:TPU:1, one launch (start us, length us, event | category | flops | bytes accessed | tf_op | source)
XLA Modules:
  0.0 88.7 jit_solution(5445368611561039447)
XLA Ops:
  0.7 2.1 %shard_map.84.refs_2_ = f32[512,128]{1,0:T(8,128)S(1)} custom-call(bf16[512,1024]{1,0:T(8,128)(2,1)} %refs_0_.19, bf16[512,1024]{1,0:T(8,128)(2,1)} %refs_1_.15), custom_call_target="tpu_custom_call" | custom-call | flops 67108864 | bytes 2359296 | tf_op jit(solution)/shard_map/pallas_call | solution.py:36
  2.8 3.3 %collective-permute-start = (f32[512,128]{1,0:T(8,128)S(1)}, f32[512,128]{1,0:T(8,128)S(1)}, u32[]{:S(2)}, u32[]{:S(2)}) collective-permute-start(f32[512,128]{1,0:T(8,128)S(1)} %shard_map.84.refs_2_), channel_id=1, source_target_pairs={{0,4},{4,0},{8,12},{12,8},{16,20},{20,16},{24,28},{28,24},{32,36},... | collective-permute-start | bytes 786440 | tf_op jit(solution)/shard_map/ppermute | solution.py:322
  6.1 0.5 shard_map.85.refs_0_.refs_1_
  6.6 0.7 collective-permute-done.refs_1_.refs_2_
  7.3 9.6 %all_to_all.20.refs_0_ = f32[8,64,128]{2,1,0:T(8,128)S(1)} all-to-all(f32[8,64,128]{2,1,0:T(8,128)S(1)} %shard_map.86), channel_id=1, replica_groups={{0,8,16,24,32,40,48,56},{4,12,20,28,36,44,52,60},{68,76,84,92,100,108,1..., dimensions={0} | all-to-all | bytes 524288 | tf_op jit(solution)/shard_map/all_to_all | solution.py:325
  17.0 4.9 %collective-permute-start.1 = (f32[64,128]{1,0:T(8,128)S(1)}, f32[64,128]{1,0:T(8,128)S(1)}, u32[]{:S(2)}, u32[]{:S(2)}) collective-permute-start(f32[64,128]{1,0:T(8,128)S(1)} %get-tuple-element.42.refs_3_.refs_0_), channel_id=1, source_target_pairs={{0,68},{4,64},{8,76},{12,72},{16,84},{20,80},{24,92},{28,88},{32,1... | collective-permute-start | bytes 98312 | tf_op jit(solution)/shard_map/ppermute | solution.py:333
  21.9 1.6 %shard_map.88 = (bf16[512,512]{1,0:T(8,128)(2,1)S(1)}, bf16[12,256,256]{2,1,0:T(8,128)(2,1)S(1)}, f32[512,512]{1,0:T(8,128)S(1)}) custom-call(bf16[512,1024]{1,0:T(8,128)(2,1)S(1)} %copy-done.2, bf16[512,1024]{1,0:T(8,128)(2,1)S(1)} %copy-done, bf16[512,1024]{1,0:T(8,128)(2,1)S(1)} %copy-done.1, f32[64,128]{1,0:T(8,128)S(1)} %get-tuple-element.42.refs_3_.refs_0_), custom_call_target="tpu_custom_call" | custom-call | flops 805306368 | bytes 6291456 | tf_op jit(solution)/shard_map/pallas_call | solution.py:36
  23.5 0.4 collective-permute-done.1.refs_1_
  23.9 4.4 %collective-permute-start.2 = (f32[64,128]{1,0:T(8,128)S(1)}, f32[64,128]{1,0:T(8,128)S(1)}, u32[]{:S(2)}, u32[]{:S(2)}) collective-permute-start(f32[64,128]{1,0:T(8,128)S(1)} %shard_map.89.refs_3_), channel_id=1, source_target_pairs={{0,196},{4,192},{8,204},{12,200},{16,212},{20,208},{24,220},{28,21... | collective-permute-start | bytes 98312 | tf_op jit(solution)/shard_map/ppermute | solution.py:336
  28.3 1.6 %shard_map.90 = (bf16[512,512]{1,0:T(8,128)(2,1)S(1)}, bf16[12,256,256]{2,1,0:T(8,128)(2,1)S(1)}, f32[512,512]{1,0:T(8,128)S(1)}) custom-call(bf16[512,1024]{1,0:T(8,128)(2,1)S(1)} %copy-done.2, bf16[512,1024]{1,0:T(8,128)(2,1)S(1)} %copy-done, bf16[512,1024]{1,0:T(8,128)(2,1)S(1)} %copy-done.1, f32[64,128]{1,0:T(8,128)S(1)} %shard_map.89.refs_3_), custom_call_target="tpu_custom_call" | custom-call | flops 805306368 | bytes 6291456 | tf_op jit(solution)/shard_map/pallas_call | solution.py:36
  30.0 10.1 %all_to_all.21.refs_0_ = f32[8,64,128]{2,1,0:T(8,128)S(1)} all-to-all(f32[8,64,128]{2,1,0:T(8,128)S(1)} %shard_map.91), channel_id=1, replica_groups={{0,8,16,24,32,40,48,56},{4,12,20,28,36,44,52,60},{68,76,84,92,100,108,1..., dimensions={0} | all-to-all | bytes 524288 | tf_op jit(solution)/shard_map/all_to_all | solution.py:346
  40.1 0.8 collective-permute-start.3
  40.9 0.6 shard_map.93
  41.5 0.5 collective-permute-done.3.refs_1_.refs_4_
  42.0 0.6 shard_map.94
  42.6 3.0 %collective-permute-start.6 = (f32[8,128]{1,0:T(8,128)S(1)}, f32[8,128]{1,0:T(8,128)S(1)}, u32[]{:S(2)}, u32[]{:S(2)}) collective-permute-start(f32[8,128]{1,0:T(8,128)S(1)} %get-tuple-element.53.refs_4_), channel_id=1, source_target_pairs={{0,2},{1,3},{2,0},{3,1},{4,6},{5,7},{6,4},{7,5},{8,10},{9,11},{10,... | collective-permute-start | bytes 12296 | tf_op jit(solution)/shard_map/ppermute | solution.py:415
  45.7 0.8 collective-permute-start.5
  46.7 2.6 %collective-permute-done.5.refs_6_ = f32[8,128]{1,0:T(8,128)S(1)} collective-permute-done((f32[8,128]{1,0:T(8,128)S(1)}, f32[8,128]{1,0:T(8,128)S(1)}, u32[]{:S(2)}, u32[]{:S(2)}) %collective-permute-start.5) | collective-permute-done | bytes 4128 | tf_op jit(solution)/shard_map/ppermute | solution.py:415
  49.3 0.6 shard_map.95
  50.0 1.9 %collective-permute-start.7 = (f32[512,128]{1,0:T(8,128)S(1)}, f32[512,128]{1,0:T(8,128)S(1)}, u32[]{:S(2)}, u32[]{:S(2)}) collective-permute-start(f32[512,128]{1,0:T(8,128)S(1)} %get-tuple-element.56.refs_6_), channel_id=1, source_target_pairs={{0,4},{4,0},{8,12},{12,8},{16,20},{20,16},{24,28},{28,24},{32,36},... | collective-permute-start | bytes 786440 | tf_op jit(solution)/shard_map/ppermute | solution.py:322
  51.8 0.5 shard_map.96
  52.4 0.6 collective-permute-done.7.refs_1_.refs_2_
  53.0 8.9 %all_to_all.22.refs_0_ = f32[8,64,128]{2,1,0:T(8,128)S(1)} all-to-all(f32[8,64,128]{2,1,0:T(8,128)S(1)} %shard_map.97), channel_id=1, replica_groups={{0,8,16,24,32,40,48,56},{4,12,20,28,36,44,52,60},{68,76,84,92,100,108,1..., dimensions={0} | all-to-all | bytes 524288 | tf_op jit(solution)/shard_map/all_to_all | solution.py:325
  61.9 4.0 %collective-permute-start.8 = (f32[64,128]{1,0:T(8,128)S(1)}, f32[64,128]{1,0:T(8,128)S(1)}, u32[]{:S(2)}, u32[]{:S(2)}) collective-permute-start(f32[64,128]{1,0:T(8,128)S(1)} %get-tuple-element.59.refs_9_.refs_0_), channel_id=1, source_target_pairs={{0,68},{4,64},{8,76},{12,72},{16,84},{20,80},{24,92},{28,88},{32,1... | collective-permute-start | bytes 98312 | tf_op jit(solution)/shard_map/ppermute | solution.py:333
  65.8 2.4 %shard_map.99 = (bf16[512,512]{1,0:T(8,128)(2,1)S(1)}, bf16[512,512]{1,0:T(8,128)(2,1)S(1)}, f32[512,512]{1,0:T(8,128)S(1)}, f32[512,512]{1,0:T(8,128)S(1)}) custom-call(bf16[512,1024]{1,0:T(8,128)(2,1)S(1)} %copy-done.2, bf16[512,1024]{1,0:T(8,128)(2,1)S(1)} %copy-done, bf16[512,1024]{1,0:T(8,128)(2,1)S(1)} %copy-done.1, ...), custom_call_target="tpu_custom_call" | custom-call | flops 1073741824 | bytes 9965568 | tf_op jit(solution)/shard_map/pallas_call | solution.py:36
  68.6 2.8 %collective-permute-start.9 = (f32[64,128]{1,0:T(8,128)S(1)}, f32[64,128]{1,0:T(8,128)S(1)}, u32[]{:S(2)}, u32[]{:S(2)}) collective-permute-start(f32[64,128]{1,0:T(8,128)S(1)} %shard_map.100.refs_9_), channel_id=1, source_target_pairs={{0,196},{4,192},{8,204},{12,200},{16,212},{20,208},{24,220},{28,21... | collective-permute-start | bytes 98312 | tf_op jit(solution)/shard_map/ppermute | solution.py:336
  71.4 2.4 %shard_map.101 = (bf16[512,512]{1,0:T(8,128)(2,1)S(1)}, bf16[512,512]{1,0:T(8,128)(2,1)S(1)}, f32[512,512]{1,0:T(8,128)S(1)}, f32[512,512]{1,0:T(8,128)S(1)}) custom-call(bf16[512,1024]{1,0:T(8,128)(2,1)S(1)} %copy-done.2, bf16[512,1024]{1,0:T(8,128)(2,1)S(1)} %copy-done, bf16[512,1024]{1,0:T(8,128)(2,1)S(1)} %copy-done.1, ...), custom_call_target="tpu_custom_call" | custom-call | flops 1073741824 | bytes 9965568 | tf_op jit(solution)/shard_map/pallas_call | solution.py:36
  73.8 0.7 collective-permute-done.9.refs_2_
  74.5 8.5 %all_to_all.23.refs_0_ = f32[8,64,128]{2,1,0:T(8,128)S(1)} all-to-all(f32[8,64,128]{2,1,0:T(8,128)S(1)} %shard_map.102), channel_id=1, replica_groups={{0,8,16,24,32,40,48,56},{4,12,20,28,36,44,52,60},{68,76,84,92,100,108,1..., dimensions={0} | all-to-all | bytes 524288 | tf_op jit(solution)/shard_map/all_to_all | solution.py:346
  83.1 2.0 %collective-permute-start.10 = (f32[512,128]{1,0:T(8,128)S(1)}, f32[512,128]{1,0:T(8,128)S(1)}, u32[]{:S(2)}, u32[]{:S(2)}) collective-permute-start(f32[512,128]{1,0:T(8,128)S(1)} %get-tuple-element.72.refs_9_), channel_id=1, source_target_pairs={{0,4},{4,0},{8,12},{12,8},{16,20},{20,16},{24,28},{28,24},{32,36},... | collective-permute-start | bytes 786440 | tf_op jit(solution)/shard_map/ppermute | solution.py:354
  85.2 1.8 %shard_map.104 = (bf16[512,512]{1,0:T(8,128)(2,1)S(1)}, bf16[512,512]{1,0:T(8,128)(2,1)S(1)}, bf16[512,1024]{1,0:T(8,128)(2,1)}, bf16[512,1024]{1,0:T(8,128)(2,1)}) custom-call(bf16[512,1024]{1,0:T(8,128)(2,1)S(1)} %copy-done, bf16[512,1024]{1,0:T(8,128)(2,1)S(1)} %copy-done.1, f32[512,128]{1,0:T(8,128)S(1)} %get-tuple-element.66.refs_2_, ...), custom_call_target="tpu_custom_call" | custom-call | flops 134217728 | bytes 4194304 | tf_op jit(solution)/shard_map/pallas_call | solution.py:447
  87.0 1.6 %shard_map.105 = (bf16[512,1024]{1,0:T(8,128)(2,1)}, bf16[512,1024]{1,0:T(8,128)(2,1)}) custom-call(bf16[512,1024]{1,0:T(8,128)(2,1)S(1)} %copy-done, bf16[512,1024]{1,0:T(8,128)(2,1)S(1)} %copy-done.1, f32[512,128]{1,0:T(8,128)S(1)} %collective-permute-done.10.refs_2_, f32[512,512]{1,0:T(8,128)S(1)} %get-tuple-element.75.refs_3_, ...), custom_call_target="tpu_custom_call" | custom-call | flops 134217728 | bytes 7602176 | tf_op jit(solution)/shard_map/pallas_call | solution.py:36
  (26 shorter events, 1.0 us)
Async XLA Ops:
  0.6 5.5 %copy-start.1 = (bf16[512,1024]{1,0:T(8,128)(2,1)S(1)}, bf16[512,1024]{1,0:T(8,128)(2,1)}, u32[]{:S(2)}) copy-start(bf16[512,1024]{1,0:T(8,128)(2,1)} %refs_1_.15) | copy-start | bytes 3145732
  0.6 5.5 %copy-start = (bf16[512,1024]{1,0:T(8,128)(2,1)S(1)}, bf16[512,1024]{1,0:T(8,128)(2,1)}, u32[]{:S(2)}) copy-start(bf16[512,1024]{1,0:T(8,128)(2,1)} %refs_0_.19) | copy-start | bytes 3145732
  2.8 19.1 %copy-start.2 = (bf16[512,1024]{1,0:T(8,128)(2,1)S(1)}, bf16[512,1024]{1,0:T(8,128)(2,1)}, u32[]{:S(2)}) copy-start(bf16[512,1024]{1,0:T(8,128)(2,1)} %refs_0_.17) | copy-start | bytes 3145732
  2.8 4.5 %collective-permute-start = (f32[512,128]{1,0:T(8,128)S(1)}, f32[512,128]{1,0:T(8,128)S(1)}, u32[]{:S(2)}, u32[]{:S(2)}) collective-permute-start(f32[512,128]{1,0:T(8,128)S(1)} %shard_map.84.refs_2_), channel_id=1, source_target_pairs={{0,4},{4,0},{8,12},{12,8},{16,20},{20,16},{24,28},{28,24},{32,36},... | collective-permute-start | bytes 786440 | tf_op jit(solution)/shard_map/ppermute | solution.py:322
  17.0 6.9 %collective-permute-start.1 = (f32[64,128]{1,0:T(8,128)S(1)}, f32[64,128]{1,0:T(8,128)S(1)}, u32[]{:S(2)}, u32[]{:S(2)}) collective-permute-start(f32[64,128]{1,0:T(8,128)S(1)} %get-tuple-element.42.refs_3_.refs_0_), channel_id=1, source_target_pairs={{0,68},{4,64},{8,76},{12,72},{16,84},{20,80},{24,92},{28,88},{32,1... | collective-permute-start | bytes 98312 | tf_op jit(solution)/shard_map/ppermute | solution.py:333
  23.9 6.0 %collective-permute-start.2 = (f32[64,128]{1,0:T(8,128)S(1)}, f32[64,128]{1,0:T(8,128)S(1)}, u32[]{:S(2)}, u32[]{:S(2)}) collective-permute-start(f32[64,128]{1,0:T(8,128)S(1)} %shard_map.89.refs_3_), channel_id=1, source_target_pairs={{0,196},{4,192},{8,204},{12,200},{16,212},{20,208},{24,220},{28,21... | collective-permute-start | bytes 98312 | tf_op jit(solution)/shard_map/ppermute | solution.py:336
  29.9 11.0 %copy-start.3 = (bf16[512,1024]{1,0:T(8,128)(2,1)S(1)}, bf16[512,1024]{1,0:T(8,128)(2,1)}, u32[]{:S(2)}) copy-start(bf16[512,1024]{1,0:T(8,128)(2,1)} %refs_2_.9) | copy-start | bytes 3145732
  29.9 11.0 %copy-start.4 = (f32[1024]{0:T(1024)S(1)}, f32[1024]{0:T(1024)}, u32[]{:S(2)}) copy-start(f32[1024]{0:T(1024)} %param.8) | copy-start | bytes 12292
  40.1 1.9 %collective-permute-start.3 = (f32[512,128]{1,0:T(8,128)S(1)}, f32[512,128]{1,0:T(8,128)S(1)}, u32[]{:S(2)}, u32[]{:S(2)}) collective-permute-start(f32[512,128]{1,0:T(8,128)S(1)} %get-tuple-element.48.refs_5_), channel_id=1, source_target_pairs={{0,4},{4,0},{8,12},{12,8},{16,20},{20,16},{24,28},{28,24},{32,36},... | collective-permute-start | bytes 786440 | tf_op jit(solution)/shard_map/ppermute | solution.py:354
  42.6 4.0 %collective-permute-start.6 = (f32[8,128]{1,0:T(8,128)S(1)}, f32[8,128]{1,0:T(8,128)S(1)}, u32[]{:S(2)}, u32[]{:S(2)}) collective-permute-start(f32[8,128]{1,0:T(8,128)S(1)} %get-tuple-element.53.refs_4_), channel_id=1, source_target_pairs={{0,2},{1,3},{2,0},{3,1},{4,6},{5,7},{6,4},{7,5},{8,10},{9,11},{10,... | collective-permute-start | bytes 12296 | tf_op jit(solution)/shard_map/ppermute | solution.py:415
  45.7 3.7 %collective-permute-start.5 = (f32[8,128]{1,0:T(8,128)S(1)}, f32[8,128]{1,0:T(8,128)S(1)}, u32[]{:S(2)}, u32[]{:S(2)}) collective-permute-start(f32[8,128]{1,0:T(8,128)S(1)} %get-tuple-element.53.refs_4_), channel_id=1, source_target_pairs={{0,3},{1,2},{2,1},{3,0},{4,7},{5,6},{6,5},{7,4},{8,11},{9,10},{10,... | collective-permute-start | bytes 12296 | tf_op jit(solution)/shard_map/ppermute | solution.py:415
  46.4 2.9 %collective-permute-start.4 = (f32[8,128]{1,0:T(8,128)S(1)}, f32[8,128]{1,0:T(8,128)S(1)}, u32[]{:S(2)}, u32[]{:S(2)}) collective-permute-start(f32[8,128]{1,0:T(8,128)S(1)} %get-tuple-element.53.refs_4_), channel_id=1, source_target_pairs={{0,1},{1,0},{2,3},{3,2},{4,5},{5,4},{6,7},{7,6},{8,9},{9,8},{10,11... | collective-permute-start | bytes 12296 | tf_op jit(solution)/shard_map/ppermute | solution.py:415
  50.0 3.0 %collective-permute-start.7 = (f32[512,128]{1,0:T(8,128)S(1)}, f32[512,128]{1,0:T(8,128)S(1)}, u32[]{:S(2)}, u32[]{:S(2)}) collective-permute-start(f32[512,128]{1,0:T(8,128)S(1)} %get-tuple-element.56.refs_6_), channel_id=1, source_target_pairs={{0,4},{4,0},{8,12},{12,8},{16,20},{20,16},{24,28},{28,24},{32,36},... | collective-permute-start | bytes 786440 | tf_op jit(solution)/shard_map/ppermute | solution.py:322
  61.9 6.7 %collective-permute-start.8 = (f32[64,128]{1,0:T(8,128)S(1)}, f32[64,128]{1,0:T(8,128)S(1)}, u32[]{:S(2)}, u32[]{:S(2)}) collective-permute-start(f32[64,128]{1,0:T(8,128)S(1)} %get-tuple-element.59.refs_9_.refs_0_), channel_id=1, source_target_pairs={{0,68},{4,64},{8,76},{12,72},{16,84},{20,80},{24,92},{28,88},{32,1... | collective-permute-start | bytes 98312 | tf_op jit(solution)/shard_map/ppermute | solution.py:333
  68.6 5.8 %collective-permute-start.9 = (f32[64,128]{1,0:T(8,128)S(1)}, f32[64,128]{1,0:T(8,128)S(1)}, u32[]{:S(2)}, u32[]{:S(2)}) collective-permute-start(f32[64,128]{1,0:T(8,128)S(1)} %shard_map.100.refs_9_), channel_id=1, source_target_pairs={{0,196},{4,192},{8,204},{12,200},{16,212},{20,208},{24,220},{28,21... | collective-permute-start | bytes 98312 | tf_op jit(solution)/shard_map/ppermute | solution.py:336
  83.1 3.8 %collective-permute-start.10 = (f32[512,128]{1,0:T(8,128)S(1)}, f32[512,128]{1,0:T(8,128)S(1)}, u32[]{:S(2)}, u32[]{:S(2)}) collective-permute-start(f32[512,128]{1,0:T(8,128)S(1)} %get-tuple-element.72.refs_9_), channel_id=1, source_target_pairs={{0,4},{4,0},{8,12},{12,8},{16,20},{20,16},{24,28},{28,24},{32,36},... | collective-permute-start | bytes 786440 | tf_op jit(solution)/shard_map/ppermute | solution.py:354

commit v4 on v3

--- a/solution.py
+++ b/solution.py
@@ -30,14 +30,17 @@
     nbytes = sum(a.size * a.dtype.itemsize for a in args)
     nbytes += sum(o.size * o.dtype.itemsize for o in outs)
 
+    ins = ins if isinstance(ins, list) else [ins] * len(args)
+    out = out if isinstance(out, list) else [out] * len(outs)
+
     def body(*refs):
         kernel(*refs[: len(args)], *refs[len(args) + len(after) :])
 
     return pl.pallas_call(
         body,
         out_shape=outs,
-        in_specs=[ins] * len(args) + [ANY] * len(after),
-        out_specs=[out] * len(outs),
+        in_specs=ins + [ANY] * len(after),
+        out_specs=out,
         scratch_shapes=list(scratch),
         compiler_params=pltpu.CompilerParams(vmem_limit_bytes=vmem << 20),
         cost_estimate=pl.CostEstimate(flops=flops, bytes_accessed=nbytes, transcendentals=0),
@@ -81,19 +84,21 @@
         s_ref[at(j), :] = dot(a_ref[:, c], b_ref[:, c], 0, 0)
 
 
+def columns(side, half):
+    mine = my_half()
+    base = (mine if side == OWN else 1 - mine) * (half * HEAD_DIM)
+    return pl.ds(pl.multiple_of(base, half * HEAD_DIM), half * HEAD_DIM)
+
+
 def state_kernel(side, a_hbm, b_hbm, s_ref, a_ref, b_ref, sems):
     half = a_ref.shape[1] // HEAD_DIM
     copies = []
+    for i, (src, dst) in enumerate(((a_hbm, a_ref), (b_hbm, b_ref))):
+        copies.append(pltpu.make_async_copy(src.at[:, columns(side, half)], dst, sems.at[i]))
+        copies[-1].start()
+    for copy in copies:
+        copy.wait()
     for j in range(half):
-        for i, (src, dst) in enumerate(((a_hbm, a_ref), (b_hbm, b_ref))):
-            copy = pltpu.make_async_copy(
-                src.at[:, cols(side, j, half)], dst.at[:, at(j)], sems.at[i, j]
-            )
-            copy.start()
-            copies.append(copy)
-    for j in range(half):
-        copies[2 * j].wait()
-        copies[2 * j + 1].wait()
         s_ref[at(j), :] = dot(a_ref[:, at(j)], b_ref[:, at(j)], 0, 0)
 
 
@@ -187,9 +192,9 @@
     grad(OWN, qt_ref, m_ref, c_ref, g_ref, inv_ref, cf_ref, gm_ref, s_ref)
 
 
-def back_kernel(
+def back(
     side, q_ref, k_ref, v_ref, gm_ref, s_ref, m_ref, inv_ref, g_ref, wt_ref,
-    at_ref, gq_ref, gk_ref, gv_ref,
+    at_ref, gq_ref, gk_ref, gv_ref, then=lambda j: None,
 ):
     n = q_ref.shape[0] // 2
     half = gm_ref.shape[1] // HEAD_DIM
@@ -208,17 +213,44 @@
         top, left, right = wt_ref[3 * j], wt_ref[3 * j + 1], wt_ref[3 * j + 2]
         gv_ref[:n, at(j)] = dot(top, gm[:n], 1, 0) + dot(left, gm[n:], 1, 0)
         gv_ref[n:, at(j)] = dot(right, gm[n:], 1, 0)
+        then(j)
 
 
 def send_out(pairs, half, sems):
-    mine = my_half()
     copies = []
     for i, (side, src, dst) in enumerate(pairs):
-        base = (mine if side == OWN else 1 - mine) * (half * HEAD_DIM)
-        c = pl.ds(pl.multiple_of(base, half * HEAD_DIM), half * HEAD_DIM)
-        copies.append(pltpu.make_async_copy(src, dst.at[:, c], sems.at[i]))
+        copies.append(pltpu.make_async_copy(src, dst.at[:, columns(side, half)], sems.at[i]))
         copies[-1].start()
     return copies
+
+
+def send_heads(j, half, side, pairs, sems):
+    copies = []
+    for i, (src, dst) in enumerate(pairs):
+        copies.append(
+            pltpu.make_async_copy(src.at[:, at(j)], dst.at[:, cols(side, j, half)], sems.at[i, j])
+        )
+        copies[-1].start()
+    return copies
+
+
+def back_other_kernel(*refs):
+    back(OTHER, *refs)
+
+
+def back_own_kernel(*refs):
+    ins, (at_other, gq_other) = refs[:9], refs[9:11]
+    gk_ref, gv_ref, at_hbm, gq_hbm, at_ref, gq_ref, sems, head_sems = refs[11:]
+    half = gk_ref.shape[1] // HEAD_DIM
+    copies = send_out([(OTHER, at_other, at_hbm), (OTHER, gq_other, gq_hbm)], half, sems)
+    pairs = ((at_ref, at_hbm), (gq_ref, gq_hbm))
+
+    def then(j):
+        copies.extend(send_heads(j, half, OWN, pairs, head_sems))
+
+    back(OWN, *ins, at_ref, gq_ref, gk_ref, gv_ref, then)
+    for copy in copies:
+        copy.wait()
 
 
 def last(side, k_ref, v_ref, s_ref, gki_ref, gvi_ref, gk_ref, gv_ref, then=lambda j: None):
@@ -231,19 +263,8 @@
         then(j)
 
 
-def last_own_kernel(
-    k_ref, v_ref, s_ref, gki_ref, gvi_ref, ato_ref, ats_ref, gqo_ref, gqs_ref,
-    gk_ref, gv_ref, at_hbm, gq_hbm, sems,
-):
-    half = gki_ref.shape[1] // HEAD_DIM
-    pairs = [
-        (OWN, ato_ref, at_hbm), (OTHER, ats_ref, at_hbm),
-        (OWN, gqo_ref, gq_hbm), (OTHER, gqs_ref, gq_hbm),
-    ]
-    copies = send_out(pairs, half, sems)
-    last(OWN, k_ref, v_ref, s_ref, gki_ref, gvi_ref, gk_ref, gv_ref)
-    for copy in copies:
-        copy.wait()
+def last_own_kernel(*refs):
+    last(OWN, *refs)
 
 
 def last_other_kernel(
@@ -252,14 +273,10 @@
 ):
     half = gki_ref.shape[1] // HEAD_DIM
     copies = send_out([(OWN, gko_ref, gk_hbm), (OWN, gvo_ref, gv_hbm)], half, sems)
+    pairs = ((gk_ref, gk_hbm), (gv_ref, gv_hbm))
 
     def then(j):
-        for i, (src, dst) in enumerate(((gk_ref, gk_hbm), (gv_ref, gv_hbm))):
-            copy = pltpu.make_async_copy(
-                src.at[:, at(j)], dst.at[:, cols(OTHER, j, half)], head_sems.at[i, j]
-            )
-            copy.start()
-            copies.append(copy)
+        copies.extend(send_heads(j, half, OTHER, pairs, head_sems))
 
     last(OTHER, k_ref, v_ref, s_ref, gki_ref, gvi_ref, gk_ref, gv_ref, then)
     for copy in copies:
@@ -379,7 +396,7 @@
 
     (send,) = made_by(
         "state", OTHER, state_kernel, [states], in_hbm, small,
-        ins=HBM, scratch=halves + [dmas((2, half))],
+        ins=HBM, scratch=halves + [dmas((2,))],
     )
 
     def state_own(ready):
@@ -435,48 +452,44 @@
         )
         return made["grad"]
 
-    def back(side, ready):
+    def back_args(side):
         gm = gm_other if side == OTHER else made["grad"][0]
         mixture, weights = made["mix", side][0], made["intra", side][1]
-        args = [query, keys, values, gm, before[side], mixture, inverse, gain, weights]
+        return [query, keys, values, gm, before[side], mixture, inverse, gain, weights]
+
+    def back_other(ready):
         outs = [part(BF), part(BF), part(F32), part(F32)]
-        return made_by("back", side, back_kernel, outs, args, 4 * square, [ready])
+        made["back"] = call(back_other_kernel, outs, back_args(OTHER), 4 * square, [ready])
+        return made["back"]
+
+    def back_own(ready):
+        *made["rows"], gk, gv = call(
+            lambda *refs: back_own_kernel(*refs[:11], *refs[13:15], *refs[11:13], *refs[15:]),
+            [whole, whole, part(F32), part(F32)],
+            [*back_args(OWN), *made["back"][:2]],
+            4 * square,
+            [ready],
+            out=[HBM, HBM, VMEM, VMEM],
+            scratch=halves + [dmas((2,)), dmas((2, half))],
+        )
+        made["own"] = [gk, gv]
+        return made["own"]
 
     def last_own(ready, mine):
-        own, other = made["back", OWN], made["back", OTHER]
-        made["last"] = pl.pallas_call(
-            lambda *refs: last_own_kernel(*refs[:9], *refs[10:]),
-            out_shape=[part(BF), part(BF), whole, whole],
-            in_specs=[VMEM] * 9 + [ANY],
-            out_specs=[VMEM, VMEM, HBM, HBM],
-            scratch_shapes=[dmas((4,))],
-            compiler_params=pltpu.CompilerParams(vmem_limit_bytes=16 << 20),
-            cost_estimate=pl.CostEstimate(
-                flops=2 * small, bytes_accessed=8 * whole.size, transcendentals=0
-            ),
-        )(keys, values, mine, own[2], own[3], own[0], other[0], own[1], other[1], ready)
+        args = [keys, values, mine, *made["own"]]
+        made["last"] = call(last_own_kernel, [part(BF), part(BF)], args, 2 * small, [ready])
         return made["last"]
 
-    mine, theirs = carried(
-        send,
-        True,
-        [
-            grad_own,
-            lambda ready: back(OTHER, ready),
-            lambda ready: back(OWN, ready),
-            last_own,
-        ],
-    )
-    gk_own, gv_own, attended, grad_q = made["last"]
-    grad_k, grad_v = call(
+    _, theirs = carried(send, True, [grad_own, back_other, back_own, last_own])
+    grads = call(
         last_other_kernel,
         [whole, whole],
-        [keys, values, theirs, *made["back", OTHER][2:], gk_own, gv_own],
+        [keys, values, theirs, *made["back"][2:], *made["last"]],
         2 * small,
         out=HBM,
         scratch=halves + [dmas((2,)), dmas((2, half))],
     )
-    return attended, grad_q, grad_k, grad_v
+    return (*made["rows"], *grads)
 
 
 def solution(mesh):

time: 89 us -> 88.4 us (level)
  Pallas kernels: 16.6 us -> 15.5 us
    pallas_call x22, Pallas kernels: 16.6 us -> 15.5 us  [call(): pl.pallas_call(body, out_shape=outs, in_specs=ins + [ANY] * len(after), o...]
  transfers between devices with their start and end apart: 11 -> 11, of which waited for: 8 -> 9; matrix products, arithmetic and copies ran while one was open for 0% -> 0% of each run, Pallas kernels for 13% -> 12%
where the time goes in v4:
time: 88.4 us; the launch traced here: 88.1 us
  blocking collectives  37.6 us (43%)
  starting transfers between devices  27.8 us (31%)
  Pallas kernels  15.5 us (18%)
  waiting for transfers between devices  6.23 us (7%)
  between operations  0.95 us (1%)
    all_to_all x4, blocking collectives, carried(): pieces = lax.all_to_all(pieces, 'ctx', 0, 0, axis_index_groups=groups)  37.6 us
    pallas_call x22, Pallas kernels, call(): pl.pallas_call(body, out_shape=outs, in_specs=ins + [ANY] * len(after), o...  15.5 us
    ppermute x2, starting transfers between devices, carried(): near = lax.ppermute(total, 'ctx', near_z)  8.88 us
    ppermute x2, starting transfers between devices, carried(): far = lax.ppermute(total, 'ctx', far_z)  7.17 us
    ppermute x2, starting transfers between devices, carried(): other = lax.ppermute(send, 'ctx', swap)  5.18 us
    ppermute x3, starting transfers between devices, body(): lax.ppermute(sums, 'head', [(i, i ^ j) for i in range(heads)])  3.78 us
    ppermute x3, waiting for transfers between devices, body(): lax.ppermute(sums, 'head', [(i, i ^ j) for i in range(heads)])  2.89 us
    ppermute x2, starting transfers between devices, carried(): theirs = lax.ppermute(give, 'ctx', swap)  2.8 us
  transfers between devices with their start and end apart: 11, of which 9 were waited for; matrix products, arithmetic and copies ran while one was open for 0% of the time, Pallas kernels for 12%

profile of v4, /device:TPU:1, one launch (start us, length us, event | category | flops | bytes accessed | tf_op | source)
XLA Modules:
  0.0 88.1 jit_solution(13306878336265490503)
XLA Ops:
  0.7 1.7 %shard_map.84.refs_2_ = f32[512,128]{1,0:T(8,128)S(1)} custom-call(bf16[512,1024]{1,0:T(8,128)(2,1)} %refs_0_.19, bf16[512,1024]{1,0:T(8,128)(2,1)} %refs_1_.15), custom_call_target="tpu_custom_call" | custom-call | flops 67108864 | bytes 2359296 | tf_op jit(solution)/shard_map/pallas_call | solution.py:39
  2.4 3.3 %collective-permute-start = (f32[512,128]{1,0:T(8,128)S(1)}, f32[512,128]{1,0:T(8,128)S(1)}, u32[]{:S(2)}, u32[]{:S(2)}) collective-permute-start(f32[512,128]{1,0:T(8,128)S(1)} %shard_map.84.refs_2_), channel_id=1, source_target_pairs={{0,4},{4,0},{8,12},{12,8},{16,20},{20,16},{24,28},{28,24},{32,36},... | collective-permute-start | bytes 786440 | tf_op jit(solution)/shard_map/ppermute | solution.py:339
  5.7 0.5 shard_map.85.refs_0_.refs_1_
  6.2 0.7 collective-permute-done.refs_1_.refs_2_
  6.9 9.6 %all_to_all.20.refs_0_ = f32[8,64,128]{2,1,0:T(8,128)S(1)} all-to-all(f32[8,64,128]{2,1,0:T(8,128)S(1)} %shard_map.86), channel_id=1, replica_groups={{0,8,16,24,32,40,48,56},{4,12,20,28,36,44,52,60},{68,76,84,92,100,108,1..., dimensions={0} | all-to-all | bytes 524288 | tf_op jit(solution)/shard_map/all_to_all | solution.py:342
  16.6 4.9 %collective-permute-start.1 = (f32[64,128]{1,0:T(8,128)S(1)}, f32[64,128]{1,0:T(8,128)S(1)}, u32[]{:S(2)}, u32[]{:S(2)}) collective-permute-start(f32[64,128]{1,0:T(8,128)S(1)} %get-tuple-element.40.refs_3_.refs_0_), channel_id=1, source_target_pairs={{0,68},{4,64},{8,76},{12,72},{16,84},{20,80},{24,92},{28,88},{32,1... | collective-permute-start | bytes 98312 | tf_op jit(solution)/shard_map/ppermute | solution.py:350
  21.5 1.6 %shard_map.88 = (bf16[512,512]{1,0:T(8,128)(2,1)S(1)}, bf16[12,256,256]{2,1,0:T(8,128)(2,1)S(1)}, f32[512,512]{1,0:T(8,128)S(1)}) custom-call(bf16[512,1024]{1,0:T(8,128)(2,1)S(1)} %copy-done.2, bf16[512,1024]{1,0:T(8,128)(2,1)S(1)} %copy-done, bf16[512,1024]{1,0:T(8,128)(2,1)S(1)} %copy-done.1, f32[64,128]{1,0:T(8,128)S(1)} %get-tuple-element.40.refs_3_.refs_0_), custom_call_target="tpu_custom_call" | custom-call | flops 805306368 | bytes 6291456 | tf_op jit(solution)/shard_map/pallas_call | solution.py:39
  23.1 0.4 collective-permute-done.1.refs_1_
  23.5 4.4 %collective-permute-start.2 = (f32[64,128]{1,0:T(8,128)S(1)}, f32[64,128]{1,0:T(8,128)S(1)}, u32[]{:S(2)}, u32[]{:S(2)}) collective-permute-start(f32[64,128]{1,0:T(8,128)S(1)} %shard_map.89.refs_3_), channel_id=1, source_target_pairs={{0,196},{4,192},{8,204},{12,200},{16,212},{20,208},{24,220},{28,21... | collective-permute-start | bytes 98312 | tf_op jit(solution)/shard_map/ppermute | solution.py:353
  27.9 1.6 %shard_map.90 = (bf16[512,512]{1,0:T(8,128)(2,1)S(1)}, bf16[12,256,256]{2,1,0:T(8,128)(2,1)S(1)}, f32[512,512]{1,0:T(8,128)S(1)}) custom-call(bf16[512,1024]{1,0:T(8,128)(2,1)S(1)} %copy-done.2, bf16[512,1024]{1,0:T(8,128)(2,1)S(1)} %copy-done, bf16[512,1024]{1,0:T(8,128)(2,1)S(1)} %copy-done.1, f32[64,128]{1,0:T(8,128)S(1)} %shard_map.89.refs_3_), custom_call_target="tpu_custom_call" | custom-call | flops 805306368 | bytes 6291456 | tf_op jit(solution)/shard_map/pallas_call | solution.py:39
  29.6 10.1 %all_to_all.21.refs_0_ = f32[8,64,128]{2,1,0:T(8,128)S(1)} all-to-all(f32[8,64,128]{2,1,0:T(8,128)S(1)} %shard_map.91), channel_id=1, replica_groups={{0,8,16,24,32,40,48,56},{4,12,20,28,36,44,52,60},{68,76,84,92,100,108,1..., dimensions={0} | all-to-all | bytes 524288 | tf_op jit(solution)/shard_map/all_to_all | solution.py:363
  39.7 0.8 collective-permute-start.3
  40.5 0.6 shard_map.93
  41.1 0.5 collective-permute-done.3.refs_1_.refs_4_
  41.6 0.6 shard_map.94
  42.2 3.0 %collective-permute-start.6 = (f32[8,128]{1,0:T(8,128)S(1)}, f32[8,128]{1,0:T(8,128)S(1)}, u32[]{:S(2)}, u32[]{:S(2)}) collective-permute-start(f32[8,128]{1,0:T(8,128)S(1)} %get-tuple-element.51.refs_4_), channel_id=1, source_target_pairs={{0,2},{1,3},{2,0},{3,1},{4,6},{5,7},{6,4},{7,5},{8,10},{9,11},{10,... | collective-permute-start | bytes 12296 | tf_op jit(solution)/shard_map/ppermute | solution.py:432
  45.2 0.8 collective-permute-start.5
  46.3 2.6 %collective-permute-done.5.refs_6_ = f32[8,128]{1,0:T(8,128)S(1)} collective-permute-done((f32[8,128]{1,0:T(8,128)S(1)}, f32[8,128]{1,0:T(8,128)S(1)}, u32[]{:S(2)}, u32[]{:S(2)}) %collective-permute-start.5) | collective-permute-done | bytes 4128 | tf_op jit(solution)/shard_map/ppermute | solution.py:432
  48.9 0.6 shard_map.95
  49.5 1.9 %collective-permute-start.7 = (f32[512,128]{1,0:T(8,128)S(1)}, f32[512,128]{1,0:T(8,128)S(1)}, u32[]{:S(2)}, u32[]{:S(2)}) collective-permute-start(f32[512,128]{1,0:T(8,128)S(1)} %get-tuple-element.54.refs_6_), channel_id=1, source_target_pairs={{0,4},{4,0},{8,12},{12,8},{16,20},{20,16},{24,28},{28,24},{32,36},... | collective-permute-start | bytes 786440 | tf_op jit(solution)/shard_map/ppermute | solution.py:339
  51.4 0.5 shard_map.96
  51.9 0.6 collective-permute-done.7.refs_1_.refs_2_
  52.6 8.9 %all_to_all.22.refs_0_ = f32[8,64,128]{2,1,0:T(8,128)S(1)} all-to-all(f32[8,64,128]{2,1,0:T(8,128)S(1)} %shard_map.97), channel_id=1, replica_groups={{0,8,16,24,32,40,48,56},{4,12,20,28,36,44,52,60},{68,76,84,92,100,108,1..., dimensions={0} | all-to-all | bytes 524288 | tf_op jit(solution)/shard_map/all_to_all | solution.py:342
  61.5 4.0 %collective-permute-start.8 = (f32[64,128]{1,0:T(8,128)S(1)}, f32[64,128]{1,0:T(8,128)S(1)}, u32[]{:S(2)}, u32[]{:S(2)}) collective-permute-start(f32[64,128]{1,0:T(8,128)S(1)} %get-tuple-element.60.refs_9_.refs_0_), channel_id=1, source_target_pairs={{0,68},{4,64},{8,76},{12,72},{16,84},{20,80},{24,92},{28,88},{32,1... | collective-permute-start | bytes 98312 | tf_op jit(solution)/shard_map/ppermute | solution.py:350
  65.4 2.4 %shard_map.99 = (bf16[512,512]{1,0:T(8,128)(2,1)S(1)}, bf16[512,512]{1,0:T(8,128)(2,1)S(1)}, f32[512,512]{1,0:T(8,128)S(1)}, f32[512,512]{1,0:T(8,128)S(1)}) custom-call(bf16[512,1024]{1,0:T(8,128)(2,1)S(1)} %copy-done.2, bf16[512,1024]{1,0:T(8,128)(2,1)S(1)} %copy-done, bf16[512,1024]{1,0:T(8,128)(2,1)S(1)} %copy-done.1, ...), custom_call_target="tpu_custom_call" | custom-call | flops 1073741824 | bytes 9965568 | tf_op jit(solution)/shard_map/pallas_call | solution.py:39
  68.2 2.8 %collective-permute-start.9 = (f32[64,128]{1,0:T(8,128)S(1)}, f32[64,128]{1,0:T(8,128)S(1)}, u32[]{:S(2)}, u32[]{:S(2)}) collective-permute-start(f32[64,128]{1,0:T(8,128)S(1)} %shard_map.100.refs_11_), channel_id=1, source_target_pairs={{0,196},{4,192},{8,204},{12,200},{16,212},{20,208},{24,220},{28,21... | collective-permute-start | bytes 98312 | tf_op jit(solution)/shard_map/ppermute | solution.py:353
  71.0 3.0 %shard_map.101 = (bf16[512,1024]{1,0:T(8,128)(2,1)}, bf16[512,1024]{1,0:T(8,128)(2,1)}, f32[512,512]{1,0:T(8,128)S(1)}, f32[512,512]{1,0:T(8,128)S(1)}) custom-call(bf16[512,1024]{1,0:T(8,128)(2,1)S(1)} %copy-done.2, bf16[512,1024]{1,0:T(8,128)(2,1)S(1)} %copy-done, bf16[512,1024]{1,0:T(8,128)(2,1)S(1)} %copy-done.1, ...), custom_call_target="tpu_custom_call" | custom-call | flops 1073741824 | bytes 12062720 | tf_op jit(solution)/shard_map/pallas_call | solution.py:39
  74.1 9.0 %all_to_all.23.refs_0_ = f32[8,64,128]{2,1,0:T(8,128)S(1)} all-to-all(f32[8,64,128]{2,1,0:T(8,128)S(1)} %shard_map.102), channel_id=1, replica_groups={{0,8,16,24,32,40,48,56},{4,12,20,28,36,44,52,60},{68,76,84,92,100,108,1..., dimensions={0} | all-to-all | bytes 524288 | tf_op jit(solution)/shard_map/all_to_all | solution.py:363
  83.2 2.0 %collective-permute-start.10 = (f32[512,128]{1,0:T(8,128)S(1)}, f32[512,128]{1,0:T(8,128)S(1)}, u32[]{:S(2)}, u32[]{:S(2)}) collective-permute-start(f32[512,128]{1,0:T(8,128)S(1)} %get-tuple-element.68.refs_5_), channel_id=1, source_target_pairs={{0,4},{4,0},{8,12},{12,8},{16,20},{20,16},{24,28},{28,24},{32,36},... | collective-permute-start | bytes 786440 | tf_op jit(solution)/shard_map/ppermute | solution.py:371
  85.2 0.5 shard_map.104
  85.8 0.6 collective-permute-done.10.refs_2_
  86.4 1.6 %shard_map.105 = (bf16[512,1024]{1,0:T(8,128)(2,1)}, bf16[512,1024]{1,0:T(8,128)(2,1)}) custom-call(bf16[512,1024]{1,0:T(8,128)(2,1)S(1)} %copy-done, bf16[512,1024]{1,0:T(8,128)(2,1)S(1)} %copy-done.1, f32[512,128]{1,0:T(8,128)S(1)} %collective-permute-done.10.refs_2_, f32[512,512]{1,0:T(8,128)S(1)} %get-tuple-element.69.refs_3_, ...), custom_call_target="tpu_custom_call" | custom-call | flops 134217728 | bytes 7602176 | tf_op jit(solution)/shard_map/pallas_call | solution.py:39
  (26 shorter events, 1.1 us)
Async XLA Ops:
  0.6 5.1 %copy-start.1 = (bf16[512,1024]{1,0:T(8,128)(2,1)S(1)}, bf16[512,1024]{1,0:T(8,128)(2,1)}, u32[]{:S(2)}) copy-start(bf16[512,1024]{1,0:T(8,128)(2,1)} %refs_1_.15) | copy-start | bytes 3145732
  0.6 5.1 %copy-start = (bf16[512,1024]{1,0:T(8,128)(2,1)S(1)}, bf16[512,1024]{1,0:T(8,128)(2,1)}, u32[]{:S(2)}) copy-start(bf16[512,1024]{1,0:T(8,128)(2,1)} %refs_0_.19) | copy-start | bytes 3145732
  2.4 19.1 %copy-start.2 = (bf16[512,1024]{1,0:T(8,128)(2,1)S(1)}, bf16[512,1024]{1,0:T(8,128)(2,1)}, u32[]{:S(2)}) copy-start(bf16[512,1024]{1,0:T(8,128)(2,1)} %refs_0_.17) | copy-start | bytes 3145732
  2.4 4.5 %collective-permute-start = (f32[512,128]{1,0:T(8,128)S(1)}, f32[512,128]{1,0:T(8,128)S(1)}, u32[]{:S(2)}, u32[]{:S(2)}) collective-permute-start(f32[512,128]{1,0:T(8,128)S(1)} %shard_map.84.refs_2_), channel_id=1, source_target_pairs={{0,4},{4,0},{8,12},{12,8},{16,20},{20,16},{24,28},{28,24},{32,36},... | collective-permute-start | bytes 786440 | tf_op jit(solution)/shard_map/ppermute | solution.py:339
  16.6 6.9 %collective-permute-start.1 = (f32[64,128]{1,0:T(8,128)S(1)}, f32[64,128]{1,0:T(8,128)S(1)}, u32[]{:S(2)}, u32[]{:S(2)}) collective-permute-start(f32[64,128]{1,0:T(8,128)S(1)} %get-tuple-element.40.refs_3_.refs_0_), channel_id=1, source_target_pairs={{0,68},{4,64},{8,76},{12,72},{16,84},{20,80},{24,92},{28,88},{32,1... | collective-permute-start | bytes 98312 | tf_op jit(solution)/shard_map/ppermute | solution.py:350
  23.5 6.0 %collective-permute-start.2 = (f32[64,128]{1,0:T(8,128)S(1)}, f32[64,128]{1,0:T(8,128)S(1)}, u32[]{:S(2)}, u32[]{:S(2)}) collective-permute-start(f32[64,128]{1,0:T(8,128)S(1)} %shard_map.89.refs_3_), channel_id=1, source_target_pairs={{0,196},{4,192},{8,204},{12,200},{16,212},{20,208},{24,220},{28,21... | collective-permute-start | bytes 98312 | tf_op jit(solution)/shard_map/ppermute | solution.py:353
  29.5 11.0 %copy-start.3 = (bf16[512,1024]{1,0:T(8,128)(2,1)S(1)}, bf16[512,1024]{1,0:T(8,128)(2,1)}, u32[]{:S(2)}) copy-start(bf16[512,1024]{1,0:T(8,128)(2,1)} %refs_2_.9) | copy-start | bytes 3145732
  29.5 11.0 %copy-start.4 = (f32[1024]{0:T(1024)S(1)}, f32[1024]{0:T(1024)}, u32[]{:S(2)}) copy-start(f32[1024]{0:T(1024)} %param.8) | copy-start | bytes 12292
  39.7 1.9 %collective-permute-start.3 = (f32[512,128]{1,0:T(8,128)S(1)}, f32[512,128]{1,0:T(8,128)S(1)}, u32[]{:S(2)}, u32[]{:S(2)}) collective-permute-start(f32[512,128]{1,0:T(8,128)S(1)} %get-tuple-element.46.refs_5_), channel_id=1, source_target_pairs={{0,4},{4,0},{8,12},{12,8},{16,20},{20,16},{24,28},{28,24},{32,36},... | collective-permute-start | bytes 786440 | tf_op jit(solution)/shard_map/ppermute | solution.py:371
  42.2 4.0 %collective-permute-start.6 = (f32[8,128]{1,0:T(8,128)S(1)}, f32[8,128]{1,0:T(8,128)S(1)}, u32[]{:S(2)}, u32[]{:S(2)}) collective-permute-start(f32[8,128]{1,0:T(8,128)S(1)} %get-tuple-element.51.refs_4_), channel_id=1, source_target_pairs={{0,2},{1,3},{2,0},{3,1},{4,6},{5,7},{6,4},{7,5},{8,10},{9,11},{10,... | collective-permute-start | bytes 12296 | tf_op jit(solution)/shard_map/ppermute | solution.py:432
  45.2 3.7 %collective-permute-start.5 = (f32[8,128]{1,0:T(8,128)S(1)}, f32[8,128]{1,0:T(8,128)S(1)}, u32[]{:S(2)}, u32[]{:S(2)}) collective-permute-start(f32[8,128]{1,0:T(8,128)S(1)} %get-tuple-element.51.refs_4_), channel_id=1, source_target_pairs={{0,3},{1,2},{2,1},{3,0},{4,7},{5,6},{6,5},{7,4},{8,11},{9,10},{10,... | collective-permute-start | bytes 12296 | tf_op jit(solution)/shard_map/ppermute | solution.py:432
  46.0 2.9 %collective-permute-start.4 = (f32[8,128]{1,0:T(8,128)S(1)}, f32[8,128]{1,0:T(8,128)S(1)}, u32[]{:S(2)}, u32[]{:S(2)}) collective-permute-start(f32[8,128]{1,0:T(8,128)S(1)} %get-tuple-element.51.refs_4_), channel_id=1, source_target_pairs={{0,1},{1,0},{2,3},{3,2},{4,5},{5,4},{6,7},{7,6},{8,9},{9,8},{10,11... | collective-permute-start | bytes 12296 | tf_op jit(solution)/shard_map/ppermute | solution.py:432
  49.5 3.0 %collective-permute-start.7 = (f32[512,128]{1,0:T(8,128)S(1)}, f32[512,128]{1,0:T(8,128)S(1)}, u32[]{:S(2)}, u32[]{:S(2)}) collective-permute-start(f32[512,128]{1,0:T(8,128)S(1)} %get-tuple-element.54.refs_6_), channel_id=1, source_target_pairs={{0,4},{4,0},{8,12},{12,8},{16,20},{20,16},{24,28},{28,24},{32,36},... | collective-permute-start | bytes 786440 | tf_op jit(solution)/shard_map/ppermute | solution.py:339
  61.5 6.7 %collective-permute-start.8 = (f32[64,128]{1,0:T(8,128)S(1)}, f32[64,128]{1,0:T(8,128)S(1)}, u32[]{:S(2)}, u32[]{:S(2)}) collective-permute-start(f32[64,128]{1,0:T(8,128)S(1)} %get-tuple-element.60.refs_9_.refs_0_), channel_id=1, source_target_pairs={{0,68},{4,64},{8,76},{12,72},{16,84},{20,80},{24,92},{28,88},{32,1... | collective-permute-start | bytes 98312 | tf_op jit(solution)/shard_map/ppermute | solution.py:350
  68.2 5.8 %collective-permute-start.9 = (f32[64,128]{1,0:T(8,128)S(1)}, f32[64,128]{1,0:T(8,128)S(1)}, u32[]{:S(2)}, u32[]{:S(2)}) collective-permute-start(f32[64,128]{1,0:T(8,128)S(1)} %shard_map.100.refs_11_), channel_id=1, source_target_pairs={{0,196},{4,192},{8,204},{12,200},{16,212},{20,208},{24,220},{28,21... | collective-permute-start | bytes 98312 | tf_op jit(solution)/shard_map/ppermute | solution.py:353
  83.2 3.2 %collective-permute-start.10 = (f32[512,128]{1,0:T(8,128)S(1)}, f32[512,128]{1,0:T(8,128)S(1)}, u32[]{:S(2)}, u32[]{:S(2)}) collective-permute-start(f32[512,128]{1,0:T(8,128)S(1)} %get-tuple-element.68.refs_5_), channel_id=1, source_target_pairs={{0,4},{4,0},{8,12},{12,8},{16,20},{20,16},{24,28},{28,24},{32,36},... | collective-permute-start | bytes 786440 | tf_op jit(solution)/shard_map/ppermute | solution.py:371

commit v5 on v4

--- a/solution.py
+++ b/solution.py
@@ -69,6 +69,7 @@
 
 
 OWN, OTHER = 0, 1
+FIRST = ((0, 1), (1, 3))
 
 
 def cols(side, j, half):
@@ -126,7 +127,7 @@
     return top, left, right
 
 
-def intra_kernel(side, q_ref, k_ref, v_ref, qt_ref, wt_ref, o_ref):
+def intra_kernel(side, q_ref, k_ref, v_ref, qt_ref, o_ref):
     n = q_ref.shape[0] // 2
     half = o_ref.shape[1] // HEAD_DIM
     for j in range(half):
@@ -136,8 +137,15 @@
         top, left, right = lower(q, k)
         o_ref[:n, at(j)] = dot(top, v[:n], 1, 0)
         o_ref[n:, at(j)] = dot(left, v[:n], 1, 0) + dot(right, v[n:], 1, 0)
-        for i, block in enumerate(lower_t(q, k)):
-            wt_ref[3 * j + i] = block
+
+
+def weights_kernel(q_ref, k_ref, own_ref, other_ref):
+    half = own_ref.shape[0] // 3
+    for side, wt_ref in ((OWN, own_ref), (OTHER, other_ref)):
+        for j in range(half):
+            c = cols(side, j, half)
+            for i, block in enumerate(lower_t(q_ref[:, c], k_ref[:, c])):
+                wt_ref[3 * j + i] = block
 
 
 def mix_kernel(side, q_ref, s_ref, i_ref, c_ref, g_ref, *refs):
@@ -193,26 +201,26 @@
 
 
 def back(
-    side, q_ref, k_ref, v_ref, gm_ref, s_ref, m_ref, inv_ref, g_ref, wt_ref,
+    side, heads, q_ref, k_ref, v_ref, gm_ref, s_ref, m_ref, inv_ref, g_ref, wt_ref,
     at_ref, gq_ref, gk_ref, gv_ref, then=lambda j: None,
 ):
     n = q_ref.shape[0] // 2
     half = gm_ref.shape[1] // HEAD_DIM
-    for j in range(half):
+    for i, j in enumerate(heads):
         c = cols(side, j, half)
-        at_ref[:, at(j)] = (m_ref[:, at(j)] * inv_ref[...] * g_ref[:, c]).astype(BF)
+        at_ref[:, at(i)] = (m_ref[:, at(j)] * inv_ref[...] * g_ref[:, c]).astype(BF)
         q, k, v, gm = q_ref[:, c], k_ref[:, c], v_ref[:, c], gm_ref[:, at(j)]
         top, left, right = lower(gm, v)
         s = s_ref[at(j), :].astype(BF)
-        gq_ref[:n, at(j)] = (dot(top, k[:n], 1, 0) + dot(gm[:n], s, 1, 1)).astype(BF)
-        gq_ref[n:, at(j)] = (
+        gq_ref[:n, at(i)] = (dot(top, k[:n], 1, 0) + dot(gm[:n], s, 1, 1)).astype(BF)
+        gq_ref[n:, at(i)] = (
             dot(left, k[:n], 1, 0) + dot(right, k[n:], 1, 0) + dot(gm[n:], s, 1, 1)
         ).astype(BF)
-        gk_ref[:n, at(j)] = dot(top, q[:n], 0, 0) + dot(left, q[n:], 0, 0)
-        gk_ref[n:, at(j)] = dot(right, q[n:], 0, 0)
+        gk_ref[:n, at(i)] = dot(top, q[:n], 0, 0) + dot(left, q[n:], 0, 0)
+        gk_ref[n:, at(i)] = dot(right, q[n:], 0, 0)
         top, left, right = wt_ref[3 * j], wt_ref[3 * j + 1], wt_ref[3 * j + 2]
-        gv_ref[:n, at(j)] = dot(top, gm[:n], 1, 0) + dot(left, gm[n:], 1, 0)
-        gv_ref[n:, at(j)] = dot(right, gm[n:], 1, 0)
+        gv_ref[:n, at(i)] = dot(top, gm[:n], 1, 0) + dot(left, gm[n:], 1, 0)
+        gv_ref[n:, at(i)] = dot(right, gm[n:], 1, 0)
         then(j)
 
 
@@ -221,6 +229,18 @@
     for i, (side, src, dst) in enumerate(pairs):
         copies.append(pltpu.make_async_copy(src, dst.at[:, columns(side, half)], sems.at[i]))
         copies[-1].start()
+    return copies
+
+
+def send_two(j, half, pairs, sems):
+    copies = []
+    if j % 2:
+        base = cols(OTHER, j - 1, half).start
+        c = pl.ds(pl.multiple_of(base, 2 * HEAD_DIM), 2 * HEAD_DIM)
+        here = slice((j - 1) * HEAD_DIM, (j + 1) * HEAD_DIM)
+        for i, (src, dst) in enumerate(pairs):
+            copies.append(pltpu.make_async_copy(src.at[:, here], dst.at[:, c], sems.at[i, j]))
+            copies[-1].start()
     return copies
 
 
@@ -234,51 +254,59 @@
     return copies
 
 
-def back_other_kernel(*refs):
-    back(OTHER, *refs)
+def back_other_kernel(heads, *refs):
+    back(OTHER, heads, *refs)
 
 
 def back_own_kernel(*refs):
-    ins, (at_other, gq_other) = refs[:9], refs[9:11]
-    gk_ref, gv_ref, at_hbm, gq_hbm, at_ref, gq_ref, sems, head_sems = refs[11:]
+    ins, others = refs[:9], refs[9:13]
+    gk_ref, gv_ref, at_hbm, gq_hbm, at_ref, gq_ref, sems, head_sems = refs[13:]
     half = gk_ref.shape[1] // HEAD_DIM
-    copies = send_out([(OTHER, at_other, at_hbm), (OTHER, gq_other, gq_hbm)], half, sems)
+    copies = []
+    for i, src in enumerate(others):
+        first, count = FIRST[i // 2]
+        base = cols(OTHER, first, half).start
+        dst = (at_hbm, gq_hbm)[i % 2].at[:, pl.ds(pl.multiple_of(base, HEAD_DIM), count * HEAD_DIM)]
+        copies.append(pltpu.make_async_copy(src, dst, sems.at[i]))
+        copies[-1].start()
     pairs = ((at_ref, at_hbm), (gq_ref, gq_hbm))
 
     def then(j):
         copies.extend(send_heads(j, half, OWN, pairs, head_sems))
 
-    back(OWN, *ins, at_ref, gq_ref, gk_ref, gv_ref, then)
+    back(OWN, range(half), *ins, at_ref, gq_ref, gk_ref, gv_ref, then)
     for copy in copies:
         copy.wait()
 
 
-def last(side, k_ref, v_ref, s_ref, gki_ref, gvi_ref, gk_ref, gv_ref, then=lambda j: None):
-    half = gki_ref.shape[1] // HEAD_DIM
-    for j in range(half):
+def last(side, k_ref, v_ref, s_ref, inner, gk_ref, gv_ref, then=lambda j: None):
+    half = gk_ref.shape[1] // HEAD_DIM
+    pieces = [(*refs, i) for refs in inner for i in range(refs[0].shape[1] // HEAD_DIM)]
+    for j, (gki_ref, gvi_ref, i) in enumerate(pieces):
         c = cols(side, j, half)
         s = s_ref[at(j), :].astype(BF)
-        gk_ref[:, at(j)] = (gki_ref[:, at(j)] + dot(v_ref[:, c], s, 1, 1)).astype(BF)
-        gv_ref[:, at(j)] = (gvi_ref[:, at(j)] + dot(k_ref[:, c], s, 1, 0)).astype(BF)
+        gk_ref[:, at(j)] = (gki_ref[:, at(i)] + dot(v_ref[:, c], s, 1, 1)).astype(BF)
+        gv_ref[:, at(j)] = (gvi_ref[:, at(i)] + dot(k_ref[:, c], s, 1, 0)).astype(BF)
         then(j)
 
 
-def last_own_kernel(*refs):
-    last(OWN, *refs)
+def last_own_kernel(k_ref, v_ref, s_ref, gki_ref, gvi_ref, gk_ref, gv_ref):
+    last(OWN, k_ref, v_ref, s_ref, ((gki_ref, gvi_ref),), gk_ref, gv_ref)
 
 
 def last_other_kernel(
-    k_ref, v_ref, s_ref, gki_ref, gvi_ref, gko_ref, gvo_ref,
+    k_ref, v_ref, s_ref, gka_ref, gva_ref, gkb_ref, gvb_ref, gko_ref, gvo_ref,
     gk_hbm, gv_hbm, gk_ref, gv_ref, sems, head_sems,
 ):
-    half = gki_ref.shape[1] // HEAD_DIM
+    half = gk_ref.shape[1] // HEAD_DIM
+    inner = ((gka_ref, gva_ref), (gkb_ref, gvb_ref))
     copies = send_out([(OWN, gko_ref, gk_hbm), (OWN, gvo_ref, gv_hbm)], half, sems)
     pairs = ((gk_ref, gk_hbm), (gv_ref, gv_hbm))
 
     def then(j):
-        copies.extend(send_heads(j, half, OTHER, pairs, head_sems))
-
-    last(OTHER, k_ref, v_ref, s_ref, gki_ref, gvi_ref, gk_ref, gv_ref, then)
+        copies.extend(send_two(j, half, pairs, head_sems))
+
+    last(OTHER, k_ref, v_ref, s_ref, inner, gk_ref, gv_ref, then)
     for copy in copies:
         copy.wait()
 
@@ -303,11 +331,20 @@
     t_ref[...] = total
 
 
-def outer_kernel(reverse, g_ref, near_ref, far_ref, o_ref):
-    z = lax.axis_index("ctx") // (X * CORES)
-    bit = 0 if reverse else 1
-    near, far = lax.rem(z // 2, 2) == bit, z // 4 == bit
-    total = jnp.where(near, near_ref[...], 0.0) + jnp.where(far, far_ref[...], 0.0)
+def rank(reverse):
+    pair = lax.axis_index("ctx") // (2 * X * CORES)
+    return 3 - pair if reverse else pair
+
+
+def middle_kernel(reverse, t_ref, far_ref, o_ref):
+    place = rank(reverse)
+    own = jnp.where(place == 3, 0.0, t_ref[...])
+    o_ref[...] = own + jnp.where(place >= 2, far_ref[...], 0.0)
+
+
+def outer_kernel(reverse, g_ref, far_ref, near_ref, o_ref):
+    place = rank(reverse)
+    total = jnp.where(place >= 2, far_ref[...], 0.0) + jnp.where(place >= 1, near_ref[...], 0.0)
     for i in range(g_ref.shape[0]):
         o_ref[i] = g_ref[i] + total
 
@@ -347,15 +384,22 @@
         pieces.size,
         vmem=4,
     )
+    far = lax.ppermute(total, "ctx", far_z)
+    after = windows[1](total)[-1:]
+    (total,) = call(
+        functools.partial(middle_kernel, reverse),
+        [array(total.shape, F32)],
+        [total, far],
+        total.size,
+        after,
+        vmem=4,
+    )
     near = lax.ppermute(total, "ctx", near_z)
-    after = windows[1](total)[-1:]
-    total = add(total, near, after, total.shape)
-    far = lax.ppermute(total, "ctx", far_z)
     after = windows[2](total)[-1:]
     (pieces,) = call(
         functools.partial(outer_kernel, reverse),
         [array(pieces.shape, F32)],
-        [inner, near, far],
+        [inner, far, near],
         pieces.size,
         after,
         vmem=4,
@@ -405,14 +449,13 @@
     def intra(side, ready):
         outs = [
             array((half * HEAD_DIM, length), BF),
-            array((3 * half, length // 2, length // 2), BF),
             part(F32),
         ]
         args = [query, keys, values]
         return made_by("intra", side, intra_kernel, outs, args, 3 * square, [ready])
 
     def mix(side, before, after, *sums):
-        args = [query, before, made["intra", side][2], cotangent, gain, *sums]
+        args = [query, before, made["intra", side][1], cotangent, gain, *sums]
         return made_by("mix", side, mix_kernel, [part(F32), rows], args, small, after)
 
     mine, theirs = carried(
@@ -428,9 +471,25 @@
     before = (mine, theirs)
     _, sums = mix(OTHER, theirs, (), made["mix", OWN][1])
     heads = lax.axis_size("head")
+    places = range(lax.axis_size("ctx"))
+
+    def turn(first, second):
+        by = (first, second)
+        return [
+            (i * heads + j, i * heads + (j ^ by[i % CORES])) for i in places for j in range(heads)
+        ]
+
     others = [
-        lax.ppermute(sums, "head", [(i, i ^ j) for i in range(heads)]) for j in (1, 3, 2)
+        lax.ppermute(sums, ("ctx", "head"), turn(*by)) for by in zip((1, 3, 2), (3, 2, 1))
     ]
+
+    weights_t = call(
+        weights_kernel,
+        [array((3 * half, length // 2, length // 2), BF)] * 2,
+        [query, keys],
+        2 * square,
+        [sums],
+    )
 
     def grad_args(side):
         return [made["intra", side][0], made["mix", side][0], cotangent, gain]
@@ -440,6 +499,7 @@
         [part(BF), states, lanes, lanes],
         grad_args(OTHER) + [sums, *others],
         small,
+        weights_t[:1],
     )
 
     def grad_own(ready):
@@ -454,23 +514,38 @@
 
     def back_args(side):
         gm = gm_other if side == OTHER else made["grad"][0]
-        mixture, weights = made["mix", side][0], made["intra", side][1]
+        mixture, weights = made["mix", side][0], weights_t[side]
         return [query, keys, values, gm, before[side], mixture, inverse, gain, weights]
 
+    made["back"] = []
+
     def back_other(ready):
-        outs = [part(BF), part(BF), part(F32), part(F32)]
-        made["back"] = call(back_other_kernel, outs, back_args(OTHER), 4 * square, [ready])
-        return made["back"]
+        first, count = FIRST[len(made["back"])]
+        piece = lambda dtype: array((length, count * HEAD_DIM), dtype)
+        made["back"].append(
+            call(
+                functools.partial(back_other_kernel, range(first, first + count)),
+                [piece(BF), piece(BF), piece(F32), piece(F32)],
+                back_args(OTHER),
+                square * count,
+                [ready],
+            )
+        )
+        return made["back"][-1]
+
+    def grad_and_back(ready):
+        back_piece = back_other(ready)
+        return [*back_piece, *grad_own(back_piece[-1])]
 
     def back_own(ready):
         *made["rows"], gk, gv = call(
-            lambda *refs: back_own_kernel(*refs[:11], *refs[13:15], *refs[11:13], *refs[15:]),
+            lambda *refs: back_own_kernel(*refs[:13], *refs[15:17], *refs[13:15], *refs[17:]),
             [whole, whole, part(F32), part(F32)],
-            [*back_args(OWN), *made["back"][:2]],
+            [*back_args(OWN), *made["back"][0][:2], *made["back"][1][:2]],
             4 * square,
             [ready],
             out=[HBM, HBM, VMEM, VMEM],
-            scratch=halves + [dmas((2,)), dmas((2, half))],
+            scratch=halves + [dmas((4,)), dmas((2, half))],
         )
         made["own"] = [gk, gv]
         return made["own"]
@@ -480,11 +555,11 @@
         made["last"] = call(last_own_kernel, [part(BF), part(BF)], args, 2 * small, [ready])
         return made["last"]
 
-    _, theirs = carried(send, True, [grad_own, back_other, back_own, last_own])
+    _, theirs = carried(send, True, [grad_and_back, back_other, back_own, last_own])
     grads = call(
         last_other_kernel,
         [whole, whole],
-        [keys, values, theirs, *made["back"][2:], *made["last"]],
+        [keys, values, theirs, *made["back"][0][2:], *made["back"][1][2:], *made["last"]],
         2 * small,
         out=HBM,
         scratch=halves + [dmas((2,)), dmas((2, half))],

time: 88.4 us -> 88.4 us (level)
  blocking collectives: 37.6 us -> 36.3 us
  starting transfers between devices: 27.8 us -> 29 us
    ppermute x2, starting transfers between devices: 7.17 us -> 12.3 us  [carried(): far = lax.ppermute(total, 'ctx', far_z)]
    ppermute x2, starting transfers between devices: 8.88 us -> 5.4 us  [carried(): near = lax.ppermute(total, 'ctx', near_z)]
    all_to_all x4, blocking collectives: 37.6 us -> 36.3 us  [carried(): pieces = lax.all_to_all(pieces, 'ctx', 0, 0, axis_index_groups=groups)]
    ppermute x2, starting transfers between devices: 5.18 us -> 4.22 us  [carried(): other = lax.ppermute(send, 'ctx', swap)]
    pallas_call x22 -> x24, Pallas kernels: 15.5 us -> 15.9 us  [call(): pl.pallas_call(body, out_shape=outs, in_specs=ins + [ANY] * len(after), o...]
  transfers between devices with their start and end apart: 11 -> 11, of which waited for: 9 -> 8; matrix products, arithmetic and copies ran while one was open for 0% -> 0% of each run, Pallas kernels for 12% -> 13%
where the time goes in v5:
time: 88.4 us; the launch traced here: 88.1 us
  blocking collectives  36.3 us (41%)
  starting transfers between devices  29 us (33%)
  Pallas kernels  15.9 us (18%)
  waiting for transfers between devices  5.86 us (7%)
  between operations  1 us (1%)
    all_to_all x4, blocking collectives, carried(): pieces = lax.all_to_all(pieces, 'ctx', 0, 0, axis_index_groups=groups)  36.3 us
    pallas_call x24, Pallas kernels, call(): pl.pallas_call(body, out_shape=outs, in_specs=ins + [ANY] * len(after), o...  15.9 us
    ppermute x2, starting transfers between devices, carried(): far = lax.ppermute(total, 'ctx', far_z)  12.3 us
    ppermute x2, starting transfers between devices, carried(): near = lax.ppermute(total, 'ctx', near_z)  5.4 us
    ppermute x2, starting transfers between devices, carried(): other = lax.ppermute(send, 'ctx', swap)  4.22 us
    ppermute x3, starting transfers between devices, body(): lax.ppermute(sums, ('ctx', 'head'), turn(*by))  4.01 us
    ppermute x2, starting transfers between devices, carried(): theirs = lax.ppermute(give, 'ctx', swap)  3.02 us
    ppermute x3, waiting for transfers between devices, body(): lax.ppermute(sums, ('ctx', 'head'), turn(*by))  2.66 us
  transfers between devices with their start and end apart: 11, of which 8 were waited for; matrix products, arithmetic and copies ran while one was open for 0% of the time, Pallas kernels for 13%

profile of v5, /device:TPU:1, one launch (start us, length us, event | category | flops | bytes accessed | tf_op | source)
XLA Modules:
  0.0 88.1 jit_solution(12930084198094771164)
XLA Ops:
  0.7 1.7 %shard_map.84.refs_2_ = f32[512,128]{1,0:T(8,128)S(1)} custom-call(bf16[512,1024]{1,0:T(8,128)(2,1)} %refs_0_.23, bf16[512,1024]{1,0:T(8,128)(2,1)} %refs_1_.19), custom_call_target="tpu_custom_call" | custom-call | flops 67108864 | bytes 2359296 | tf_op jit(solution)/shard_map/pallas_call | solution.py:39
  2.4 3.3 %collective-permute-start = (f32[512,128]{1,0:T(8,128)S(1)}, f32[512,128]{1,0:T(8,128)S(1)}, u32[]{:S(2)}, u32[]{:S(2)}) collective-permute-start(f32[512,128]{1,0:T(8,128)S(1)} %shard_map.84.refs_2_), channel_id=1, source_target_pairs={{0,4},{4,0},{8,12},{12,8},{16,20},{20,16},{24,28},{28,24},{32,36},... | collective-permute-start | bytes 786440 | tf_op jit(solution)/shard_map/ppermute | solution.py:376
  6.2 0.7 collective-permute-done.refs_1_.refs_2_
  6.9 9.6 %all_to_all.20.refs_0_ = f32[8,64,128]{2,1,0:T(8,128)S(1)} all-to-all(f32[8,64,128]{2,1,0:T(8,128)S(1)} %shard_map.86), channel_id=1, replica_groups={{0,8,16,24,32,40,48,56},{4,12,20,28,36,44,52,60},{68,76,84,92,100,108,1..., dimensions={0} | all-to-all | bytes 524288 | tf_op jit(solution)/shard_map/all_to_all | solution.py:379
  16.6 7.1 %collective-permute-start.1 = (f32[64,128]{1,0:T(8,128)S(1)}, f32[64,128]{1,0:T(8,128)S(1)}, u32[]{:S(2)}, u32[]{:S(2)}) collective-permute-start(f32[64,128]{1,0:T(8,128)S(1)} %get-tuple-element.44.refs_3_.refs_0_), channel_id=1, source_target_pairs={{0,196},{4,192},{8,204},{12,200},{16,212},{20,208},{24,220},{28,21... | collective-permute-start | bytes 98312 | tf_op jit(solution)/shard_map/ppermute | solution.py:387
  23.6 1.2 %shard_map.88 = (bf16[512,512]{1,0:T(8,128)(2,1)S(1)}, f32[512,512]{1,0:T(8,128)S(1)}) custom-call(bf16[512,1024]{1,0:T(8,128)(2,1)S(1)} %copy-done.2, bf16[512,1024]{1,0:T(8,128)(2,1)S(1)} %copy-done, bf16[512,1024]{1,0:T(8,128)(2,1)S(1)} %copy-done.1, f32[64,128]{1,0:T(8,128)S(1)} %get-tuple-element.44.refs_3_.refs_0_), custom_call_target="tpu_custom_call" | custom-call | flops 805306368 | bytes 4718592 | tf_op jit(solution)/shard_map/pallas_call | solution.py:39
  25.3 2.8 %collective-permute-start.2 = (f32[64,128]{1,0:T(8,128)S(1)}, f32[64,128]{1,0:T(8,128)S(1)}, u32[]{:S(2)}, u32[]{:S(2)}) collective-permute-start(f32[64,128]{1,0:T(8,128)S(1)} %shard_map.89.refs_3_), channel_id=1, source_target_pairs={{0,68},{4,64},{8,76},{12,72},{16,84},{20,80},{24,92},{28,88},{32,1... | collective-permute-start | bytes 98312 | tf_op jit(solution)/shard_map/ppermute | solution.py:397
  28.1 1.2 %shard_map.90 = (bf16[512,512]{1,0:T(8,128)(2,1)S(1)}, f32[512,512]{1,0:T(8,128)S(1)}) custom-call(bf16[512,1024]{1,0:T(8,128)(2,1)S(1)} %copy-done.2, bf16[512,1024]{1,0:T(8,128)(2,1)S(1)} %copy-done, bf16[512,1024]{1,0:T(8,128)(2,1)S(1)} %copy-done.1, f32[64,128]{1,0:T(8,128)S(1)} %shard_map.89.refs_3_), custom_call_target="tpu_custom_call" | custom-call | flops 805306368 | bytes 4718592 | tf_op jit(solution)/shard_map/pallas_call | solution.py:39
  29.3 0.7 collective-permute-done.2.refs_2_
  30.0 9.3 %all_to_all.21.refs_0_ = f32[8,64,128]{2,1,0:T(8,128)S(1)} all-to-all(f32[8,64,128]{2,1,0:T(8,128)S(1)} %shard_map.91), channel_id=1, replica_groups={{0,8,16,24,32,40,48,56},{4,12,20,28,36,44,52,60},{68,76,84,92,100,108,1..., dimensions={0} | all-to-all | bytes 524288 | tf_op jit(solution)/shard_map/all_to_all | solution.py:407
  39.4 1.0 %collective-permute-start.3 = (f32[512,128]{1,0:T(8,128)S(1)}, f32[512,128]{1,0:T(8,128)S(1)}, u32[]{:S(2)}, u32[]{:S(2)}) collective-permute-start(f32[512,128]{1,0:T(8,128)S(1)} %get-tuple-element.50.refs_5_), channel_id=1, source_target_pairs={{0,4},{4,0},{8,12},{12,8},{16,20},{20,16},{24,28},{28,24},{32,36},... | collective-permute-start | bytes 786440 | tf_op jit(solution)/shard_map/ppermute | solution.py:415
  40.4 0.6 shard_map.93
  41.1 0.5 collective-permute-done.3.refs_1_.refs_4_
  41.6 0.6 shard_map.94
  42.2 1.4 %collective-permute-start.6 = (f32[8,128]{1,0:T(8,128)S(1)}, f32[8,128]{1,0:T(8,128)S(1)}, u32[]{:S(2)}, u32[]{:S(2)}) collective-permute-start(f32[8,128]{1,0:T(8,128)S(1)} %get-tuple-element.55.refs_2_.refs_4_), channel_id=1, source_target_pairs={{0,2},{1,3},{2,0},{3,1},{4,5},{5,4},{6,7},{7,6},{8,10},{9,11},{10,... | collective-permute-start | bytes 12296 | tf_op jit(solution)/shard_map/ppermute | solution.py:483
  43.6 2.6 %collective-permute-start.5 = (f32[8,128]{1,0:T(8,128)S(1)}, f32[8,128]{1,0:T(8,128)S(1)}, u32[]{:S(2)}, u32[]{:S(2)}) collective-permute-start(f32[8,128]{1,0:T(8,128)S(1)} %get-tuple-element.55.refs_2_.refs_4_), channel_id=1, source_target_pairs={{0,3},{1,2},{2,1},{3,0},{4,6},{5,7},{6,4},{7,5},{8,11},{9,10},{10,... | collective-permute-start | bytes 12296 | tf_op jit(solution)/shard_map/ppermute | solution.py:483
  46.2 1.0 %shard_map.95 = (bf16[12,256,256]{2,1,0:T(8,128)(2,1)S(1)}, bf16[12,256,256]{2,1,0:T(8,128)(2,1)S(1)}) custom-call(bf16[512,1024]{1,0:T(8,128)(2,1)S(1)} %copy-done.2, bf16[512,1024]{1,0:T(8,128)(2,1)S(1)} %copy-done, f32[8,128]{1,0:T(8,128)S(1)} %get-tuple-element.55.refs_2_.refs_4_), custom_call_target="tpu_custom_call" | custom-call | flops 536870912 | bytes 5242880 | tf_op jit(solution)/shard_map/pallas_call | solution.py:39
  47.6 2.3 %collective-permute-done.4.refs_5_ = f32[8,128]{1,0:T(8,128)S(1)} collective-permute-done((f32[8,128]{1,0:T(8,128)S(1)}, f32[8,128]{1,0:T(8,128)S(1)}, u32[]{:S(2)}, u32[]{:S(2)}) %collective-permute-start.4) | collective-permute-done | bytes 4128 | tf_op jit(solution)/shard_map/ppermute | solution.py:483
  49.9 0.6 shard_map.96
  50.5 0.9 %collective-permute-start.7 = (f32[512,128]{1,0:T(8,128)S(1)}, f32[512,128]{1,0:T(8,128)S(1)}, u32[]{:S(2)}, u32[]{:S(2)}) collective-permute-start(f32[512,128]{1,0:T(8,128)S(1)} %get-tuple-element.61.refs_9_), channel_id=1, source_target_pairs={{0,4},{4,0},{8,12},{12,8},{16,20},{20,16},{24,28},{28,24},{32,36},... | collective-permute-start | bytes 786440 | tf_op jit(solution)/shard_map/ppermute | solution.py:376
  51.4 0.7 shard_map.97
  52.1 0.5 shard_map.98
  52.7 8.8 %all_to_all.22.refs_0_ = f32[8,64,128]{2,1,0:T(8,128)S(1)} all-to-all(f32[8,64,128]{2,1,0:T(8,128)S(1)} %shard_map.99), channel_id=1, replica_groups={{0,8,16,24,32,40,48,56},{4,12,20,28,36,44,52,60},{68,76,84,92,100,108,1..., dimensions={0} | all-to-all | bytes 524288 | tf_op jit(solution)/shard_map/all_to_all | solution.py:379
  61.6 5.3 %collective-permute-start.8 = (f32[64,128]{1,0:T(8,128)S(1)}, f32[64,128]{1,0:T(8,128)S(1)}, u32[]{:S(2)}, u32[]{:S(2)}) collective-permute-start(f32[64,128]{1,0:T(8,128)S(1)} %get-tuple-element.67.refs_9_.refs_0_), channel_id=1, source_target_pairs={{0,196},{4,192},{8,204},{12,200},{16,212},{20,208},{24,220},{28,21... | collective-permute-start | bytes 98312 | tf_op jit(solution)/shard_map/ppermute | solution.py:387
  66.8 1.8 %shard_map.101 = (bf16[512,384]{1,0:T(8,128)(2,1)S(1)}, bf16[512,384]{1,0:T(8,128)(2,1)S(1)}, f32[512,384]{1,0:T(8,128)S(1)}, f32[512,384]{1,0:T(8,128)S(1)}) custom-call(bf16[512,1024]{1,0:T(8,128)(2,1)S(1)} %copy-done.2, bf16[512,1024]{1,0:T(8,128)(2,1)S(1)} %copy-done, bf16[512,1024]{1,0:T(8,128)(2,1)S(1)} %copy-done.1, ...), custom_call_target="tpu_custom_call" | custom-call | flops 805306368 | bytes 9179136 | tf_op jit(solution)/shard_map/pallas_call | solution.py:39
  69.0 2.6 %collective-permute-start.9 = (f32[64,128]{1,0:T(8,128)S(1)}, f32[64,128]{1,0:T(8,128)S(1)}, u32[]{:S(2)}, u32[]{:S(2)}) collective-permute-start(f32[64,128]{1,0:T(8,128)S(1)} %shard_map.102.refs_13_), channel_id=1, source_target_pairs={{0,68},{4,64},{8,76},{12,72},{16,84},{20,80},{24,92},{28,88},{32,1... | collective-permute-start | bytes 98312 | tf_op jit(solution)/shard_map/ppermute | solution.py:397
  71.5 2.9 %shard_map.103 = (bf16[512,1024]{1,0:T(8,128)(2,1)}, bf16[512,1024]{1,0:T(8,128)(2,1)}, f32[512,512]{1,0:T(8,128)S(1)}, f32[512,512]{1,0:T(8,128)S(1)}) custom-call(bf16[512,1024]{1,0:T(8,128)(2,1)S(1)} %copy-done.2, bf16[512,1024]{1,0:T(8,128)(2,1)S(1)} %copy-done, bf16[512,1024]{1,0:T(8,128)(2,1)S(1)} %copy-done.1, ...), custom_call_target="tpu_custom_call" | custom-call | flops 1073741824 | bytes 12062720 | tf_op jit(solution)/shard_map/pallas_call | solution.py:39
  74.5 8.5 %all_to_all.23.refs_0_ = f32[8,64,128]{2,1,0:T(8,128)S(1)} all-to-all(f32[8,64,128]{2,1,0:T(8,128)S(1)} %shard_map.104), channel_id=1, replica_groups={{0,8,16,24,32,40,48,56},{4,12,20,28,36,44,52,60},{68,76,84,92,100,108,1..., dimensions={0} | all-to-all | bytes 524288 | tf_op jit(solution)/shard_map/all_to_all | solution.py:407
  83.1 2.0 %collective-permute-start.10 = (f32[512,128]{1,0:T(8,128)S(1)}, f32[512,128]{1,0:T(8,128)S(1)}, u32[]{:S(2)}, u32[]{:S(2)}) collective-permute-start(f32[512,128]{1,0:T(8,128)S(1)} %get-tuple-element.75.refs_5_), channel_id=1, source_target_pairs={{0,4},{4,0},{8,12},{12,8},{16,20},{20,16},{24,28},{28,24},{32,36},... | collective-permute-start | bytes 786440 | tf_op jit(solution)/shard_map/ppermute | solution.py:415
  85.1 0.5 shard_map.106
  85.7 0.6 collective-permute-done.10.refs_2_
  86.3 1.7 %shard_map.107 = (bf16[512,1024]{1,0:T(8,128)(2,1)}, bf16[512,1024]{1,0:T(8,128)(2,1)}) custom-call(bf16[512,1024]{1,0:T(8,128)(2,1)S(1)} %copy-done, bf16[512,1024]{1,0:T(8,128)(2,1)S(1)} %copy-done.1, f32[512,128]{1,0:T(8,128)S(1)} %collective-permute-done.10.refs_2_, f32[512,128]{1,0:T(8,128)S(1)} %get-tuple-element.76.refs_3_, ...), custom_call_target="tpu_custom_call" | custom-call | flops 134217728 | bytes 7602176 | tf_op jit(solution)/shard_map/pallas_call | solution.py:39
  (28 shorter events, 1.8 us)
Async XLA Ops:
  0.6 5.1 %copy-start = (bf16[512,1024]{1,0:T(8,128)(2,1)S(1)}, bf16[512,1024]{1,0:T(8,128)(2,1)}, u32[]{:S(2)}) copy-start(bf16[512,1024]{1,0:T(8,128)(2,1)} %refs_0_.23) | copy-start | bytes 3145732
  0.6 5.1 %copy-start.1 = (bf16[512,1024]{1,0:T(8,128)(2,1)S(1)}, bf16[512,1024]{1,0:T(8,128)(2,1)}, u32[]{:S(2)}) copy-start(bf16[512,1024]{1,0:T(8,128)(2,1)} %refs_1_.19) | copy-start | bytes 3145732
  2.4 21.3 %copy-start.2 = (bf16[512,1024]{1,0:T(8,128)(2,1)S(1)}, bf16[512,1024]{1,0:T(8,128)(2,1)}, u32[]{:S(2)}) copy-start(bf16[512,1024]{1,0:T(8,128)(2,1)} %refs_0_.21) | copy-start | bytes 3145732
  2.4 4.5 %collective-permute-start = (f32[512,128]{1,0:T(8,128)S(1)}, f32[512,128]{1,0:T(8,128)S(1)}, u32[]{:S(2)}, u32[]{:S(2)}) collective-permute-start(f32[512,128]{1,0:T(8,128)S(1)} %shard_map.84.refs_2_), channel_id=1, source_target_pairs={{0,4},{4,0},{8,12},{12,8},{16,20},{20,16},{24,28},{28,24},{32,36},... | collective-permute-start | bytes 786440 | tf_op jit(solution)/shard_map/ppermute | solution.py:376
  16.6 8.7 %collective-permute-start.1 = (f32[64,128]{1,0:T(8,128)S(1)}, f32[64,128]{1,0:T(8,128)S(1)}, u32[]{:S(2)}, u32[]{:S(2)}) collective-permute-start(f32[64,128]{1,0:T(8,128)S(1)} %get-tuple-element.44.refs_3_.refs_0_), channel_id=1, source_target_pairs={{0,196},{4,192},{8,204},{12,200},{16,212},{20,208},{24,220},{28,21... | collective-permute-start | bytes 98312 | tf_op jit(solution)/shard_map/ppermute | solution.py:387
  25.3 4.7 %collective-permute-start.2 = (f32[64,128]{1,0:T(8,128)S(1)}, f32[64,128]{1,0:T(8,128)S(1)}, u32[]{:S(2)}, u32[]{:S(2)}) collective-permute-start(f32[64,128]{1,0:T(8,128)S(1)} %shard_map.89.refs_3_), channel_id=1, source_target_pairs={{0,68},{4,64},{8,76},{12,72},{16,84},{20,80},{24,92},{28,88},{32,1... | collective-permute-start | bytes 98312 | tf_op jit(solution)/shard_map/ppermute | solution.py:397
  29.3 11.2 %copy-start.3 = (bf16[512,1024]{1,0:T(8,128)(2,1)S(1)}, bf16[512,1024]{1,0:T(8,128)(2,1)}, u32[]{:S(2)}) copy-start(bf16[512,1024]{1,0:T(8,128)(2,1)} %refs_2_.11) | copy-start | bytes 3145732
  29.3 11.1 %copy-start.4 = (f32[1024]{0:T(1024)S(1)}, f32[1024]{0:T(1024)}, u32[]{:S(2)}) copy-start(f32[1024]{0:T(1024)} %param.8) | copy-start | bytes 12292
  39.4 2.2 %collective-permute-start.3 = (f32[512,128]{1,0:T(8,128)S(1)}, f32[512,128]{1,0:T(8,128)S(1)}, u32[]{:S(2)}, u32[]{:S(2)}) collective-permute-start(f32[512,128]{1,0:T(8,128)S(1)} %get-tuple-element.50.refs_5_), channel_id=1, source_target_pairs={{0,4},{4,0},{8,12},{12,8},{16,20},{20,16},{24,28},{28,24},{32,36},... | collective-permute-start | bytes 786440 | tf_op jit(solution)/shard_map/ppermute | solution.py:415
  42.2 5.0 %collective-permute-start.6 = (f32[8,128]{1,0:T(8,128)S(1)}, f32[8,128]{1,0:T(8,128)S(1)}, u32[]{:S(2)}, u32[]{:S(2)}) collective-permute-start(f32[8,128]{1,0:T(8,128)S(1)} %get-tuple-element.55.refs_2_.refs_4_), channel_id=1, source_target_pairs={{0,2},{1,3},{2,0},{3,1},{4,5},{5,4},{6,7},{7,6},{8,10},{9,11},{10,... | collective-permute-start | bytes 12296 | tf_op jit(solution)/shard_map/ppermute | solution.py:483
  43.6 4.0 %collective-permute-start.5 = (f32[8,128]{1,0:T(8,128)S(1)}, f32[8,128]{1,0:T(8,128)S(1)}, u32[]{:S(2)}, u32[]{:S(2)}) collective-permute-start(f32[8,128]{1,0:T(8,128)S(1)} %get-tuple-element.55.refs_2_.refs_4_), channel_id=1, source_target_pairs={{0,3},{1,2},{2,1},{3,0},{4,6},{5,7},{6,4},{7,5},{8,11},{9,10},{10,... | collective-permute-start | bytes 12296 | tf_op jit(solution)/shard_map/ppermute | solution.py:483
  46.2 3.7 %collective-permute-start.4 = (f32[8,128]{1,0:T(8,128)S(1)}, f32[8,128]{1,0:T(8,128)S(1)}, u32[]{:S(2)}, u32[]{:S(2)}) collective-permute-start(f32[8,128]{1,0:T(8,128)S(1)} %get-tuple-element.55.refs_2_.refs_4_), channel_id=1, source_target_pairs={{0,1},{1,0},{2,3},{3,2},{4,7},{5,6},{6,5},{7,4},{8,9},{9,8},{10,11... | collective-permute-start | bytes 12296 | tf_op jit(solution)/shard_map/ppermute | solution.py:483
  50.5 2.1 %collective-permute-start.7 = (f32[512,128]{1,0:T(8,128)S(1)}, f32[512,128]{1,0:T(8,128)S(1)}, u32[]{:S(2)}, u32[]{:S(2)}) collective-permute-start(f32[512,128]{1,0:T(8,128)S(1)} %get-tuple-element.61.refs_9_), channel_id=1, source_target_pairs={{0,4},{4,0},{8,12},{12,8},{16,20},{20,16},{24,28},{28,24},{32,36},... | collective-permute-start | bytes 786440 | tf_op jit(solution)/shard_map/ppermute | solution.py:376
  61.6 7.4 %collective-permute-start.8 = (f32[64,128]{1,0:T(8,128)S(1)}, f32[64,128]{1,0:T(8,128)S(1)}, u32[]{:S(2)}, u32[]{:S(2)}) collective-permute-start(f32[64,128]{1,0:T(8,128)S(1)} %get-tuple-element.67.refs_9_.refs_0_), channel_id=1, source_target_pairs={{0,196},{4,192},{8,204},{12,200},{16,212},{20,208},{24,220},{28,21... | collective-permute-start | bytes 98312 | tf_op jit(solution)/shard_map/ppermute | solution.py:387
  69.0 5.5 %collective-permute-start.9 = (f32[64,128]{1,0:T(8,128)S(1)}, f32[64,128]{1,0:T(8,128)S(1)}, u32[]{:S(2)}, u32[]{:S(2)}) collective-permute-start(f32[64,128]{1,0:T(8,128)S(1)} %shard_map.102.refs_13_), channel_id=1, source_target_pairs={{0,68},{4,64},{8,76},{12,72},{16,84},{20,80},{24,92},{28,88},{32,1... | collective-permute-start | bytes 98312 | tf_op jit(solution)/shard_map/ppermute | solution.py:397
  83.1 3.2 %collective-permute-start.10 = (f32[512,128]{1,0:T(8,128)S(1)}, f32[512,128]{1,0:T(8,128)S(1)}, u32[]{:S(2)}, u32[]{:S(2)}) collective-permute-start(f32[512,128]{1,0:T(8,128)S(1)} %get-tuple-element.75.refs_5_), channel_id=1, source_target_pairs={{0,4},{4,0},{8,12},{12,8},{16,20},{20,16},{24,28},{28,24},{32,36},... | collective-permute-start | bytes 786440 | tf_op jit(solution)/shard_map/ppermute | solution.py:415

commit v6 on v5

--- a/solution.py
+++ b/solution.py
@@ -91,16 +91,19 @@
     return pl.ds(pl.multiple_of(base, half * HEAD_DIM), half * HEAD_DIM)
 
 
-def state_kernel(side, a_hbm, b_hbm, s_ref, a_ref, b_ref, sems):
-    half = a_ref.shape[1] // HEAD_DIM
+def state_kernel(side, a_hbm, b_hbm, a_ref, b_ref, s_ref, sems):
+    half = s_ref.shape[0] // HEAD_DIM
     copies = []
-    for i, (src, dst) in enumerate(((a_hbm, a_ref), (b_hbm, b_ref))):
-        copies.append(pltpu.make_async_copy(src.at[:, columns(side, half)], dst, sems.at[i]))
-        copies[-1].start()
-    for copy in copies:
+    for i, which in enumerate((side, OWN + OTHER - side)):
+        c = columns(which, half)
+        for j, (src, dst) in enumerate(((a_hbm, a_ref), (b_hbm, b_ref))):
+            copies.append(pltpu.make_async_copy(src.at[:, c], dst.at[:, c], sems.at[i, j]))
+            copies[-1].start()
+    for copy in copies[:2]:
         copy.wait()
-    for j in range(half):
-        s_ref[at(j), :] = dot(a_ref[:, at(j)], b_ref[:, at(j)], 0, 0)
+    state_own_kernel(side, a_ref, b_ref, s_ref)
+    for copy in copies[2:]:
+        copy.wait()
 
 
 def triangle(n, flip=False):
@@ -438,9 +441,9 @@
 
     in_hbm = [pltpu.with_memory_space_constraint(a, pltpu.HBM) for a in (keys, values)]
 
-    (send,) = made_by(
-        "state", OTHER, state_kernel, [states], in_hbm, small,
-        ins=HBM, scratch=halves + [dmas((2,))],
+    keys, values, send = made_by(
+        "state", OTHER, state_kernel, [whole, whole, states], in_hbm, small,
+        ins=HBM, scratch=[dmas((2, 2))],
     )
 
     def state_own(ready):

time: 88.4 us -> 88.4 us (level)
  no operation moved by 1% of the time
where the time goes in v6:
time: 88.4 us; the launch traced here: 88.1 us
  blocking collectives  36.4 us (41%)
  starting transfers between devices  29 us (33%)
  Pallas kernels  16 us (18%)
  waiting for transfers between devices  5.77 us (7%)
  between operations  0.98 us (1%)
    all_to_all x4, blocking collectives, carried(): pieces = lax.all_to_all(pieces, 'ctx', 0, 0, axis_index_groups=groups)  36.4 us
    pallas_call x24, Pallas kernels, call(): pl.pallas_call(body, out_shape=outs, in_specs=ins + [ANY] * len(after), o...  16 us
    ppermute x2, starting transfers between devices, carried(): far = lax.ppermute(total, 'ctx', far_z)  12.4 us
    ppermute x2, starting transfers between devices, carried(): near = lax.ppermute(total, 'ctx', near_z)  5.52 us
    ppermute x2, starting transfers between devices, carried(): other = lax.ppermute(send, 'ctx', swap)  4.22 us
    ppermute x3, starting transfers between devices, body(): lax.ppermute(sums, ('ctx', 'head'), turn(*by))  4.01 us
    ppermute x2, starting transfers between devices, carried(): theirs = lax.ppermute(give, 'ctx', swap)  2.91 us
    ppermute x3, waiting for transfers between devices, body(): lax.ppermute(sums, ('ctx', 'head'), turn(*by))  2.65 us
  transfers between devices with their start and end apart: 11, of which 8 were waited for; matrix products, arithmetic and copies ran while one was open for 0% of the time, Pallas kernels for 13%

profile of v6, /device:TPU:1, one launch (start us, length us, event | category | flops | bytes accessed | tf_op | source)
XLA Modules:
  0.0 88.1 jit_solution(5524904027789845465)
XLA Ops:
  0.6 1.7 %shard_map.84 = (bf16[512,1024]{1,0:T(8,128)(2,1)S(1)}, bf16[512,1024]{1,0:T(8,128)(2,1)S(1)}, f32[512,128]{1,0:T(8,128)S(1)}) custom-call(bf16[512,1024]{1,0:T(8,128)(2,1)} %refs_0_.9, bf16[512,1024]{1,0:T(8,128)(2,1)} %refs_1_.1), custom_call_target="tpu_custom_call" | custom-call | flops 67108864 | bytes 4456448 | tf_op jit(solution)/shard_map/pallas_call | solution.py:39
  2.4 3.3 %collective-permute-start = (f32[512,128]{1,0:T(8,128)S(1)}, f32[512,128]{1,0:T(8,128)S(1)}, u32[]{:S(2)}, u32[]{:S(2)}) collective-permute-start(f32[512,128]{1,0:T(8,128)S(1)} %get-tuple-element.49.refs_2_), channel_id=1, source_target_pairs={{0,4},{4,0},{8,12},{12,8},{16,20},{20,16},{24,28},{28,24},{32,36},... | collective-permute-start | bytes 786440 | tf_op jit(solution)/shard_map/ppermute | solution.py:379
  6.2 0.7 collective-permute-done.refs_1_.refs_2_
  6.9 9.6 %all_to_all.20.refs_0_ = f32[8,64,128]{2,1,0:T(8,128)S(1)} all-to-all(f32[8,64,128]{2,1,0:T(8,128)S(1)} %shard_map.86), channel_id=1, replica_groups={{0,8,16,24,32,40,48,56},{4,12,20,28,36,44,52,60},{68,76,84,92,100,108,1..., dimensions={0} | all-to-all | bytes 524288 | tf_op jit(solution)/shard_map/all_to_all | solution.py:382
  16.6 7.1 %collective-permute-start.1 = (f32[64,128]{1,0:T(8,128)S(1)}, f32[64,128]{1,0:T(8,128)S(1)}, u32[]{:S(2)}, u32[]{:S(2)}) collective-permute-start(f32[64,128]{1,0:T(8,128)S(1)} %get-tuple-element.50.refs_3_.refs_0_), channel_id=1, source_target_pairs={{0,196},{4,192},{8,204},{12,200},{16,212},{20,208},{24,220},{28,21... | collective-permute-start | bytes 98312 | tf_op jit(solution)/shard_map/ppermute | solution.py:390
  23.6 1.2 %shard_map.88 = (bf16[512,512]{1,0:T(8,128)(2,1)S(1)}, f32[512,512]{1,0:T(8,128)S(1)}) custom-call(bf16[512,1024]{1,0:T(8,128)(2,1)S(1)} %copy-done, bf16[512,1024]{1,0:T(8,128)(2,1)S(1)} %get-tuple-element.47.refs_0_.refs_1_, bf16[512,1024]{1,0:T(8,128)(2,1)S(1)} %get-tuple-element.48.refs_1_.refs_2_, f32[64,128]{1,0:T(8,128)S(1)} %get-tuple-element.50.refs_3_.refs_0_), custom_call_target="tpu_custom_call" | custom-call | flops 805306368 | bytes 4718592 | tf_op jit(solution)/shard_map/pallas_call | solution.py:39
  25.2 2.8 %collective-permute-start.2 = (f32[64,128]{1,0:T(8,128)S(1)}, f32[64,128]{1,0:T(8,128)S(1)}, u32[]{:S(2)}, u32[]{:S(2)}) collective-permute-start(f32[64,128]{1,0:T(8,128)S(1)} %shard_map.89.refs_3_), channel_id=1, source_target_pairs={{0,68},{4,64},{8,76},{12,72},{16,84},{20,80},{24,92},{28,88},{32,1... | collective-permute-start | bytes 98312 | tf_op jit(solution)/shard_map/ppermute | solution.py:400
  28.1 1.2 %shard_map.90 = (bf16[512,512]{1,0:T(8,128)(2,1)S(1)}, f32[512,512]{1,0:T(8,128)S(1)}) custom-call(bf16[512,1024]{1,0:T(8,128)(2,1)S(1)} %copy-done, bf16[512,1024]{1,0:T(8,128)(2,1)S(1)} %get-tuple-element.47.refs_0_.refs_1_, bf16[512,1024]{1,0:T(8,128)(2,1)S(1)} %get-tuple-element.48.refs_1_.refs_2_, f32[64,128]{1,0:T(8,128)S(1)} %shard_map.89.refs_3_), custom_call_target="tpu_custom_call" | custom-call | flops 805306368 | bytes 4718592 | tf_op jit(solution)/shard_map/pallas_call | solution.py:39
  29.3 0.7 collective-permute-done.2.refs_2_
  30.0 9.3 %all_to_all.21.refs_0_ = f32[8,64,128]{2,1,0:T(8,128)S(1)} all-to-all(f32[8,64,128]{2,1,0:T(8,128)S(1)} %shard_map.91), channel_id=1, replica_groups={{0,8,16,24,32,40,48,56},{4,12,20,28,36,44,52,60},{68,76,84,92,100,108,1..., dimensions={0} | all-to-all | bytes 524288 | tf_op jit(solution)/shard_map/all_to_all | solution.py:410
  39.4 1.0 %collective-permute-start.3 = (f32[512,128]{1,0:T(8,128)S(1)}, f32[512,128]{1,0:T(8,128)S(1)}, u32[]{:S(2)}, u32[]{:S(2)}) collective-permute-start(f32[512,128]{1,0:T(8,128)S(1)} %get-tuple-element.56.refs_5_), channel_id=1, source_target_pairs={{0,4},{4,0},{8,12},{12,8},{16,20},{20,16},{24,28},{28,24},{32,36},... | collective-permute-start | bytes 786440 | tf_op jit(solution)/shard_map/ppermute | solution.py:418
  40.4 0.6 shard_map.93
  41.1 0.5 collective-permute-done.3.refs_1_.refs_4_
  41.6 0.6 shard_map.94
  42.2 1.4 %collective-permute-start.6 = (f32[8,128]{1,0:T(8,128)S(1)}, f32[8,128]{1,0:T(8,128)S(1)}, u32[]{:S(2)}, u32[]{:S(2)}) collective-permute-start(f32[8,128]{1,0:T(8,128)S(1)} %get-tuple-element.61.refs_2_.refs_4_), channel_id=1, source_target_pairs={{0,2},{1,3},{2,0},{3,1},{4,5},{5,4},{6,7},{7,6},{8,10},{9,11},{10,... | collective-permute-start | bytes 12296 | tf_op jit(solution)/shard_map/ppermute | solution.py:486
  43.6 2.6 %collective-permute-start.5 = (f32[8,128]{1,0:T(8,128)S(1)}, f32[8,128]{1,0:T(8,128)S(1)}, u32[]{:S(2)}, u32[]{:S(2)}) collective-permute-start(f32[8,128]{1,0:T(8,128)S(1)} %get-tuple-element.61.refs_2_.refs_4_), channel_id=1, source_target_pairs={{0,3},{1,2},{2,1},{3,0},{4,6},{5,7},{6,4},{7,5},{8,11},{9,10},{10,... | collective-permute-start | bytes 12296 | tf_op jit(solution)/shard_map/ppermute | solution.py:486
  46.2 1.0 %shard_map.95 = (bf16[12,256,256]{2,1,0:T(8,128)(2,1)S(1)}, bf16[12,256,256]{2,1,0:T(8,128)(2,1)S(1)}) custom-call(bf16[512,1024]{1,0:T(8,128)(2,1)S(1)} %copy-done, bf16[512,1024]{1,0:T(8,128)(2,1)S(1)} %get-tuple-element.47.refs_0_.refs_1_, f32[8,128]{1,0:T(8,128)S(1)} %get-tuple-element.61.refs_2_.refs_4_), custom_call_target="tpu_custom_call" | custom-call | flops 536870912 | bytes 5242880 | tf_op jit(solution)/shard_map/pallas_call | solution.py:39
  47.6 2.3 %collective-permute-done.4.refs_5_ = f32[8,128]{1,0:T(8,128)S(1)} collective-permute-done((f32[8,128]{1,0:T(8,128)S(1)}, f32[8,128]{1,0:T(8,128)S(1)}, u32[]{:S(2)}, u32[]{:S(2)}) %collective-permute-start.4) | collective-permute-done | bytes 4128 | tf_op jit(solution)/shard_map/ppermute | solution.py:486
  49.9 0.6 shard_map.96
  50.5 0.9 %collective-permute-start.7 = (f32[512,128]{1,0:T(8,128)S(1)}, f32[512,128]{1,0:T(8,128)S(1)}, u32[]{:S(2)}, u32[]{:S(2)}) collective-permute-start(f32[512,128]{1,0:T(8,128)S(1)} %get-tuple-element.67.refs_9_), channel_id=1, source_target_pairs={{0,4},{4,0},{8,12},{12,8},{16,20},{20,16},{24,28},{28,24},{32,36},... | collective-permute-start | bytes 786440 | tf_op jit(solution)/shard_map/ppermute | solution.py:379
  51.4 0.7 shard_map.97
  52.1 0.5 shard_map.98
  52.7 8.8 %all_to_all.22.refs_0_ = f32[8,64,128]{2,1,0:T(8,128)S(1)} all-to-all(f32[8,64,128]{2,1,0:T(8,128)S(1)} %shard_map.99), channel_id=1, replica_groups={{0,8,16,24,32,40,48,56},{4,12,20,28,36,44,52,60},{68,76,84,92,100,108,1..., dimensions={0} | all-to-all | bytes 524288 | tf_op jit(solution)/shard_map/all_to_all | solution.py:382
  61.6 5.3 %collective-permute-start.8 = (f32[64,128]{1,0:T(8,128)S(1)}, f32[64,128]{1,0:T(8,128)S(1)}, u32[]{:S(2)}, u32[]{:S(2)}) collective-permute-start(f32[64,128]{1,0:T(8,128)S(1)} %get-tuple-element.73.refs_9_.refs_0_), channel_id=1, source_target_pairs={{0,196},{4,192},{8,204},{12,200},{16,212},{20,208},{24,220},{28,21... | collective-permute-start | bytes 98312 | tf_op jit(solution)/shard_map/ppermute | solution.py:390
  66.9 1.8 %shard_map.101 = (bf16[512,384]{1,0:T(8,128)(2,1)S(1)}, bf16[512,384]{1,0:T(8,128)(2,1)S(1)}, f32[512,384]{1,0:T(8,128)S(1)}, f32[512,384]{1,0:T(8,128)S(1)}) custom-call(bf16[512,1024]{1,0:T(8,128)(2,1)S(1)} %copy-done, bf16[512,1024]{1,0:T(8,128)(2,1)S(1)} %get-tuple-element.47.refs_0_.refs_1_, bf16[512,1024]{1,0:T(8,128)(2,1)S(1)} %get-tuple-element.48.refs_1_.refs_2_, ...), custom_call_target="tpu_custom_call" | custom-call | flops 805306368 | bytes 9179136 | tf_op jit(solution)/shard_map/pallas_call | solution.py:39
  68.9 2.7 %collective-permute-start.9 = (f32[64,128]{1,0:T(8,128)S(1)}, f32[64,128]{1,0:T(8,128)S(1)}, u32[]{:S(2)}, u32[]{:S(2)}) collective-permute-start(f32[64,128]{1,0:T(8,128)S(1)} %shard_map.102.refs_13_), channel_id=1, source_target_pairs={{0,68},{4,64},{8,76},{12,72},{16,84},{20,80},{24,92},{28,88},{32,1... | collective-permute-start | bytes 98312 | tf_op jit(solution)/shard_map/ppermute | solution.py:400
  71.6 2.9 %shard_map.103 = (bf16[512,1024]{1,0:T(8,128)(2,1)}, bf16[512,1024]{1,0:T(8,128)(2,1)}, f32[512,512]{1,0:T(8,128)S(1)}, f32[512,512]{1,0:T(8,128)S(1)}) custom-call(bf16[512,1024]{1,0:T(8,128)(2,1)S(1)} %copy-done, bf16[512,1024]{1,0:T(8,128)(2,1)S(1)} %get-tuple-element.47.refs_0_.refs_1_, bf16[512,1024]{1,0:T(8,128)(2,1)S(1)} %get-tuple-element.48.refs_1_.refs_2_, ...), custom_call_target="tpu_custom_call" | custom-call | flops 1073741824 | bytes 12062720 | tf_op jit(solution)/shard_map/pallas_call | solution.py:39
  74.6 8.6 %all_to_all.23.refs_0_ = f32[8,64,128]{2,1,0:T(8,128)S(1)} all-to-all(f32[8,64,128]{2,1,0:T(8,128)S(1)} %shard_map.104), channel_id=1, replica_groups={{0,8,16,24,32,40,48,56},{4,12,20,28,36,44,52,60},{68,76,84,92,100,108,1..., dimensions={0} | all-to-all | bytes 524288 | tf_op jit(solution)/shard_map/all_to_all | solution.py:410
  83.3 1.9 %collective-permute-start.10 = (f32[512,128]{1,0:T(8,128)S(1)}, f32[512,128]{1,0:T(8,128)S(1)}, u32[]{:S(2)}, u32[]{:S(2)}) collective-permute-start(f32[512,128]{1,0:T(8,128)S(1)} %get-tuple-element.81.refs_5_), channel_id=1, source_target_pairs={{0,4},{4,0},{8,12},{12,8},{16,20},{20,16},{24,28},{28,24},{32,36},... | collective-permute-start | bytes 786440 | tf_op jit(solution)/shard_map/ppermute | solution.py:418
  85.2 0.5 shard_map.106
  85.7 0.6 collective-permute-done.10.refs_2_
  86.3 1.7 %shard_map.107 = (bf16[512,1024]{1,0:T(8,128)(2,1)}, bf16[512,1024]{1,0:T(8,128)(2,1)}) custom-call(bf16[512,1024]{1,0:T(8,128)(2,1)S(1)} %get-tuple-element.47.refs_0_.refs_1_, bf16[512,1024]{1,0:T(8,128)(2,1)S(1)} %get-tuple-element.48.refs_1_.refs_2_, f32[512,128]{1,0:T(8,128)S(1)} %collective-permute-done.10.refs_2_, ...), custom_call_target="tpu_custom_call" | custom-call | flops 134217728 | bytes 7602176 | tf_op jit(solution)/shard_map/pallas_call | solution.py:39
  (24 shorter events, 1.8 us)
Async XLA Ops:
  2.4 4.5 %collective-permute-start = (f32[512,128]{1,0:T(8,128)S(1)}, f32[512,128]{1,0:T(8,128)S(1)}, u32[]{:S(2)}, u32[]{:S(2)}) collective-permute-start(f32[512,128]{1,0:T(8,128)S(1)} %get-tuple-element.49.refs_2_), channel_id=1, source_target_pairs={{0,4},{4,0},{8,12},{12,8},{16,20},{20,16},{24,28},{28,24},{32,36},... | collective-permute-start | bytes 786440 | tf_op jit(solution)/shard_map/ppermute | solution.py:379
  5.7 17.9 %copy-start = (bf16[512,1024]{1,0:T(8,128)(2,1)S(1)}, bf16[512,1024]{1,0:T(8,128)(2,1)}, u32[]{:S(2)}) copy-start(bf16[512,1024]{1,0:T(8,128)(2,1)} %refs_0_.17) | copy-start | bytes 3145732
  16.6 8.7 %collective-permute-start.1 = (f32[64,128]{1,0:T(8,128)S(1)}, f32[64,128]{1,0:T(8,128)S(1)}, u32[]{:S(2)}, u32[]{:S(2)}) collective-permute-start(f32[64,128]{1,0:T(8,128)S(1)} %get-tuple-element.50.refs_3_.refs_0_), channel_id=1, source_target_pairs={{0,196},{4,192},{8,204},{12,200},{16,212},{20,208},{24,220},{28,21... | collective-permute-start | bytes 98312 | tf_op jit(solution)/shard_map/ppermute | solution.py:390
  25.2 4.7 %collective-permute-start.2 = (f32[64,128]{1,0:T(8,128)S(1)}, f32[64,128]{1,0:T(8,128)S(1)}, u32[]{:S(2)}, u32[]{:S(2)}) collective-permute-start(f32[64,128]{1,0:T(8,128)S(1)} %shard_map.89.refs_3_), channel_id=1, source_target_pairs={{0,68},{4,64},{8,76},{12,72},{16,84},{20,80},{24,92},{28,88},{32,1... | collective-permute-start | bytes 98312 | tf_op jit(solution)/shard_map/ppermute | solution.py:400
  29.3 11.2 %copy-start.1 = (bf16[512,1024]{1,0:T(8,128)(2,1)S(1)}, bf16[512,1024]{1,0:T(8,128)(2,1)}, u32[]{:S(2)}) copy-start(bf16[512,1024]{1,0:T(8,128)(2,1)} %refs_2_.3) | copy-start | bytes 3145732
  29.3 11.1 %copy-start.2 = (f32[1024]{0:T(1024)S(1)}, f32[1024]{0:T(1024)}, u32[]{:S(2)}) copy-start(f32[1024]{0:T(1024)} %param.8) | copy-start | bytes 12292
  39.4 2.2 %collective-permute-start.3 = (f32[512,128]{1,0:T(8,128)S(1)}, f32[512,128]{1,0:T(8,128)S(1)}, u32[]{:S(2)}, u32[]{:S(2)}) collective-permute-start(f32[512,128]{1,0:T(8,128)S(1)} %get-tuple-element.56.refs_5_), channel_id=1, source_target_pairs={{0,4},{4,0},{8,12},{12,8},{16,20},{20,16},{24,28},{28,24},{32,36},... | collective-permute-start | bytes 786440 | tf_op jit(solution)/shard_map/ppermute | solution.py:418
  42.2 5.0 %collective-permute-start.6 = (f32[8,128]{1,0:T(8,128)S(1)}, f32[8,128]{1,0:T(8,128)S(1)}, u32[]{:S(2)}, u32[]{:S(2)}) collective-permute-start(f32[8,128]{1,0:T(8,128)S(1)} %get-tuple-element.61.refs_2_.refs_4_), channel_id=1, source_target_pairs={{0,2},{1,3},{2,0},{3,1},{4,5},{5,4},{6,7},{7,6},{8,10},{9,11},{10,... | collective-permute-start | bytes 12296 | tf_op jit(solution)/shard_map/ppermute | solution.py:486
  43.6 4.0 %collective-permute-start.5 = (f32[8,128]{1,0:T(8,128)S(1)}, f32[8,128]{1,0:T(8,128)S(1)}, u32[]{:S(2)}, u32[]{:S(2)}) collective-permute-start(f32[8,128]{1,0:T(8,128)S(1)} %get-tuple-element.61.refs_2_.refs_4_), channel_id=1, source_target_pairs={{0,3},{1,2},{2,1},{3,0},{4,6},{5,7},{6,4},{7,5},{8,11},{9,10},{10,... | collective-permute-start | bytes 12296 | tf_op jit(solution)/shard_map/ppermute | solution.py:486
  46.2 3.7 %collective-permute-start.4 = (f32[8,128]{1,0:T(8,128)S(1)}, f32[8,128]{1,0:T(8,128)S(1)}, u32[]{:S(2)}, u32[]{:S(2)}) collective-permute-start(f32[8,128]{1,0:T(8,128)S(1)} %get-tuple-element.61.refs_2_.refs_4_), channel_id=1, source_target_pairs={{0,1},{1,0},{2,3},{3,2},{4,7},{5,6},{6,5},{7,4},{8,9},{9,8},{10,11... | collective-permute-start | bytes 12296 | tf_op jit(solution)/shard_map/ppermute | solution.py:486
  50.5 2.1 %collective-permute-start.7 = (f32[512,128]{1,0:T(8,128)S(1)}, f32[512,128]{1,0:T(8,128)S(1)}, u32[]{:S(2)}, u32[]{:S(2)}) collective-permute-start(f32[512,128]{1,0:T(8,128)S(1)} %get-tuple-element.67.refs_9_), channel_id=1, source_target_pairs={{0,4},{4,0},{8,12},{12,8},{16,20},{20,16},{24,28},{28,24},{32,36},... | collective-permute-start | bytes 786440 | tf_op jit(solution)/shard_map/ppermute | solution.py:379
  61.6 7.3 %collective-permute-start.8 = (f32[64,128]{1,0:T(8,128)S(1)}, f32[64,128]{1,0:T(8,128)S(1)}, u32[]{:S(2)}, u32[]{:S(2)}) collective-permute-start(f32[64,128]{1,0:T(8,128)S(1)} %get-tuple-element.73.refs_9_.refs_0_), channel_id=1, source_target_pairs={{0,196},{4,192},{8,204},{12,200},{16,212},{20,208},{24,220},{28,21... | collective-permute-start | bytes 98312 | tf_op jit(solution)/shard_map/ppermute | solution.py:390
  68.9 5.6 %collective-permute-start.9 = (f32[64,128]{1,0:T(8,128)S(1)}, f32[64,128]{1,0:T(8,128)S(1)}, u32[]{:S(2)}, u32[]{:S(2)}) collective-permute-start(f32[64,128]{1,0:T(8,128)S(1)} %shard_map.102.refs_13_), channel_id=1, source_target_pairs={{0,68},{4,64},{8,76},{12,72},{16,84},{20,80},{24,92},{28,88},{32,1... | collective-permute-start | bytes 98312 | tf_op jit(solution)/shard_map/ppermute | solution.py:400
  83.3 3.1 %collective-permute-start.10 = (f32[512,128]{1,0:T(8,128)S(1)}, f32[512,128]{1,0:T(8,128)S(1)}, u32[]{:S(2)}, u32[]{:S(2)}) collective-permute-start(f32[512,128]{1,0:T(8,128)S(1)} %get-tuple-element.81.refs_5_), channel_id=1, source_target_pairs={{0,4},{4,0},{8,12},{12,8},{16,20},{20,16},{24,28},{28,24},{32,36},... | collective-permute-start | bytes 786440 | tf_op jit(solution)/shard_map/ppermute | solution.py:418
